TPU v7x, 512 devices: a whole 4x8x8 slice. The times are simulated.
512 devices in a mesh: fsdp: 32 (over x, y_lo, core), blk: 16 (over z, y_hi).
Axes of the slice: x: 4, y: 8 (y_hi: 2, y_lo: 4; y = y_hi * 4 + y_lo), z: 8, core: 2. Of those that a mesh axis runs over, the one named last changes fastest.
Arguments:
- gradient: float32 [28672, 8192], P('fsdp', 'blk'), may hold values from -120 to 120
- left_basis: bfloat16 [768, 28672], P('blk', 'fsdp'), may hold values from -0.03125 to 0.03125
- right_basis: bfloat16 [8192, 8192], P('blk', 'fsdp'), may hold values from -0.0625 to 0.0625
- moment: float32 [768, 8192], P('blk', 'fsdp'), may hold values from -6 to 6
- variance: float32 [768, 8192], P('blk', 'fsdp'), may hold values from 0.05 to 5
Outputs:
- update: float32 [28672, 8192], P('fsdp', 'blk')
- new_moment: float32 [768, 8192], P('blk', 'fsdp')
- new_variance: float32 [768, 8192], P('blk', 'fsdp')
All inputs are finite; a program needn't handle non-finite values.
Results may differ from a plain program's by a relative error of at most 0.006.
Values may be sent and summed in bfloat16 or wider, within the bound.
No kernel may reach another device: no remote copies, remote signals or barrier semaphores. Data moves between devices by JAX's collectives and lax.ppermute only.
A program may use at most 64 MiB of HBM per device.

v0:
```python
import jax
import jax.numpy as jnp
from jax import lax
from jax.sharding import PartitionSpec as P

beta_first = 0.9
beta_second = 0.95
adam_eps = 1e-08
graft_eps = 1e-06


def body(gradient, left_basis, right_basis, moment, variance):
    grad_b = gradient.astype(jnp.bfloat16)
    panels = lax.all_gather(left_basis, "blk", axis=0, tiled=True)
    partial_value = jnp.dot(panels, grad_b, preferred_element_type=jnp.float32)
    projected = lax.psum(partial_value, "fsdp").astype(jnp.bfloat16)
    own_rows = lax.all_to_all(projected, "blk", split_axis=0, concat_axis=1, tiled=True)
    rotated = jnp.dot(
        own_rows,
        lax.all_gather(right_basis, "blk", axis=0, tiled=True),
        preferred_element_type=jnp.float32,
    )
    new_moment = beta_first * moment + (1.0 - beta_first) * rotated
    new_variance = beta_second * variance + (1.0 - beta_second) * rotated * rotated
    direction = (new_moment / (jnp.sqrt(new_variance) + adam_eps)).astype(jnp.bfloat16)
    partial_back = lax.dot_general(
        lax.all_gather(direction, "blk", axis=0, tiled=True),
        right_basis,
        (((1,), (1,)), ((), ())),
        preferred_element_type=jnp.float32,
    )
    returned = lax.psum(partial_back, "fsdp").astype(jnp.bfloat16)
    unscaled = lax.dot_general(
        panels, returned, (((0,), (0,)), ((), ())), preferred_element_type=jnp.float32
    )
    unscaled_local = jnp.sum(unscaled * unscaled)
    grad_sq, unscaled_sq = lax.psum((jnp.sum(gradient * gradient), unscaled_local), ("fsdp", "blk"))
    update = unscaled * (jnp.sqrt(grad_sq) / (jnp.sqrt(unscaled_sq) + graft_eps))
    return (update, new_moment, new_variance)


def solution(mesh):
    return jax.shard_map(
        body,
        mesh=mesh,
        in_specs=(
            P("fsdp", "blk"),
            P("blk", "fsdp"),
            P("blk", "fsdp"),
            P("blk", "fsdp"),
            P("blk", "fsdp"),
        ),
        out_specs=(P("fsdp", "blk"), P("blk", "fsdp"), P("blk", "fsdp")),
        check_vma=False,
    )
```

profile of v0, /device:TPU:1, one launch (start us, length us, event | category | flops | bytes accessed | tf_op | source)
XLA Modules:
  0.0 634.4 jit_solution(10745632505662290150)
XLA Ops:
  7.2 0.0 all-gather.3.cloned.1.call-start
  7.2 0.7 all-gather.3.cloned.1.call-update
  7.9 0.0 all-gather.5.cloned.1.call-start
  7.9 0.7 all-gather.5.cloned.1.call-update
  8.6 98.2 %all-gather.3.cloned.1.call-done = bf16[768,896]{1,0:T(8,128)(2,1)} async-done(((bf16[48,896]{1,0:T(8,128)(2,1)}), bf16[768,896]{1,0:T(8,128)(2,1)}) %all-gather.3.cloned.1.call-update) | async-done | bytes 1376272 | tf_op jit(solution)/shard_map/all_gather | solution.py:14
  106.8 2.9 fusion
  109.7 0.0 copy-start
  109.7 171.5 %all-reduce.3 = bf16[768,512]{1,0:T(8,128)(2,1)} all-reduce(f32[768,512]{1,0:T(8,128)S(1)} %fusion), channel_id=1, replica_groups=mesh['fsdp'=32,'blk'=16] {'fsdp'}, use_global_device_ids=true, to_apply=%region_0.0 | all-reduce | flops 393216 | bytes 2359296 | tf_op jit(solution)/shard_map/psum | solution.py:16
  281.2 7.9 %all-to-all-start = ((bf16[16,48,512]{2,1,0:T(8,128)(2,1)}), bf16[16,48,512]{2,1,0:T(8,128)(2,1)S(1)}, u32[]{:S(2)}, u32[]{:S(2)}) async-start(bf16[16,48,512]{2,1,0:T(8,128)(2,1)} %bitcast.15), calls=%async_computation | async-start | bytes 1572864 | tf_op jit(solution)/shard_map/all_to_all | solution.py:17
  289.1 0.0 copy-start.3
  289.1 0.0 copy-start.4
  289.1 1.1 multiply_reduce_fusion.1
  290.2 13.9 %all-to-all-done = bf16[16,48,512]{2,1,0:T(8,128)(2,1)S(1)} async-done(((bf16[16,48,512]{2,1,0:T(8,128)(2,1)}), bf16[16,48,512]{2,1,0:T(8,128)(2,1)S(1)}, u32[]{:S(2)}, u32[]{:S(2)}) %all-to-all-start) | async-done | bytes 786464 | tf_op jit(solution)/shard_map/all_to_all | solution.py:17
  304.2 0.1 copy.13
  304.2 0.0 all-gather.5.cloned.1.call-done
  304.3 0.0 copy-start.2
  304.3 3.7 divide_convert_fusion
  308.0 53.4 %all_gather.11 = bf16[768,256]{1,0:T(8,128)(2,1)S(1)} all-gather(bf16[48,256]{1,0:T(8,128)(2,1)S(1)} %get-tuple-element.14), channel_id=1, replica_groups=mesh['fsdp'=32,'blk'=16] {'blk'}, dimensions={0}, use_global_device_ids=true | all-gather | bytes 417792 | tf_op jit(solution)/shard_map/all_gather | solution.py:27
  361.5 0.4 fusion.6
  361.9 159.1 %all-reduce.4 = bf16[768,512]{1,0:T(8,128)(2,1)} all-reduce(f32[768,512]{1,0:T(8,128)S(1)} %fusion.6), channel_id=1, replica_groups=mesh['fsdp'=32,'blk'=16] {'fsdp'}, use_global_device_ids=true, to_apply=%region_1.0 | all-reduce | flops 393216 | bytes 2359296 | tf_op jit(solution)/shard_map/psum | solution.py:32
  521.0 4.0 multiply_reduce_fusion
  525.0 97.9 %all-reduce = (f32[]{:T(128)}, f32[]{:T(128)}) all-reduce(f32[]{:T(128)} %multiply_reduce_fusion.1, f32[]{:T(128)} %get-tuple-element.17), channel_id=1, replica_groups=mesh['fsdp'=32,'blk'=16] {'fsdp','blk'}, use_global_device_ids=true, to_apply=%region_3.0 | all-reduce | flops 2 | bytes 16 | tf_op jit(solution)/shard_map/psum | solution.py:37
  624.2 1.6 multiply_bitcast_fusion
  625.9 1.7 copy.12
  (6 shorter events, 0.0 us)
Async XLA Ops:
  7.2 99.7 %all-gather.3.cloned.1.call-start = ((), (), s32[]{:S(2)}) async-start(), calls=%async_computation.1 | async-start | bytes 1462272 | tf_op jit(solution)/shard_map/all_gather | solution.py:14
  7.9 296.4 %all-gather.5.cloned.1.call-start = ((), (), s32[]{:S(2)}) async-start(), calls=%async_computation.2 | async-start | bytes 4456448 | tf_op jit(solution)/shard_map/all_gather | solution.py:20
  109.7 179.4 %copy-start = (f32[896,512]{1,0:T(8,128)S(1)}, f32[896,512]{1,0:T(8,128)}, u32[]{:S(2)}) copy-start(f32[896,512]{1,0:T(8,128)} %param.5) | copy-start | bytes 5505028
  281.2 23.0 %all-to-all-start = ((bf16[16,48,512]{2,1,0:T(8,128)(2,1)}), bf16[16,48,512]{2,1,0:T(8,128)(2,1)S(1)}, u32[]{:S(2)}, u32[]{:S(2)}) async-start(bf16[16,48,512]{2,1,0:T(8,128)(2,1)} %bitcast.15), calls=%async_computation | async-start | bytes 1572864 | tf_op jit(solution)/shard_map/all_to_all | solution.py:17
  289.1 15.2 %copy-start.3 = (f32[48,256]{1,0:T(8,128)S(1)}, f32[48,256]{1,0:T(8,128)}, u32[]{:S(2)}) copy-start(f32[48,256]{1,0:T(8,128)} %param.9) | copy-start | bytes 147460
  289.1 15.2 %copy-start.4 = (f32[48,256]{1,0:T(8,128)S(1)}, f32[48,256]{1,0:T(8,128)}, u32[]{:S(2)}) copy-start(f32[48,256]{1,0:T(8,128)} %param.8) | copy-start | bytes 147460
  304.3 57.2 %copy-start.2 = (bf16[512,256]{1,0:T(8,128)(2,1)S(1)}, bf16[512,256]{1,0:T(8,128)(2,1)}, u32[]{:S(2)}) copy-start(bf16[512,256]{1,0:T(8,128)(2,1)} %param.7) | copy-start | bytes 786436
  361.5 159.6 %copy-start.1 = (bf16[768,896]{1,0:T(8,128)(2,1)S(1)}, bf16[768,896]{1,0:T(8,128)(2,1)}, u32[]{:S(2)}) copy-start(bf16[768,896]{1,0:T(8,128)(2,1)} %all-gather.3.cloned.1.call-done) | copy-start | bytes 4128772
Sparse Core Ops, SparseCore 0:
  11.2 95.5 all-gather.2
  110.0 138.3 all-gather.4
where the time goes:
time: 635 us; the launch traced here: 634 us
  blocking collectives  482 us (76%)
  waiting for transfers between devices  114 us (18%)
  between operations  15.5 us (2%)
  matrix products  11 us (2%)
  starting transfers between devices  7.96 us (1%)
    psum x1, blocking collectives, body(): projected = lax.psum(partial_value, 'fsdp').astype(jnp.bfloat16)  171 us
    psum x1, blocking collectives, body(): returned = lax.psum(partial_back, 'fsdp').astype(jnp.bfloat16)  159 us
    all_gather x1, waiting for transfers between devices, body(): panels = lax.all_gather(left_basis, 'blk', axis=0, tiled=True)  98.2 us
    psum x1, blocking collectives, body(): lax.psum((jnp.sum(gradient * gradient), unscaled_local), ('fsdp', 'blk'))  97.9 us
    all_gather x1, blocking collectives, body(): lax.all_gather(direction, 'blk', axis=0, tiled=True)  53.4 us
    all_to_all x1, waiting for transfers between devices, body(): lax.all_to_all(projected, 'blk', split_axis=0, concat_axis=1, tiled=True)  13.9 us
  transfers between devices with their start and end apart: 3, of which 2 were waited for; matrix products, arithmetic and copies ran while one was open for 1% of the time, Pallas kernels for 0%

commit v1 on v0

v1 whole, which is shorter than its diff:
```python
import jax
import jax.numpy as jnp
from jax import lax
from jax.sharding import Mesh, PartitionSpec as P

beta_first = 0.9
beta_second = 0.95
adam_eps = 1e-08
graft_eps = 1e-06

F = ("x", "y", "c")
B = ("z", "h")
f32 = jnp.float32
bf16 = jnp.bfloat16


def spread(block, axes, count):
    copies = jnp.broadcast_to(block[None], (count,) + block.shape)
    got = lax.all_to_all(copies, axes, 0, 0, tiled=True)
    return got.reshape((count * block.shape[0],) + block.shape[1:])


def collect(parts, axes, count):
    parts = parts.astype(bf16).reshape((count, parts.shape[0] // count) + parts.shape[1:])
    return jnp.sum(lax.all_to_all(parts, axes, 0, 0, tiled=True).astype(f32), axis=0)


def collect_cores(parts):
    half = parts.shape[0] // 2
    core = lax.axis_index("c")
    low, high = parts[:half], parts[half:]
    mine = jnp.where(core == 0, low, high)
    other = jnp.where(core == 0, high, low).astype(bf16)
    return mine + lax.ppermute(other, "c", [(0, 1), (1, 0)]).astype(f32)


def body(gradient, left_basis, right_basis, moment, variance):
    grad_b = gradient.astype(bf16)
    panels = spread(left_basis, B, 16)
    partial_value = jnp.dot(panels, grad_b, preferred_element_type=f32)
    rows = collect(collect_cores(partial_value), ("x", "y"), 16).astype(bf16)
    projected = lax.all_gather(spread(rows, ("x", "y"), 16), "c", axis=0, tiled=True)
    rotated = collect(
        jnp.dot(projected, right_basis, preferred_element_type=f32), B, 16
    )
    new_moment = beta_first * moment + (1.0 - beta_first) * rotated
    new_variance = beta_second * variance + (1.0 - beta_second) * rotated * rotated
    direction = (new_moment / (jnp.sqrt(new_variance) + adam_eps)).astype(bf16)
    partial_back = lax.dot_general(
        spread(direction, B, 16),
        right_basis,
        (((1,), (1,)), ((), ())),
        preferred_element_type=f32,
    )
    back = collect(collect_cores(partial_back), ("x", "y"), 16).astype(bf16)
    returned = lax.all_gather(spread(back, ("x", "y"), 16), "c", axis=0, tiled=True)
    unscaled = lax.dot_general(
        panels, returned, (((0,), (0,)), ((), ())), preferred_element_type=f32
    )
    lane = lax.broadcasted_iota(jnp.int32, (512, 128), 1)
    sums = jnp.where(lane == 0, jnp.sum(gradient * gradient), jnp.sum(unscaled * unscaled))
    sums = jnp.sum(lax.all_to_all(sums, F + B, 0, 0, tiled=True), axis=0)
    update = unscaled * (jnp.sqrt(sums[0]) / (jnp.sqrt(sums[1]) + graft_eps))
    return (update, new_moment, new_variance)


def solution(mesh):
    fine = Mesh(mesh.devices.reshape(4, 4, 2, 8, 2), F + B)
    return jax.shard_map(
        body,
        mesh=fine,
        in_specs=(P(F, B), P(B, F), P(B, F), P(B, F), P(B, F)),
        out_specs=(P(F, B), P(B, F), P(B, F)),
        check_vma=False,
    )
```

time: 635 us -> 247 us (0.39)
  blocking collectives: 482 us -> 146 us
  waiting for transfers between devices: 114 us -> 48.3 us
  starting transfers between devices: 7.96 us -> 32.3 us
  between operations: 15.5 us -> 2.15 us
  matrix products: 11 us -> 4.64 us
    psum x3 -> x0, blocking collectives: 428 us -> none  [the longest x1 171 us: body(): projected = lax.psum(partial_value, 'fsdp').astype(jnp.bfloat16)]
    all_to_all x0 -> x6, blocking collectives: none -> 138 us  [the longest x3 73.8 us: collect(): lax.all_to_all(parts, axes, 0, 0, tiled=True).astype(f32)]
    all_gather x2 -> x0, waiting for transfers between devices: 98.2 us -> none  [the longest x1 98.2 us: body(): panels = lax.all_gather(left_basis, 'blk', axis=0, tiled=True)]
    all_gather x1 -> x2, blocking collectives: 53.4 us -> 8.06 us  [the longest x1 4.32 us: body(): lax.all_gather(spread(back, ('x', 'y'), 16), 'c', axis=0, tiled=True)]
    all_to_all x1 -> x2, waiting for transfers between devices: 13.9 us -> 45.6 us  [spread(): got = lax.all_to_all(copies, axes, 0, 0, tiled=True)]
    all_to_all x1 -> x2, starting transfers between devices: 7.89 us -> 20.6 us  [spread(): got = lax.all_to_all(copies, axes, 0, 0, tiled=True)]
    ppermute x0 -> x2, starting transfers between devices: none -> 11.8 us  [collect_cores(): return mine + lax.ppermute(other, 'c', [(0, 1), (1, 0)]).astype(f32)]
  transfers between devices with their start and end apart: 3 -> 4, of which waited for: 2 -> 4; matrix products, arithmetic and copies ran while one was open for 1% -> 0% of each run, Pallas kernels for 0% -> 0%
where the time goes in v1:
time: 247 us; the launch traced here: 246 us
  blocking collectives  146 us (59%)
  waiting for transfers between devices  48.3 us (20%)
  starting transfers between devices  32.3 us (13%)
  other arithmetic  7.55 us (3%)
  local copies, waits for them, and re-layouts  5.45 us (2%)
  matrix products  4.64 us (2%)
    all_to_all x3, blocking collectives, collect(): lax.all_to_all(parts, axes, 0, 0, tiled=True).astype(f32)  73.8 us
    all_to_all x2, waiting for transfers between devices, spread(): got = lax.all_to_all(copies, axes, 0, 0, tiled=True)  45.6 us
    all_to_all x2, blocking collectives, spread(): got = lax.all_to_all(copies, axes, 0, 0, tiled=True)  37.6 us
    all_to_all x1, blocking collectives, body(): sums = jnp.sum(lax.all_to_all(sums, F + B, 0, 0, tiled=True), axis=0)  26.1 us
    all_to_all x2, starting transfers between devices, spread(): got = lax.all_to_all(copies, axes, 0, 0, tiled=True)  20.6 us
    ppermute x2, starting transfers between devices, collect_cores(): return mine + lax.ppermute(other, 'c', [(0, 1), (1, 0)]).astype(f32)  11.8 us
  transfers between devices with their start and end apart: 4, of which 4 were waited for; matrix products, arithmetic and copies ran while one was open for 0% of the time, Pallas kernels for 0%

profile of v1, /device:TPU:1, one launch (start us, length us, event | category | flops | bytes accessed | tf_op | source)
XLA Modules:
  0.0 246.0 jit_solution(3751591348401453862)
XLA Ops:
  0.6 2.1 broadcast_in_dim.14
  2.8 16.4 %all-to-all-start = ((bf16[16,48,896]{2,1,0:T(8,128)(2,1)}), bf16[16,48,896]{2,1,0:T(8,128)(2,1)S(1)}, u32[]{:S(2)}, u32[]{:S(2)}) async-start(bf16[16,48,896]{2,1,0:T(8,128)(2,1)} %broadcast_in_dim.14), calls=%async_computation | async-start | bytes 2752512 | tf_op jit(solution)/shard_map/all_to_all | solution.py:19
  19.1 34.2 %all-to-all-done = bf16[16,48,896]{2,1,0:T(8,128)(2,1)S(1)} async-done(((bf16[16,48,896]{2,1,0:T(8,128)(2,1)}), bf16[16,48,896]{2,1,0:T(8,128)(2,1)S(1)}, u32[]{:S(2)}, u32[]{:S(2)}) %all-to-all-start) | async-done | bytes 1376288 | tf_op jit(solution)/shard_map/all_to_all | solution.py:19
  54.4 5.8 %collective-permute-start = (bf16[384,512]{1,0:T(8,128)(2,1)S(1)}, bf16[384,512]{1,0:T(8,128)(2,1)S(1)}, u32[]{:S(2)}, u32[]{:S(2)}) collective-permute-start(bf16[384,512]{1,0:T(8,128)(2,1)S(1)} %select_convert_fusion.1), channel_id=1, source_target_pairs={{0,16},{16,0},{1,17},{17,1},{2,18},{18,2},{3,19},{19,3},{4,20},{20... | collective-permute-start | bytes 1179656 | tf_op jit(solution)/shard_map/ppermute | solution.py:34
  60.3 1.3 collective-permute-done
  61.8 32.2 %all_to_all.41 = bf16[16,24,512]{2,1,0:T(8,128)(2,1)} all-to-all(bf16[16,24,512]{2,1,0:T(8,128)(2,1)S(1)} %bitcast.21), channel_id=1, replica_groups=mesh['x'=4,'y'=4,'c'=2,'z'=8,'h'=2] {'x','y'}, dimensions={0} | all-to-all | bytes 786432 | tf_op jit(solution)/shard_map/all_to_all | solution.py:25
  94.0 1.1 reduce_sum.60
  95.1 16.3 %all_to_all.42 = bf16[16,24,512]{2,1,0:T(8,128)(2,1)S(1)} all-to-all(bf16[16,24,512]{2,1,0:T(8,128)(2,1)S(1)} %broadcast_in_dim.15), channel_id=1, replica_groups=mesh['x'=4,'y'=4,'c'=2,'z'=8,'h'=2] {'x','y'}, dimensions={0} | all-to-all | bytes 786432 | tf_op jit(solution)/shard_map/all_to_all | solution.py:19
  111.4 3.7 %all_gather.6 = bf16[768,512]{1,0:T(8,128)(2,1)S(1)} all-gather(bf16[384,512]{1,0:T(8,128)(2,1)S(1)} %bitcast.22), channel_id=1, replica_groups=mesh['x'=4,'y'=4,'c'=2,'z'=8,'h'=2] {'c'}, dimensions={0}, use_global_device_ids=true | all-gather | bytes 1179648 | tf_op jit(solution)/shard_map/all_gather | solution.py:42
  115.5 24.7 %all_to_all.43 = bf16[16,48,256]{2,1,0:T(8,128)(2,1)S(1)} all-to-all(bf16[16,48,256]{2,1,0:T(8,128)(2,1)S(1)} %bitcast.23), channel_id=1, replica_groups=mesh['x'=4,'y'=4,'c'=2,'z'=8,'h'=2] {'z','h'}, dimensions={0} | all-to-all | bytes 786432 | tf_op jit(solution)/shard_map/all_to_all | solution.py:25
  140.9 21.3 %all_to_all.44 = bf16[16,48,256]{2,1,0:T(8,128)(2,1)S(1)} all-to-all(bf16[16,48,256]{2,1,0:T(8,128)(2,1)S(1)} %broadcast_in_dim.16), channel_id=1, replica_groups=mesh['x'=4,'y'=4,'c'=2,'z'=8,'h'=2] {'z','h'}, dimensions={0} | all-to-all | bytes 786432 | tf_op jit(solution)/shard_map/all_to_all | solution.py:19
  162.7 5.9 %collective-permute-start.1 = (bf16[384,512]{1,0:T(8,128)(2,1)S(1)}, bf16[384,512]{1,0:T(8,128)(2,1)S(1)}, u32[]{:S(2)}, u32[]{:S(2)}) collective-permute-start(bf16[384,512]{1,0:T(8,128)(2,1)S(1)} %select_convert_fusion), channel_id=1, source_target_pairs={{0,16},{16,0},{1,17},{17,1},{2,18},{18,2},{3,19},{19,3},{4,20},{20... | collective-permute-start | bytes 1179656 | tf_op jit(solution)/shard_map/ppermute | solution.py:34
  168.6 1.3 collective-permute-done.1
  170.2 17.0 %all_to_all.45 = bf16[16,24,512]{2,1,0:T(8,128)(2,1)} all-to-all(bf16[16,24,512]{2,1,0:T(8,128)(2,1)S(1)} %bitcast.20), channel_id=1, replica_groups=mesh['x'=4,'y'=4,'c'=2,'z'=8,'h'=2] {'x','y'}, dimensions={0} | all-to-all | bytes 786432 | tf_op jit(solution)/shard_map/all_to_all | solution.py:25
  187.2 1.1 reduce_sum.62
  189.0 4.2 %all-to-all-start.6 = ((bf16[16,24,512]{2,1,0:T(8,128)(2,1)}), bf16[16,24,512]{2,1,0:T(8,128)(2,1)}, u32[]{:S(2)}, u32[]{:S(2)}) async-start(bf16[16,24,512]{2,1,0:T(8,128)(2,1)} %broadcast_in_dim.17), calls=%async_computation.6 | async-start | bytes 786432 | tf_op jit(solution)/shard_map/all_to_all | solution.py:19
  193.2 1.1 multiply_reduce_fusion.1
  194.4 11.4 %all-to-all-done.6 = bf16[16,24,512]{2,1,0:T(8,128)(2,1)} async-done(((bf16[16,24,512]{2,1,0:T(8,128)(2,1)}), bf16[16,24,512]{2,1,0:T(8,128)(2,1)}, u32[]{:S(2)}, u32[]{:S(2)}) %all-to-all-start.6) | async-done | bytes 393248 | tf_op jit(solution)/shard_map/all_to_all | solution.py:19
  205.8 4.3 %all_gather.7 = bf16[768,512]{1,0:T(8,128)(2,1)S(1)} all-gather(bf16[384,512]{1,0:T(8,128)(2,1)} %bitcast.6), channel_id=1, replica_groups=mesh['x'=4,'y'=4,'c'=2,'z'=8,'h'=2] {'c'}, dimensions={0}, use_global_device_ids=true | all-gather | bytes 1179648 | tf_op jit(solution)/shard_map/all_gather | solution.py:56
  210.1 2.9 %multiply_reduce_fusion = (f32[]{:T(128)}, f32[512,896]{1,0:T(8,128)}) fusion(bf16[768,512]{1,0:T(8,128)(2,1)S(1)} %all_gather.7, bf16[768,896]{1,0:T(8,128)(2,1)S(1)} %bitcast.19), kind=kOutput, calls=%fused_computation.1 | convolution fusion | flops 705560576 | bytes 3997700 | tf_op jit(solution)/shard_map/dot_general | solution.py:57
  213.0 1.3 compare_select_fusion
  214.5 26.1 %all_to_all.46 = f32[512,1,128]{2,1,0:T(1,128)S(1)} all-to-all(f32[512,1,128]{2,1,0:T(1,128)S(1)} %iota.7), channel_id=1, replica_groups=mesh['x'=4,'y'=4,'c'=2,'z'=8,'h'=2] {'x','y','c','z','h'}, dimensions={0} | all-to-all | bytes 524288 | tf_op jit(solution)/shard_map/all_to_all | solution.py:62
  242.7 1.6 multiply_bitcast_fusion
  244.3 1.7 copy.11
  (23 shorter events, 4.7 us)
Async XLA Ops:
  0.6 114.5 %copy-start = (bf16[512,256]{1,0:T(8,128)(2,1)S(1)}, bf16[512,256]{1,0:T(8,128)(2,1)}, u32[]{:S(2)}) copy-start(bf16[512,256]{1,0:T(8,128)(2,1)} %param.7) | copy-start | bytes 786436
  2.8 50.6 %copy-start.1 = (f32[896,512]{1,0:T(8,128)S(1)}, f32[896,512]{1,0:T(8,128)}, u32[]{:S(2)}) copy-start(f32[896,512]{1,0:T(8,128)} %param.5) | copy-start | bytes 5505028
  2.8 50.6 %all-to-all-start = ((bf16[16,48,896]{2,1,0:T(8,128)(2,1)}), bf16[16,48,896]{2,1,0:T(8,128)(2,1)S(1)}, u32[]{:S(2)}, u32[]{:S(2)}) async-start(bf16[16,48,896]{2,1,0:T(8,128)(2,1)} %broadcast_in_dim.14), calls=%async_computation | async-start | bytes 2752512 | tf_op jit(solution)/shard_map/all_to_all | solution.py:19
  54.4 7.2 %collective-permute-start = (bf16[384,512]{1,0:T(8,128)(2,1)S(1)}, bf16[384,512]{1,0:T(8,128)(2,1)S(1)}, u32[]{:S(2)}, u32[]{:S(2)}) collective-permute-start(bf16[384,512]{1,0:T(8,128)(2,1)S(1)} %select_convert_fusion.1), channel_id=1, source_target_pairs={{0,16},{16,0},{1,17},{17,1},{2,18},{18,2},{3,19},{19,3},{4,20},{20... | collective-permute-start | bytes 1179656 | tf_op jit(solution)/shard_map/ppermute | solution.py:34
  115.1 25.1 %copy-start.2 = (f32[48,256]{1,0:T(8,128)S(1)}, f32[48,256]{1,0:T(8,128)}, u32[]{:S(2)}) copy-start(f32[48,256]{1,0:T(8,128)} %param.9) | copy-start | bytes 147460
  115.1 25.1 %copy-start.3 = (f32[48,256]{1,0:T(8,128)S(1)}, f32[48,256]{1,0:T(8,128)}, u32[]{:S(2)}) copy-start(f32[48,256]{1,0:T(8,128)} %param.8) | copy-start | bytes 147460
  162.7 7.2 %collective-permute-start.1 = (bf16[384,512]{1,0:T(8,128)(2,1)S(1)}, bf16[384,512]{1,0:T(8,128)(2,1)S(1)}, u32[]{:S(2)}, u32[]{:S(2)}) collective-permute-start(bf16[384,512]{1,0:T(8,128)(2,1)S(1)} %select_convert_fusion), channel_id=1, source_target_pairs={{0,16},{16,0},{1,17},{17,1},{2,18},{18,2},{3,19},{19,3},{4,20},{20... | collective-permute-start | bytes 1179656 | tf_op jit(solution)/shard_map/ppermute | solution.py:34
  189.0 16.7 %all-to-all-start.6 = ((bf16[16,24,512]{2,1,0:T(8,128)(2,1)}), bf16[16,24,512]{2,1,0:T(8,128)(2,1)}, u32[]{:S(2)}, u32[]{:S(2)}) async-start(bf16[16,24,512]{2,1,0:T(8,128)(2,1)} %broadcast_in_dim.17), calls=%async_computation.6 | async-start | bytes 786432 | tf_op jit(solution)/shard_map/all_to_all | solution.py:19

commit v2 on v1

v2 whole, which is shorter than its diff:
```python
import jax
import jax.numpy as jnp
from jax import lax
from jax.sharding import Mesh, PartitionSpec as P

beta_first = 0.9
beta_second = 0.95
adam_eps = 1e-08
graft_eps = 1e-06

F = ("x", "y", "c")
B = ("z", "h")
PAIR = [(0, 1), (1, 0)]
f32 = jnp.float32
bf16 = jnp.bfloat16


def spread(block, axes, count):
    copies = jnp.broadcast_to(block[None], (count,) + block.shape)
    return lax.all_to_all(copies, axes, 0, 0, tiled=True)


def collect(parts, axes):
    got = lax.all_to_all(parts.astype(bf16), axes, 0, 0, tiled=True)
    terms = [got[i].astype(f32) for i in range(got.shape[0])]
    while len(terms) > 1:
        terms = [a + b for a, b in zip(terms[::2], terms[1::2])]
    return terms[0]


def collect_rows(low, high):
    core = lax.axis_index("c")
    mine = jnp.where(core == 0, low, high)
    other = jnp.where(core == 0, high, low).astype(bf16)
    half = mine + lax.ppermute(other, "c", PAIR).astype(f32)
    return collect(half.reshape(16, 24, half.shape[-1]), ("x", "y"))


def gather_rows(rows):
    half = spread(rows, ("x", "y"), 16).reshape(384, rows.shape[-1])
    return lax.all_gather(half, "c", axis=0, tiled=True)


def body(gradient, left_basis, right_basis, moment, variance):
    theirs = lax.ppermute(left_basis, "h", PAIR)
    moments = lax.ppermute(jnp.stack([moment, variance]), "h", PAIR)
    moment = jnp.concatenate([moment, moments[0]])
    variance = jnp.concatenate([variance, moments[1]])

    grad_b = gradient.astype(bf16)
    panels_own = spread(left_basis, "z", 8).reshape(384, 896)
    panels_other = spread(theirs, "z", 8).reshape(384, 896)
    projected = gather_rows(
        collect_rows(
            jnp.dot(panels_own, grad_b, preferred_element_type=f32),
            jnp.dot(panels_other, grad_b, preferred_element_type=f32),
        ).astype(bf16)
    )
    partial_rot = jnp.dot(projected, right_basis, preferred_element_type=f32).astype(bf16)
    partial_rot = partial_rot.reshape(2, 8, 48, 256).transpose(1, 0, 2, 3).reshape(8, 96, 256)
    rotated = collect(partial_rot, "z")
    partner = lax.ppermute(rotated, "h", PAIR)
    rotated = rotated + jnp.concatenate([partner[48:], partner[:48]])
    new_moment = beta_first * moment + (1.0 - beta_first) * rotated
    new_variance = beta_second * variance + (1.0 - beta_second) * rotated * rotated
    direction = (new_moment / (jnp.sqrt(new_variance) + adam_eps)).astype(bf16)
    directions = spread(direction, "z", 8).reshape(8, 2, 48, 256)
    directions = directions.transpose(1, 0, 2, 3).reshape(768, 256)
    partial_back = lax.dot_general(
        directions, right_basis, (((1,), (1,)), ((), ())), preferred_element_type=f32
    )
    returned = gather_rows(collect_rows(partial_back[:384], partial_back[384:]).astype(bf16))
    panels = jnp.concatenate([panels_own, panels_other])
    unscaled = lax.dot_general(
        panels, returned, (((0,), (0,)), ((), ())), preferred_element_type=f32
    )
    lane = lax.broadcasted_iota(jnp.int32, (1, 128), 1)
    sums = jnp.where(lane == 0, jnp.sum(gradient * gradient), jnp.sum(unscaled * unscaled))
    sums = jnp.sum(lax.all_gather(sums, "c"), axis=0)
    sums = jnp.sum(spread(sums, ("x", "y", "z", "h"), 256), axis=(0, 1))
    update = unscaled * (jnp.sqrt(sums[0]) / (jnp.sqrt(sums[1]) + graft_eps))
    return (update, new_moment[:48], new_variance[:48])


def solution(mesh):
    fine = Mesh(mesh.devices.reshape(4, 4, 2, 8, 2), F + B)
    return jax.shard_map(
        body,
        mesh=fine,
        in_specs=(P(F, B), P(B, F), P(B, F), P(B, F), P(B, F)),
        out_specs=(P(F, B), P(B, F), P(B, F)),
        check_vma=False,
    )
```

time: 247 us -> 233 us (0.943)
  blocking collectives: 146 us -> 77.5 us
  waiting for transfers between devices: 48.3 us -> 76.1 us
  starting transfers between devices: 32.3 us -> 57.6 us
    all_to_all x6 -> x4, blocking collectives: 138 us -> 67.8 us  [the longest x2 35.7 us: collect(): got = lax.all_to_all(parts.astype(bf16), axes, 0, 0, tiled=True)]
    all_to_all x2 -> x5, waiting for transfers between devices: 45.6 us -> 64.2 us  [the longest x4 54 us: spread(): return lax.all_to_all(copies, axes, 0, 0, tiled=True)]
    ppermute x2 -> x5, starting transfers between devices: 11.8 us -> 25.2 us  [the longest x2 8.28 us: collect_rows(): half = mine + lax.ppermute(other, 'c', PAIR).astype(f32)]
    all_to_all x2 -> x5, starting transfers between devices: 20.6 us -> 32.3 us  [the longest x4 28.9 us: spread(): return lax.all_to_all(copies, axes, 0, 0, tiled=True)]
    ppermute x2 -> x5, waiting for transfers between devices: 2.65 us -> 11.9 us  [the longest x1 7.3 us: body(): partner = lax.ppermute(rotated, 'h', PAIR)]
    all_gather x2 -> x3, blocking collectives: 8.06 us -> 9.67 us  [the longest x2 7.83 us: gather_rows(): return lax.all_gather(half, 'c', axis=0, tiled=True)]
  transfers between devices with their start and end apart: 4 -> 10, of which waited for: 4 -> 9; matrix products, arithmetic and copies ran while one was open for 0% -> 2% of each run, Pallas kernels for 0% -> 0%
where the time goes in v2:
time: 233 us; the launch traced here: 232 us
  blocking collectives  77.5 us (33%)
  waiting for transfers between devices  76.1 us (33%)
  starting transfers between devices  57.6 us (25%)
  matrix products  6.95 us (3%)
  local copies, waits for them, and re-layouts  5.91 us (3%)
  other arithmetic  5.36 us (2%)
    all_to_all x4, waiting for transfers between devices, spread(): return lax.all_to_all(copies, axes, 0, 0, tiled=True)  54 us
    all_to_all x2, blocking collectives, collect(): got = lax.all_to_all(parts.astype(bf16), axes, 0, 0, tiled=True)  35.7 us
    all_to_all x2, blocking collectives, spread(): return lax.all_to_all(copies, axes, 0, 0, tiled=True)  32.1 us
    all_to_all x4, starting transfers between devices, spread(): return lax.all_to_all(copies, axes, 0, 0, tiled=True)  28.9 us
    all_to_all x1, waiting for transfers between devices, collect(): got = lax.all_to_all(parts.astype(bf16), axes, 0, 0, tiled=True)  10.3 us
    ppermute x2, starting transfers between devices, collect_rows(): half = mine + lax.ppermute(other, 'c', PAIR).astype(f32)  8.28 us
    all_gather x2, blocking collectives, gather_rows(): return lax.all_gather(half, 'c', axis=0, tiled=True)  7.83 us
    ppermute x1, starting transfers between devices, body(): theirs = lax.ppermute(left_basis, 'h', PAIR)  7.45 us
  transfers between devices with their start and end apart: 10, of which 9 were waited for; matrix products, arithmetic and copies ran while one was open for 2% of the time, Pallas kernels for 0%

profile of v2, /device:TPU:1, one launch (start us, length us, event | category | flops | bytes accessed | tf_op | source)
XLA Modules:
  0.0 231.7 jit_solution(1779840530922045871)
XLA Ops:
  2.5 11.0 %all-to-all-start = ((bf16[8,48,896]{2,1,0:T(8,128)(2,1)}), bf16[8,48,896]{2,1,0:T(8,128)(2,1)S(1)}, u32[]{:S(2)}, u32[]{:S(2)}) async-start(bf16[8,48,896]{2,1,0:T(8,128)(2,1)} %broadcast_in_dim.26), calls=%async_computation | async-start | bytes 1376256 | tf_op jit(solution)/shard_map/all_to_all | solution.py:20
  13.5 7.5 %collective-permute-start = (bf16[48,896]{1,0:T(8,128)(2,1)S(1)}, bf16[48,896]{1,0:T(8,128)(2,1)S(1)}, u32[]{:S(2)}, u32[]{:S(2)}) collective-permute-start(bf16[48,896]{1,0:T(8,128)(2,1)S(1)} %copy-done.6), channel_id=1, source_target_pairs={{0,1},{1,0},{2,3},{3,2},{4,5},{5,4},{6,7},{7,6},{8,9},{9,8},{10,11... | collective-permute-start | bytes 258056 | tf_op jit(solution)/shard_map/ppermute | solution.py:45
  21.0 2.0 collective-permute-done
  22.9 12.0 %all-to-all-done = bf16[8,48,896]{2,1,0:T(8,128)(2,1)S(1)} async-done(((bf16[8,48,896]{2,1,0:T(8,128)(2,1)}), bf16[8,48,896]{2,1,0:T(8,128)(2,1)S(1)}, u32[]{:S(2)}, u32[]{:S(2)}) %all-to-all-start) | async-done | bytes 688160 | tf_op jit(solution)/shard_map/all_to_all | solution.py:20
  36.0 4.2 %all-to-all-start.1 = ((bf16[8,48,896]{2,1,0:T(8,128)(2,1)}), bf16[8,48,896]{2,1,0:T(8,128)(2,1)}, u32[]{:S(2)}, u32[]{:S(2)}) async-start(bf16[8,48,896]{2,1,0:T(8,128)(2,1)} %broadcast_in_dim.27), calls=%async_computation.1 | async-start | bytes 1376256 | tf_op jit(solution)/shard_map/all_to_all | solution.py:20
  41.9 18.0 %all-to-all-done.1 = bf16[8,48,896]{2,1,0:T(8,128)(2,1)} async-done(((bf16[8,48,896]{2,1,0:T(8,128)(2,1)}), bf16[8,48,896]{2,1,0:T(8,128)(2,1)}, u32[]{:S(2)}, u32[]{:S(2)}) %all-to-all-start.1) | async-done | bytes 688160 | tf_op jit(solution)/shard_map/all_to_all | solution.py:20
  61.6 4.2 %collective-permute-start.2 = (bf16[384,512]{1,0:T(8,128)(2,1)S(1)}, bf16[384,512]{1,0:T(8,128)(2,1)S(1)}, u32[]{:S(2)}, u32[]{:S(2)}) collective-permute-start(bf16[384,512]{1,0:T(8,128)(2,1)S(1)} %get-tuple-element.15), channel_id=1, source_target_pairs={{0,16},{16,0},{1,17},{17,1},{2,18},{18,2},{3,19},{19,3},{4,20},{20... | collective-permute-start | bytes 1179656 | tf_op jit(solution)/shard_map/ppermute | solution.py:35
  67.3 19.9 %all_to_all.45 = bf16[16,24,512]{2,1,0:T(8,128)(2,1)S(1)} all-to-all(bf16[16,24,512]{2,1,0:T(8,128)(2,1)S(1)} %bitcast.44), channel_id=1, replica_groups=mesh['x'=4,'y'=4,'c'=2,'z'=8,'h'=2] {'x','y'}, dimensions={0} | all-to-all | bytes 786432 | tf_op jit(solution)/shard_map/all_to_all | solution.py:24
  87.3 16.3 %all_to_all.46 = bf16[16,24,512]{2,1,0:T(8,128)(2,1)S(1)} all-to-all(bf16[16,24,512]{2,1,0:T(8,128)(2,1)S(1)} %broadcast_in_dim.53), channel_id=1, replica_groups=mesh['x'=4,'y'=4,'c'=2,'z'=8,'h'=2] {'x','y'}, dimensions={0} | all-to-all | bytes 786432 | tf_op jit(solution)/shard_map/all_to_all | solution.py:20
  103.6 3.9 %all_gather.10 = bf16[768,512]{1,0:T(8,128)(2,1)S(1)} all-gather(bf16[384,512]{1,0:T(8,128)(2,1)S(1)} %bitcast.47), channel_id=1, replica_groups=mesh['x'=4,'y'=4,'c'=2,'z'=8,'h'=2] {'c'}, dimensions={0}, use_global_device_ids=true | all-gather | bytes 1179648 | tf_op jit(solution)/shard_map/all_gather | solution.py:41
  108.6 3.5 %all-to-all-start.4 = ((bf16[8,96,256]{2,1,0:T(8,128)(2,1)}), bf16[8,96,256]{2,1,0:T(8,128)(2,1)S(1)}, u32[]{:S(2)}, u32[]{:S(2)}) async-start(bf16[8,96,256]{2,1,0:T(8,128)(2,1)} %bitcast.9), calls=%async_computation.4 | async-start | bytes 786432 | tf_op jit(solution)/shard_map/all_to_all | solution.py:24
  112.1 4.8 %collective-permute-start.1 = (f32[2,48,256]{2,1,0:T(8,128)S(1)}, f32[2,48,256]{2,1,0:T(8,128)S(1)}, u32[]{:S(2)}, u32[]{:S(2)}) collective-permute-start(f32[2,48,256]{2,1,0:T(8,128)S(1)} %pad_maximum_fusion), channel_id=1, source_target_pairs={{0,1},{1,0},{2,3},{3,2},{4,5},{5,4},{6,7},{7,6},{8,9},{9,8},{10,11... | collective-permute-start | bytes 294920 | tf_op jit(solution)/shard_map/ppermute | solution.py:46
  116.9 10.3 %all-to-all-done.4 = bf16[8,96,256]{2,1,0:T(8,128)(2,1)S(1)} async-done(((bf16[8,96,256]{2,1,0:T(8,128)(2,1)}), bf16[8,96,256]{2,1,0:T(8,128)(2,1)S(1)}, u32[]{:S(2)}, u32[]{:S(2)}) %all-to-all-start.4) | async-done | bytes 393248 | tf_op jit(solution)/shard_map/all_to_all | solution.py:24
  127.2 4.8 %collective-permute-start.3 = (f32[96,256]{1,0:T(8,128)S(1)}, f32[96,256]{1,0:T(8,128)S(1)}, u32[]{:S(2)}, u32[]{:S(2)}) collective-permute-start(f32[96,256]{1,0:T(8,128)S(1)} %fusion.32), channel_id=1, source_target_pairs={{0,1},{1,0},{2,3},{3,2},{4,5},{5,4},{6,7},{7,6},{8,9},{9,8},{10,11... | collective-permute-start | bytes 294920 | tf_op jit(solution)/shard_map/ppermute | solution.py:62
  132.0 7.3 %collective-permute-done.3 = f32[96,256]{1,0:T(8,128)S(1)} collective-permute-done((f32[96,256]{1,0:T(8,128)S(1)}, f32[96,256]{1,0:T(8,128)S(1)}, u32[]{:S(2)}, u32[]{:S(2)}) %collective-permute-start.3) | collective-permute-done | bytes 98336 | tf_op jit(solution)/shard_map/ppermute | solution.py:62
  139.5 15.8 %all_to_all.47 = bf16[8,96,256]{2,1,0:T(8,128)(2,1)S(1)} all-to-all(bf16[8,96,256]{2,1,0:T(8,128)(2,1)S(1)} %broadcast_in_dim.55), channel_id=1, replica_groups=mesh['x'=4,'y'=4,'c'=2,'z'=8,'h'=2] {'z'}, dimensions={0} | all-to-all | bytes 786432 | tf_op jit(solution)/shard_map/all_to_all | solution.py:20
  155.8 4.1 %collective-permute-start.4 = (bf16[384,512]{1,0:T(8,128)(2,1)S(1)}, bf16[384,512]{1,0:T(8,128)(2,1)S(1)}, u32[]{:S(2)}, u32[]{:S(2)}) collective-permute-start(bf16[384,512]{1,0:T(8,128)(2,1)S(1)} %select_convert_fusion), channel_id=1, source_target_pairs={{0,16},{16,0},{1,17},{17,1},{2,18},{18,2},{3,19},{19,3},{4,20},{20... | collective-permute-start | bytes 1179656 | tf_op jit(solution)/shard_map/ppermute | solution.py:35
  161.5 15.8 %all_to_all.48 = bf16[16,24,512]{2,1,0:T(8,128)(2,1)S(1)} all-to-all(bf16[16,24,512]{2,1,0:T(8,128)(2,1)S(1)} %bitcast.45), channel_id=1, replica_groups=mesh['x'=4,'y'=4,'c'=2,'z'=8,'h'=2] {'x','y'}, dimensions={0} | all-to-all | bytes 786432 | tf_op jit(solution)/shard_map/all_to_all | solution.py:24
  178.1 4.3 %all-to-all-start.7 = ((bf16[16,24,512]{2,1,0:T(8,128)(2,1)}), bf16[16,24,512]{2,1,0:T(8,128)(2,1)}, u32[]{:S(2)}, u32[]{:S(2)}) async-start(bf16[16,24,512]{2,1,0:T(8,128)(2,1)} %broadcast_in_dim.57), calls=%async_computation.7 | async-start | bytes 786432 | tf_op jit(solution)/shard_map/all_to_all | solution.py:20
  183.5 11.8 %all-to-all-done.7 = bf16[16,24,512]{2,1,0:T(8,128)(2,1)} async-done(((bf16[16,24,512]{2,1,0:T(8,128)(2,1)}), bf16[16,24,512]{2,1,0:T(8,128)(2,1)}, u32[]{:S(2)}, u32[]{:S(2)}) %all-to-all-start.7) | async-done | bytes 393248 | tf_op jit(solution)/shard_map/all_to_all | solution.py:20
  195.4 4.0 %all_gather.11 = bf16[768,512]{1,0:T(8,128)(2,1)S(1)} all-gather(bf16[384,512]{1,0:T(8,128)(2,1)} %bitcast.19), channel_id=1, replica_groups=mesh['x'=4,'y'=4,'c'=2,'z'=8,'h'=2] {'c'}, dimensions={0}, use_global_device_ids=true | all-gather | bytes 1179648 | tf_op jit(solution)/shard_map/all_gather | solution.py:41
  199.3 2.8 %multiply_reduce_fusion = (f32[]{:T(128)}, f32[896,512]{1,0:T(8,128)S(1)}) fusion(bf16[768,512]{1,0:T(8,128)(2,1)S(1)} %all_gather.11, bf16[384,896]{1,0:T(8,128)(2,1)} %bitcast.1, bf16[384,896]{1,0:T(8,128)(2,1)S(1)} %bitcast.43), kind=kOutput, calls=%fused_computation | convolution fusion | flops 708313088 | bytes 3997700 | tf_op jit(solution)/shard_map/dot_general | solution.py:74
  206.1 9.3 %all-to-all-start.8 = ((f32[256,1,128]{2,1,0:T(1,128)}), f32[256,1,128]{2,1,0:T(1,128)S(1)}, u32[]{:S(2)}, u32[]{:S(2)}) async-start(f32[256,1,128]{2,1,0:T(1,128)} %broadcast_in_dim.60), calls=%async_computation.8 | async-start | bytes 262144 | tf_op jit(solution)/shard_map/all_to_all | solution.py:20
  216.1 12.1 %all-to-all-done.8 = f32[256,1,128]{2,1,0:T(1,128)S(1)} async-done(((f32[256,1,128]{2,1,0:T(1,128)}), f32[256,1,128]{2,1,0:T(1,128)S(1)}, u32[]{:S(2)}, u32[]{:S(2)}) %all-to-all-start.8) | async-done | bytes 131104 | tf_op jit(solution)/shard_map/all_to_all | solution.py:20
  (48 shorter events, 19.9 us)
Async XLA Ops:
  0.6 106.8 %copy-start = (bf16[512,256]{1,0:T(8,128)(2,1)S(1)}, bf16[512,256]{1,0:T(8,128)(2,1)}, u32[]{:S(2)}) copy-start(bf16[512,256]{1,0:T(8,128)(2,1)} %param.7) | copy-start | bytes 786436
  0.6 12.9 %copy-start.6 = (bf16[48,896]{1,0:T(8,128)(2,1)S(1)}, bf16[48,896]{1,0:T(8,128)(2,1)}, u32[]{:S(2)}) copy-start(bf16[48,896]{1,0:T(8,128)(2,1)} %param.6) | copy-start | bytes 258052
  2.5 37.7 %copy-start.1 = (f32[896,512]{1,0:T(8,128)S(1)}, f32[896,512]{1,0:T(8,128)}, u32[]{:S(2)}) copy-start(f32[896,512]{1,0:T(8,128)} %param.5) | copy-start | bytes 5505028
  2.5 32.5 %all-to-all-start = ((bf16[8,48,896]{2,1,0:T(8,128)(2,1)}), bf16[8,48,896]{2,1,0:T(8,128)(2,1)S(1)}, u32[]{:S(2)}, u32[]{:S(2)}) async-start(bf16[8,48,896]{2,1,0:T(8,128)(2,1)} %broadcast_in_dim.26), calls=%async_computation | async-start | bytes 1376256 | tf_op jit(solution)/shard_map/all_to_all | solution.py:20
  13.5 9.4 %collective-permute-start = (bf16[48,896]{1,0:T(8,128)(2,1)S(1)}, bf16[48,896]{1,0:T(8,128)(2,1)S(1)}, u32[]{:S(2)}, u32[]{:S(2)}) collective-permute-start(bf16[48,896]{1,0:T(8,128)(2,1)S(1)} %copy-done.6), channel_id=1, source_target_pairs={{0,1},{1,0},{2,3},{3,2},{4,5},{5,4},{6,7},{7,6},{8,9},{9,8},{10,11... | collective-permute-start | bytes 258056 | tf_op jit(solution)/shard_map/ppermute | solution.py:45
  35.0 5.2 %copy-start.2 = (bf16[8,48,896]{2,1,0:T(8,128)(2,1)}, bf16[8,48,896]{2,1,0:T(8,128)(2,1)S(1)}, u32[]{:S(2)}) copy-start(bf16[8,48,896]{2,1,0:T(8,128)(2,1)S(1)} %all-to-all-done) | copy-start | bytes 2064388
  36.0 23.9 %all-to-all-start.1 = ((bf16[8,48,896]{2,1,0:T(8,128)(2,1)}), bf16[8,48,896]{2,1,0:T(8,128)(2,1)}, u32[]{:S(2)}, u32[]{:S(2)}) async-start(bf16[8,48,896]{2,1,0:T(8,128)(2,1)} %broadcast_in_dim.27), calls=%async_computation.1 | async-start | bytes 1376256 | tf_op jit(solution)/shard_map/all_to_all | solution.py:20
  61.6 5.5 %collective-permute-start.2 = (bf16[384,512]{1,0:T(8,128)(2,1)S(1)}, bf16[384,512]{1,0:T(8,128)(2,1)S(1)}, u32[]{:S(2)}, u32[]{:S(2)}) collective-permute-start(bf16[384,512]{1,0:T(8,128)(2,1)S(1)} %get-tuple-element.15), channel_id=1, source_target_pairs={{0,16},{16,0},{1,17},{17,1},{2,18},{18,2},{3,19},{19,3},{4,20},{20... | collective-permute-start | bytes 1179656 | tf_op jit(solution)/shard_map/ppermute | solution.py:35
  103.6 8.5 %copy-start.4 = (f32[48,256]{1,0:T(8,128)S(1)}, f32[48,256]{1,0:T(8,128)}, u32[]{:S(2)}) copy-start(f32[48,256]{1,0:T(8,128)} %param.9) | copy-start | bytes 147460
  103.6 8.5 %copy-start.5 = (f32[48,256]{1,0:T(8,128)S(1)}, f32[48,256]{1,0:T(8,128)}, u32[]{:S(2)}) copy-start(f32[48,256]{1,0:T(8,128)} %param.8) | copy-start | bytes 147460
  108.6 18.5 %all-to-all-start.4 = ((bf16[8,96,256]{2,1,0:T(8,128)(2,1)}), bf16[8,96,256]{2,1,0:T(8,128)(2,1)S(1)}, u32[]{:S(2)}, u32[]{:S(2)}) async-start(bf16[8,96,256]{2,1,0:T(8,128)(2,1)} %bitcast.9), calls=%async_computation.4 | async-start | bytes 786432 | tf_op jit(solution)/shard_map/all_to_all | solution.py:24
  112.1 19.9 %collective-permute-start.1 = (f32[2,48,256]{2,1,0:T(8,128)S(1)}, f32[2,48,256]{2,1,0:T(8,128)S(1)}, u32[]{:S(2)}, u32[]{:S(2)}) collective-permute-start(f32[2,48,256]{2,1,0:T(8,128)S(1)} %pad_maximum_fusion), channel_id=1, source_target_pairs={{0,1},{1,0},{2,3},{3,2},{4,5},{5,4},{6,7},{7,6},{8,9},{9,8},{10,11... | collective-permute-start | bytes 294920 | tf_op jit(solution)/shard_map/ppermute | solution.py:46
  127.2 12.1 %collective-permute-start.3 = (f32[96,256]{1,0:T(8,128)S(1)}, f32[96,256]{1,0:T(8,128)S(1)}, u32[]{:S(2)}, u32[]{:S(2)}) collective-permute-start(f32[96,256]{1,0:T(8,128)S(1)} %fusion.32), channel_id=1, source_target_pairs={{0,1},{1,0},{2,3},{3,2},{4,5},{5,4},{6,7},{7,6},{8,9},{9,8},{10,11... | collective-permute-start | bytes 294920 | tf_op jit(solution)/shard_map/ppermute | solution.py:62
  155.8 5.4 %collective-permute-start.4 = (bf16[384,512]{1,0:T(8,128)(2,1)S(1)}, bf16[384,512]{1,0:T(8,128)(2,1)S(1)}, u32[]{:S(2)}, u32[]{:S(2)}) collective-permute-start(bf16[384,512]{1,0:T(8,128)(2,1)S(1)} %select_convert_fusion), channel_id=1, source_target_pairs={{0,16},{16,0},{1,17},{17,1},{2,18},{18,2},{3,19},{19,3},{4,20},{20... | collective-permute-start | bytes 1179656 | tf_op jit(solution)/shard_map/ppermute | solution.py:35
  178.1 21.2 %copy-start.3 = (bf16[8,48,896]{2,1,0:T(8,128)(2,1)S(1)}, bf16[8,48,896]{2,1,0:T(8,128)(2,1)}, u32[]{:S(2)}) copy-start(bf16[8,48,896]{2,1,0:T(8,128)(2,1)} %copy-done.2) | copy-start | bytes 2064388
  178.1 17.2 %all-to-all-start.7 = ((bf16[16,24,512]{2,1,0:T(8,128)(2,1)}), bf16[16,24,512]{2,1,0:T(8,128)(2,1)}, u32[]{:S(2)}, u32[]{:S(2)}) async-start(bf16[16,24,512]{2,1,0:T(8,128)(2,1)} %broadcast_in_dim.57), calls=%async_computation.7 | async-start | bytes 786432 | tf_op jit(solution)/shard_map/all_to_all | solution.py:20
  206.1 22.2 %all-to-all-start.8 = ((f32[256,1,128]{2,1,0:T(1,128)}), f32[256,1,128]{2,1,0:T(1,128)S(1)}, u32[]{:S(2)}, u32[]{:S(2)}) async-start(f32[256,1,128]{2,1,0:T(1,128)} %broadcast_in_dim.60), calls=%async_computation.8 | async-start | bytes 262144 | tf_op jit(solution)/shard_map/all_to_all | solution.py:20

commit v3 on v2

v3 whole, which is shorter than its diff:
```python
import jax
import jax.numpy as jnp
from jax import lax
from jax.experimental import pallas as pl
from jax.experimental.pallas import tpu as pltpu
from jax.sharding import Mesh, PartitionSpec as P

beta_first = 0.9
beta_second = 0.95
adam_eps = 1e-08
graft_eps = 1e-06

F = ("x", "y", "c")
B = ("z", "h")
SWAP = [(0, 1), (1, 0)]
TURN = [(16 * i + j, 16 * j + i) for i in range(16) for j in range(16)]
STEP = 4
f32 = jnp.float32
bf16 = jnp.bfloat16


def rotate_kernel(rows_ref, basis_ref, out_ref):
    rows = rows_ref[...]
    for j in range(STEP):
        out_ref[j] = jnp.dot(rows, basis_ref[j], preferred_element_type=f32).astype(bf16)


def rotate(rows, basis):
    return pl.pallas_call(
        rotate_kernel,
        grid=(32 // STEP,),
        in_specs=[
            pl.BlockSpec((24, 512), lambda i: (0, 0)),
            pl.BlockSpec((STEP, 512, 256), lambda i: (i, 0, 0)),
        ],
        out_specs=pl.BlockSpec((STEP, 24, 256), lambda i: (i, 0, 0)),
        out_shape=jax.ShapeDtypeStruct((32, 24, 256), bf16),
        cost_estimate=pl.CostEstimate(
            flops=2 * 24 * 512 * 8192, bytes_accessed=2 * 512 * 8192, transcendentals=0
        ),
    )(rows, basis)


def back_kernel(direction_ref, basis_ref, out_ref, total_ref):
    step = pl.program_id(0)

    @pl.when(step == 0)
    def _():
        total_ref[...] = jnp.zeros_like(total_ref)

    total = total_ref[...]
    for j in range(STEP):
        total += lax.dot_general(
            direction_ref[j], basis_ref[j], (((1,), (1,)), ((), ())), preferred_element_type=f32
        )
    total_ref[...] = total

    @pl.when(step == pl.num_programs(0) - 1)
    def _():
        out_ref[...] = total_ref[...].astype(bf16)


def rotate_back(direction, basis):
    return pl.pallas_call(
        back_kernel,
        grid=(32 // STEP,),
        in_specs=[
            pl.BlockSpec((STEP, 24, 256), lambda i: (i, 0, 0)),
            pl.BlockSpec((STEP, 512, 256), lambda i: (i, 0, 0)),
        ],
        out_specs=pl.BlockSpec((24, 512), lambda i: (0, 0)),
        out_shape=jax.ShapeDtypeStruct((24, 512), bf16),
        scratch_shapes=[pltpu.VMEM((24, 512), f32)],
        cost_estimate=pl.CostEstimate(
            flops=2 * 24 * 512 * 8192, bytes_accessed=2 * 512 * 8192, transcendentals=0
        ),
    )(direction, basis)


def spread(block, axes, count):
    copies = jnp.broadcast_to(block[None], (count,) + block.shape)
    return lax.all_to_all(copies, axes, 0, 0, tiled=True)


def collect(parts, axes):
    got = lax.all_to_all(parts, axes, 0, 0, tiled=True)
    terms = [got[i].astype(f32) for i in range(got.shape[0])]
    while len(terms) > 1:
        terms = [a + b for a, b in zip(terms[::2], terms[1::2])]
    return terms[0]


def body(gradient, left_basis, right_basis, moment, variance):
    first = lax.axis_index("c") == 0

    def sort(mine, theirs):
        return jnp.where(first, mine, theirs), jnp.where(first, theirs, mine)

    basis = lax.all_gather(right_basis, F)

    moments = jnp.stack([moment, variance])
    keep, send = sort(moments[:, :24], moments[:, 24:])
    blocks = sort(keep, lax.ppermute(send, "c", SWAP))
    moments = lax.ppermute(jnp.stack(blocks, axis=1), ("x", "y", "z", "h"), TURN)

    grad_b = gradient.astype(bf16)
    panels = spread(lax.all_gather(left_basis, "h", tiled=True), "z", 8).reshape(768, 896)
    partial_value = jnp.dot(panels, grad_b, preferred_element_type=f32).reshape(16, 2, 24, 512)
    keep, send = sort(partial_value[:, 0], partial_value[:, 1])
    keep += lax.ppermute(send.astype(bf16), "c", SWAP).astype(f32)
    projected = collect(keep.astype(bf16), ("x", "y")).astype(bf16)

    rotated = rotate(projected, basis).reshape(16, 2, 24, 256)
    rotated = collect(rotated, B)
    new_moment = beta_first * moments[0] + (1.0 - beta_first) * rotated
    new_variance = beta_second * moments[1] + (1.0 - beta_second) * rotated * rotated
    direction = (new_moment / (jnp.sqrt(new_variance) + adam_eps)).astype(bf16)
    returned = rotate_back(spread(direction, B, 16).reshape(32, 24, 256), basis)

    half = spread(returned, ("x", "y"), 16)
    halves = sort(half, lax.ppermute(half, "c", SWAP))
    returned = jnp.stack(halves, axis=1).reshape(768, 512)
    unscaled = lax.dot_general(
        panels, returned, (((0,), (0,)), ((), ())), preferred_element_type=f32
    )
    lane = lax.broadcasted_iota(jnp.int32, (1, 128), 1)
    sums = jnp.where(lane == 0, jnp.sum(gradient * gradient), jnp.sum(unscaled * unscaled))
    sums = jnp.sum(lax.all_gather(sums, "c"), axis=0)
    sums = jnp.sum(spread(sums, ("x", "y", "z", "h"), 256), axis=(0, 1))
    update = unscaled * (jnp.sqrt(sums[0]) / (jnp.sqrt(sums[1]) + graft_eps))

    moments = lax.ppermute(jnp.stack([new_moment, new_variance]), ("x", "y", "z", "h"), TURN)
    keep, send = sort(moments[:, 0], moments[:, 1])
    moments = jnp.concatenate(sort(keep, lax.ppermute(send, "c", SWAP)), axis=1)
    return (update, moments[0], moments[1])


def solution(mesh):
    fine = Mesh(mesh.devices.reshape(4, 4, 2, 8, 2), F + B)
    return jax.shard_map(
        body,
        mesh=fine,
        in_specs=(P(F, B), P(B, F), P(B, F), P(B, F), P(B, F)),
        out_specs=(P(F, B), P(B, F), P(B, F)),
        check_vma=False,
    )
```

time: 233 us -> 242 us (1.039)
  Pallas kernels: 0 us -> 15.5 us
  blocking collectives: 77.5 us -> 62.4 us
  between operations: 2.3 us -> 15.6 us
  matrix products: 6.95 us -> 3.84 us
  other arithmetic: 5.36 us -> 7.92 us
    pallas_call x0 -> x2, Pallas kernels: none -> 15.5 us  [the longest x1 7.93 us: rotate_back(): pl.pallas_call(back_kernel, grid=(32 // STEP,), in_specs=[pl.BlockSpec((S...]
    all_to_all x2 -> x1, blocking collectives: 35.7 us -> 20.4 us  [collect(): got = lax.all_to_all(parts, axes, 0, 0, tiled=True)]
    ppermute x5 -> x6, starting transfers between devices: 25.2 us -> 14.4 us  [the longest x1 6.22 us: body(): halves = sort(half, lax.ppermute(half, 'c', SWAP))]
    all_to_all x1, starting transfers between devices: 3.45 us -> 13.4 us  [collect(): got = lax.all_to_all(parts, axes, 0, 0, tiled=True)]
    ppermute x5 -> x6, waiting for transfers between devices: 11.9 us -> 2.2 us  [the longest x1 1.33 us: body(): keep += lax.ppermute(send.astype(bf16), 'c', SWAP).astype(f32)]
    all_to_all x4 -> x3, waiting for transfers between devices: 54 us -> 61.2 us  [spread(): return lax.all_to_all(copies, axes, 0, 0, tiled=True)]
    dot_general x4 -> x1, matrix products: 4.1 us -> 1.01 us  [body(): jnp.dot(panels, grad_b, preferred_element_type=f32).reshape(16, 2, 24, 512)]
    all_gather x2 -> x1, blocking collectives: 7.83 us -> 9.28 us  [body(): lax.all_gather(left_basis, 'h', tiled=True)]
  transfers between devices with their start and end apart: 10 -> 11, of which waited for: 9 -> 6; matrix products, arithmetic and copies ran while one was open for 2% -> 5% of each run, Pallas kernels for 0% -> 0%
where the time goes in v3:
time: 242 us; the launch traced here: 241 us
  waiting for transfers between devices  74.4 us (31%)
  blocking collectives  62.4 us (26%)
  starting transfers between devices  55.6 us (23%)
  between operations  15.6 us (6%)
  Pallas kernels  15.5 us (6%)
  other arithmetic  7.92 us (3%)
  local copies, waits for them, and re-layouts  5.79 us (2%)
  matrix products  3.84 us (2%)
    all_to_all x3, waiting for transfers between devices, spread(): return lax.all_to_all(copies, axes, 0, 0, tiled=True)  61.2 us
    all_to_all x1, blocking collectives, spread(): return lax.all_to_all(copies, axes, 0, 0, tiled=True)  30.8 us
    all_to_all x3, starting transfers between devices, spread(): return lax.all_to_all(copies, axes, 0, 0, tiled=True)  27.8 us
    all_to_all x1, blocking collectives, collect(): got = lax.all_to_all(parts, axes, 0, 0, tiled=True)  20.4 us
    all_to_all x1, starting transfers between devices, collect(): got = lax.all_to_all(parts, axes, 0, 0, tiled=True)  13.4 us
    all_to_all x1, waiting for transfers between devices, collect(): got = lax.all_to_all(parts, axes, 0, 0, tiled=True)  10.4 us
    all_gather x1, blocking collectives, body(): lax.all_gather(left_basis, 'h', tiled=True)  9.28 us
    pallas_call x1, Pallas kernels, rotate_back(): pl.pallas_call(back_kernel, grid=(32 // STEP,), in_specs=[pl.BlockSpec((S...  7.93 us
  transfers between devices with their start and end apart: 11, of which 6 were waited for; matrix products, arithmetic and copies ran while one was open for 5% of the time, Pallas kernels for 0%

profile of v3, /device:TPU:1, one launch (start us, length us, event | category | flops | bytes accessed | tf_op | source)
XLA Modules:
  0.0 241.1 jit_solution(1118353642723436406)
XLA Ops:
  7.9 9.3 %all_gather.13 = bf16[96,896]{1,0:T(8,128)(2,1)S(1)} all-gather(bf16[48,896]{1,0:T(8,128)(2,1)} %param.6), channel_id=1, replica_groups=mesh['x'=4,'y'=4,'c'=2,'z'=8,'h'=2] {'h'}, dimensions={0}, use_global_device_ids=true | all-gather | bytes 258048 | tf_op jit(solution)/shard_map/all_gather | solution.py:107
  18.4 10.0 %all-to-all-start = ((bf16[8,96,896]{2,1,0:T(8,128)(2,1)}), bf16[8,96,896]{2,1,0:T(8,128)(2,1)S(1)}, u32[]{:S(2)}, u32[]{:S(2)}) async-start(bf16[8,96,896]{2,1,0:T(8,128)(2,1)} %broadcast_in_dim.18), calls=%async_computation | async-start | bytes 2752512 | tf_op jit(solution)/shard_map/all_to_all | solution.py:82
  28.4 36.1 %all-to-all-done = bf16[8,96,896]{2,1,0:T(8,128)(2,1)S(1)} async-done(((bf16[8,96,896]{2,1,0:T(8,128)(2,1)}), bf16[8,96,896]{2,1,0:T(8,128)(2,1)S(1)}, u32[]{:S(2)}, u32[]{:S(2)}) %all-to-all-start) | async-done | bytes 1376288 | tf_op jit(solution)/shard_map/all_to_all | solution.py:82
  65.6 2.5 %collective-permute-start.2 = (bf16[16,24,512]{2,1,0:T(8,128)(2,1)S(1)}, bf16[16,24,512]{2,1,0:T(8,128)(2,1)S(1)}, u32[]{:S(2)}, u32[]{:S(2)}) collective-permute-start(bf16[16,24,512]{2,1,0:T(8,128)(2,1)S(1)} %fusion.5), channel_id=1, source_target_pairs={{0,16},{16,0},{1,17},{17,1},{2,18},{18,2},{3,19},{19,3},{4,20},{20... | collective-permute-start | bytes 1179656 | tf_op jit(solution)/shard_map/ppermute | solution.py:110
  68.1 1.3 collective-permute-done.2
  69.7 20.4 %all_to_all.30 = bf16[16,24,512]{2,1,0:T(8,128)(2,1)S(1)} all-to-all(bf16[16,24,512]{2,1,0:T(8,128)(2,1)S(1)} %fusion.4), channel_id=1, replica_groups=mesh['x'=4,'y'=4,'c'=2,'z'=8,'h'=2] {'x','y'}, dimensions={0} | all-to-all | bytes 786432 | tf_op jit(solution)/shard_map/all_to_all | solution.py:86
  90.8 7.6 %shard_map.76 = bf16[32,24,256]{2,1,0:T(8,128)(2,1)} custom-call(bf16[24,512]{1,0:T(8,128)(2,1)} %fusion.18.rows_ref, bf16[32,512,256]{2,1,0:T(8,128)(2,1)} %bitcast.93), custom_call_target="tpu_custom_call" | custom-call | flops 201326592 | bytes 8388608 | tf_op jit(solution)/shard_map/pallas_call | solution.py:29
  98.4 13.4 %all-to-all-start.2 = ((bf16[16,2,24,256]{3,2,1,0:T(8,128)(2,1)}), bf16[16,2,24,256]{3,2,1,0:T(8,128)(2,1)}, u32[]{:S(2)}, u32[]{:S(2)}) async-start(bf16[16,2,24,256]{3,2,1,0:T(8,128)(2,1)} %bitcast.97), calls=%async_computation.2 | async-start | bytes 786432 | tf_op jit(solution)/shard_map/all_to_all | solution.py:86
  111.8 2.4 %collective-permute-start = (f32[2,24,256]{2,1,0:T(8,128)S(1)}, f32[2,24,256]{2,1,0:T(8,128)S(1)}, u32[]{:S(2)}, u32[]{:S(2)}) collective-permute-start(f32[2,24,256]{2,1,0:T(8,128)S(1)} %broadcast_select_fusion.2), channel_id=1, source_target_pairs={{0,16},{16,0},{1,17},{17,1},{2,18},{18,2},{3,19},{19,3},{4,20},{20... | collective-permute-start | bytes 147464 | tf_op jit(solution)/shard_map/ppermute | solution.py:103
  115.8 10.4 %all-to-all-done.2 = bf16[16,2,24,256]{3,2,1,0:T(8,128)(2,1)} async-done(((bf16[16,2,24,256]{3,2,1,0:T(8,128)(2,1)}), bf16[16,2,24,256]{3,2,1,0:T(8,128)(2,1)}, u32[]{:S(2)}, u32[]{:S(2)}) %all-to-all-start.2) | async-done | bytes 393248 | tf_op jit(solution)/shard_map/all_to_all | solution.py:86
  127.3 30.8 %all_to_all.31 = bf16[16,2,24,256]{3,2,1,0:T(8,128)(2,1)} all-to-all(bf16[16,2,24,256]{3,2,1,0:T(8,128)(2,1)S(1)} %broadcast_in_dim.36), channel_id=1, replica_groups=mesh['x'=4,'y'=4,'c'=2,'z'=8,'h'=2] {'z','h'}, dimensions={0} | all-to-all | bytes 786432 | tf_op jit(solution)/shard_map/all_to_all | solution.py:82
  158.0 7.9 %shard_map.77 = bf16[24,512]{1,0:T(8,128)(2,1)} custom-call(bf16[32,24,256]{2,1,0:T(8,128)(2,1)} %bitcast.98, bf16[32,512,256]{2,1,0:T(8,128)(2,1)} %bitcast.94), custom_call_target="tpu_custom_call" | custom-call | flops 201326592 | bytes 8388608 | tf_op jit(solution)/shard_map/pallas_call | solution.py:64
  166.0 1.5 broadcast_in_dim.37
  167.5 7.0 %all-to-all-start.4 = ((bf16[16,24,512]{2,1,0:T(8,128)(2,1)}), bf16[16,24,512]{2,1,0:T(8,128)(2,1)}, u32[]{:S(2)}, u32[]{:S(2)}) async-start(bf16[16,24,512]{2,1,0:T(8,128)(2,1)} %broadcast_in_dim.37), calls=%async_computation.4 | async-start | bytes 786432 | tf_op jit(solution)/shard_map/all_to_all | solution.py:82
  175.2 12.8 %all-to-all-done.4 = bf16[16,24,512]{2,1,0:T(8,128)(2,1)} async-done(((bf16[16,24,512]{2,1,0:T(8,128)(2,1)}), bf16[16,24,512]{2,1,0:T(8,128)(2,1)}, u32[]{:S(2)}, u32[]{:S(2)}) %all-to-all-start.4) | async-done | bytes 393248 | tf_op jit(solution)/shard_map/all_to_all | solution.py:82
  188.0 6.2 %collective-permute-start.3 = (bf16[16,24,512]{2,1,0:T(8,128)(2,1)}, bf16[16,24,512]{2,1,0:T(8,128)(2,1)S(1)}, u32[]{:S(2)}, u32[]{:S(2)}) collective-permute-start(bf16[16,24,512]{2,1,0:T(8,128)(2,1)} %all-to-all-done.4), channel_id=1, source_target_pairs={{0,16},{16,0},{1,17},{17,1},{2,18},{18,2},{3,19},{19,3},{4,20},{20... | collective-permute-start | bytes 1179656 | tf_op jit(solution)/shard_map/ppermute | solution.py:121
  195.3 1.9 collective-permute-start.5
  198.4 2.8 %multiply_reduce_fusion = (f32[]{:T(128)}, f32[512,896]{1,0:T(8,128)}) fusion(bf16[768,512]{1,0:T(8,128)(2,1)S(1)} %bitcast.99, bf16[768,896]{1,0:T(8,128)(2,1)S(1)} %bitcast.96), kind=kOutput, calls=%fused_computation.1 | convolution fusion | flops 705560576 | bytes 3997700 | tf_op jit(solution)/shard_map/dot_general | solution.py:123
  201.2 1.3 compare_select_fusion
  202.5 2.0 all_gather.16
  205.3 10.8 %all-to-all-start.5 = ((f32[256,1,128]{2,1,0:T(1,128)}), f32[256,1,128]{2,1,0:T(1,128)S(1)}, u32[]{:S(2)}, u32[]{:S(2)}) async-start(f32[256,1,128]{2,1,0:T(1,128)} %broadcast_in_dim.40), calls=%async_computation.5 | async-start | bytes 262144 | tf_op jit(solution)/shard_map/all_to_all | solution.py:82
  216.7 12.2 %all-to-all-done.5 = f32[256,1,128]{2,1,0:T(1,128)S(1)} async-done(((f32[256,1,128]{2,1,0:T(1,128)}), f32[256,1,128]{2,1,0:T(1,128)S(1)}, u32[]{:S(2)}, u32[]{:S(2)}) %all-to-all-start.5) | async-done | bytes 131104 | tf_op jit(solution)/shard_map/all_to_all | solution.py:82
  231.0 1.6 multiply_bitcast_fusion
  232.6 1.7 copy.53
  (39 shorter events, 11.5 us)
Async XLA Ops:
  7.2 83.6 %all-gather.3.cloned.1.call-start = ((), (), s32[]{:S(2)}) async-start(), calls=%async_computation.6 | async-start | bytes 8650752 | tf_op jit(solution)/shard_map/all_gather | solution.py:99
  17.2 47.4 %copy-start = (f32[896,512]{1,0:T(8,128)S(1)}, f32[896,512]{1,0:T(8,128)}, u32[]{:S(2)}) copy-start(f32[896,512]{1,0:T(8,128)} %param.5) | copy-start | bytes 5505028
  18.4 46.2 %all-to-all-start = ((bf16[8,96,896]{2,1,0:T(8,128)(2,1)}), bf16[8,96,896]{2,1,0:T(8,128)(2,1)S(1)}, u32[]{:S(2)}, u32[]{:S(2)}) async-start(bf16[8,96,896]{2,1,0:T(8,128)(2,1)} %broadcast_in_dim.18), calls=%async_computation | async-start | bytes 2752512 | tf_op jit(solution)/shard_map/all_to_all | solution.py:82
  65.6 3.8 %collective-permute-start.2 = (bf16[16,24,512]{2,1,0:T(8,128)(2,1)S(1)}, bf16[16,24,512]{2,1,0:T(8,128)(2,1)S(1)}, u32[]{:S(2)}, u32[]{:S(2)}) collective-permute-start(bf16[16,24,512]{2,1,0:T(8,128)(2,1)S(1)} %fusion.5), channel_id=1, source_target_pairs={{0,16},{16,0},{1,17},{17,1},{2,18},{18,2},{3,19},{19,3},{4,20},{20... | collective-permute-start | bytes 1179656 | tf_op jit(solution)/shard_map/ppermute | solution.py:110
  90.8 21.0 %copy-start.1 = (f32[48,256]{1,0:T(8,128)S(1)}, f32[48,256]{1,0:T(8,128)}, u32[]{:S(2)}) copy-start(f32[48,256]{1,0:T(8,128)} %param.9) | copy-start | bytes 147460
  90.8 21.0 %copy-start.2 = (f32[48,256]{1,0:T(8,128)S(1)}, f32[48,256]{1,0:T(8,128)}, u32[]{:S(2)}) copy-start(f32[48,256]{1,0:T(8,128)} %param.8) | copy-start | bytes 147460
  98.4 27.8 %all-to-all-start.2 = ((bf16[16,2,24,256]{3,2,1,0:T(8,128)(2,1)}), bf16[16,2,24,256]{3,2,1,0:T(8,128)(2,1)}, u32[]{:S(2)}, u32[]{:S(2)}) async-start(bf16[16,2,24,256]{3,2,1,0:T(8,128)(2,1)} %bitcast.97), calls=%async_computation.2 | async-start | bytes 786432 | tf_op jit(solution)/shard_map/all_to_all | solution.py:86
  111.8 3.3 %collective-permute-start = (f32[2,24,256]{2,1,0:T(8,128)S(1)}, f32[2,24,256]{2,1,0:T(8,128)S(1)}, u32[]{:S(2)}, u32[]{:S(2)}) collective-permute-start(f32[2,24,256]{2,1,0:T(8,128)S(1)} %broadcast_select_fusion.2), channel_id=1, source_target_pairs={{0,16},{16,0},{1,17},{17,1},{2,18},{18,2},{3,19},{19,3},{4,20},{20... | collective-permute-start | bytes 147464 | tf_op jit(solution)/shard_map/ppermute | solution.py:103
  115.1 0.7 collective-permute-start.1
  167.5 20.6 %all-to-all-start.4 = ((bf16[16,24,512]{2,1,0:T(8,128)(2,1)}), bf16[16,24,512]{2,1,0:T(8,128)(2,1)}, u32[]{:S(2)}, u32[]{:S(2)}) async-start(bf16[16,24,512]{2,1,0:T(8,128)(2,1)} %broadcast_in_dim.37), calls=%async_computation.4 | async-start | bytes 786432 | tf_op jit(solution)/shard_map/all_to_all | solution.py:82
  174.5 20.8 %collective-permute-start.4 = (f32[2,2,24,256]{3,2,1,0:T(8,128)S(1)}, f32[2,2,24,256]{3,2,1,0:T(8,128)S(1)}, u32[]{:S(2)}, u32[]{:S(2)}) collective-permute-start(f32[2,2,24,256]{3,2,1,0:T(8,128)S(1)} %pad_maximum_fusion.2), channel_id=1, source_target_pairs={{0,0},{1,32},{2,64},{3,96},{4,128},{5,160},{6,192},{7,224},{8,256}... | collective-permute-start | bytes 294920 | tf_op jit(solution)/shard_map/ppermute | solution.py:132
  188.0 9.2 %collective-permute-start.3 = (bf16[16,24,512]{2,1,0:T(8,128)(2,1)}, bf16[16,24,512]{2,1,0:T(8,128)(2,1)S(1)}, u32[]{:S(2)}, u32[]{:S(2)}) collective-permute-start(bf16[16,24,512]{2,1,0:T(8,128)(2,1)} %all-to-all-done.4), channel_id=1, source_target_pairs={{0,16},{16,0},{1,17},{17,1},{2,18},{18,2},{3,19},{19,3},{4,20},{20... | collective-permute-start | bytes 1179656 | tf_op jit(solution)/shard_map/ppermute | solution.py:121
  195.3 20.7 %collective-permute-start.5 = (f32[2,24,256]{2,1,0:T(8,128)S(1)}, f32[2,24,256]{2,1,0:T(8,128)S(1)}, u32[]{:S(2)}, u32[]{:S(2)}) collective-permute-start(f32[2,24,256]{2,1,0:T(8,128)S(1)} %select_bitcast_fusion.2), channel_id=1, source_target_pairs={{0,16},{16,0},{1,17},{17,1},{2,18},{18,2},{3,19},{19,3},{4,20},{20... | collective-permute-start | bytes 147464 | tf_op jit(solution)/shard_map/ppermute | solution.py:134
  205.3 23.7 %all-to-all-start.5 = ((f32[256,1,128]{2,1,0:T(1,128)}), f32[256,1,128]{2,1,0:T(1,128)S(1)}, u32[]{:S(2)}, u32[]{:S(2)}) async-start(f32[256,1,128]{2,1,0:T(1,128)} %broadcast_in_dim.40), calls=%async_computation.5 | async-start | bytes 262144 | tf_op jit(solution)/shard_map/all_to_all | solution.py:82
Sparse Core Ops, SparseCore 0:
  10.1 79.9 all-gather.2

commit v4 on v3

v4 whole, which is shorter than its diff:
```python
import jax
import jax.numpy as jnp
from jax import lax
from jax.experimental import pallas as pl
from jax.experimental.pallas import tpu as pltpu
from jax.sharding import Mesh, PartitionSpec as P

beta_first = 0.9
beta_second = 0.95
adam_eps = 1e-08
graft_eps = 1e-06

F = ("x", "y", "c")
B = ("z", "h")
SWAP = [(0, 1), (1, 0)]
TURN = [(16 * i + j, 16 * j + i) for i in range(16) for j in range(16)]
f32 = jnp.float32
bf16 = jnp.bfloat16


def scale_kernel(sums_ref, unscaled_ref, update_ref, factor_ref):
    @pl.when(pl.program_id(0) == 0)
    def _():
        total = jnp.sum(sums_ref[...], axis=0)
        total = jnp.sum(total, axis=1, keepdims=True)
        root = jnp.sqrt(total)
        factor_ref[...] = jnp.broadcast_to(root[0:1] / (root[1:2] + graft_eps), factor_ref.shape)

    update_ref[...] = unscaled_ref[...] * factor_ref[...]


def scale(sums, unscaled):
    rows, columns = unscaled.shape
    return pl.pallas_call(
        scale_kernel,
        grid=(4,),
        in_specs=[
            pl.BlockSpec(sums.shape, lambda i: (0, 0, 0)),
            pl.BlockSpec((rows // 4, columns), lambda i: (i, 0)),
        ],
        out_specs=pl.BlockSpec((rows // 4, columns), lambda i: (i, 0)),
        out_shape=jax.ShapeDtypeStruct(unscaled.shape, f32),
        scratch_shapes=[pltpu.VMEM((1, columns), f32)],
        cost_estimate=pl.CostEstimate(
            flops=rows * columns, bytes_accessed=8 * rows * columns, transcendentals=0
        ),
    )(sums, unscaled)


def lanes(values):
    return jnp.sum(jnp.sum(values * values, axis=0).reshape(-1, 128), axis=0)


def spread(block, axes, count):
    copies = jnp.broadcast_to(block[None], (count,) + block.shape)
    return lax.all_to_all(copies, axes, 0, 0, tiled=True)


def collect(parts, axes):
    got = lax.all_to_all(parts, axes, 0, 0, tiled=True)
    terms = [got[i].astype(f32) for i in range(got.shape[0])]
    while len(terms) > 1:
        terms = [a + b for a, b in zip(terms[::2], terms[1::2])]
    return terms[0]


def body(gradient, left_basis, right_basis, moment, variance):
    first = lax.axis_index("c") == 0

    def sort(mine, theirs):
        return jnp.where(first, mine, theirs), jnp.where(first, theirs, mine)

    basis = lax.all_gather(right_basis, F)

    moments = jnp.stack([moment, variance])
    keep, send = sort(moments[:, :24], moments[:, 24:])
    blocks = sort(keep, lax.ppermute(send, "c", SWAP))
    moments = lax.ppermute(jnp.stack(blocks, axis=1), ("x", "y", "z", "h"), TURN)

    grad_b = gradient.astype(bf16)
    panels = spread(lax.all_gather(left_basis, "h", tiled=True), "z", 8)
    panels, moments, grad_lanes = lax.optimization_barrier((panels, moments, lanes(gradient)))
    panels = panels.reshape(768, 896)
    partial_value = jnp.dot(panels, grad_b, preferred_element_type=f32).reshape(16, 2, 24, 512)
    keep, send = sort(partial_value[:, 0], partial_value[:, 1])
    keep += lax.ppermute(send.astype(bf16), "c", SWAP).astype(f32)
    projected = collect(keep.astype(bf16), ("x", "y")).astype(bf16)

    rotated = jnp.einsum("rk,fkn->frn", projected, basis, preferred_element_type=f32)
    rotated = collect(rotated.astype(bf16).reshape(16, 2, 24, 256), B)
    new_moment = beta_first * moments[0] + (1.0 - beta_first) * rotated
    new_variance = beta_second * moments[1] + (1.0 - beta_second) * rotated * rotated
    direction = (new_moment / (jnp.sqrt(new_variance) + adam_eps)).astype(bf16)
    direction = spread(direction, B, 16).reshape(32, 24, 256)
    returned = lax.dot_general(
        direction, basis, (((0, 2), (0, 2)), ((), ())), preferred_element_type=f32
    )

    half = spread(returned.astype(bf16), ("x", "y"), 16)
    returned = lax.all_gather(half, "c", axis=1, tiled=True).reshape(768, 512)
    unscaled = lax.dot_general(
        panels, returned, (((0,), (0,)), ((), ())), preferred_element_type=f32
    )
    sums = jnp.stack([grad_lanes, lanes(unscaled)])
    sums = jnp.sum(lax.all_gather(sums, "c"), axis=0)
    update = scale(spread(sums, ("x", "y", "z", "h"), 256), unscaled)

    moments = lax.ppermute(jnp.stack([new_moment, new_variance]), ("x", "y", "z", "h"), TURN)
    keep, send = sort(moments[:, 0], moments[:, 1])
    moments = jnp.concatenate(sort(keep, lax.ppermute(send, "c", SWAP)), axis=1)
    return (update, moments[0], moments[1])


def solution(mesh):
    fine = Mesh(mesh.devices.reshape(4, 4, 2, 8, 2), F + B)
    return jax.shard_map(
        body,
        mesh=fine,
        in_specs=(P(F, B), P(B, F), P(B, F), P(B, F), P(B, F)),
        out_specs=(P(F, B), P(B, F), P(B, F)),
        check_vma=False,
    )
```

time: 242 us -> 222 us (0.917)
  blocking collectives: 62.4 us -> 84.3 us
  starting transfers between devices: 55.6 us -> 40.8 us
  waiting for transfers between devices: 74.4 us -> 62.5 us
  Pallas kernels: 15.5 us -> 4.18 us
  other arithmetic: 7.92 us -> 1.35 us
  matrix products: 3.84 us -> 10.2 us
    all_to_all x1 -> x2, blocking collectives: 20.4 us -> 46.5 us  [collect(): got = lax.all_to_all(parts, axes, 0, 0, tiled=True)]
    all_to_all x1 -> x0, starting transfers between devices: 13.4 us -> none  [collect(): got = lax.all_to_all(parts, axes, 0, 0, tiled=True)]
    pallas_call x2 -> x1, Pallas kernels: 15.5 us -> 4.18 us  [scale(): pl.pallas_call(scale_kernel, grid=(4,), in_specs=[pl.BlockSpec(sums.shape...]
    all_to_all x1 -> x0, waiting for transfers between devices: 10.4 us -> none  [collect(): got = lax.all_to_all(parts, axes, 0, 0, tiled=True)]
    all_to_all x1, blocking collectives: 30.8 us -> 21.3 us  [spread(): return lax.all_to_all(copies, axes, 0, 0, tiled=True)]
    dot_general x0 -> x2, matrix products: none -> 7.04 us  [the longest x1 4.74 us: body(): jnp.einsum('rk,fkn->frn', projected, basis, preferred_element_type=f32)]
    all_to_all x3, waiting for transfers between devices: 61.2 us -> 54.4 us  [spread(): return lax.all_to_all(copies, axes, 0, 0, tiled=True)]
    ppermute x1 -> x0, starting transfers between devices: 6.22 us -> none  [body(): halves = sort(half, lax.ppermute(half, 'c', SWAP))]
  transfers between devices with their start and end apart: 11 -> 9, of which waited for: 6 -> 7; matrix products, arithmetic and copies ran while one was open for 5% -> 3% of each run, Pallas kernels for 0% -> 0%
where the time goes in v4:
time: 222 us; the launch traced here: 221 us
  blocking collectives  84.3 us (38%)
  waiting for transfers between devices  62.5 us (28%)
  starting transfers between devices  40.8 us (18%)
  between operations  14.2 us (6%)
  matrix products  10.2 us (5%)
  Pallas kernels  4.18 us (2%)
  local copies, waits for them, and re-layouts  3.5 us (2%)
    all_to_all x3, waiting for transfers between devices, spread(): return lax.all_to_all(copies, axes, 0, 0, tiled=True)  54.4 us
    all_to_all x2, blocking collectives, collect(): got = lax.all_to_all(parts, axes, 0, 0, tiled=True)  46.5 us
    all_to_all x3, starting transfers between devices, spread(): return lax.all_to_all(copies, axes, 0, 0, tiled=True)  29.6 us
    all_to_all x1, blocking collectives, spread(): return lax.all_to_all(copies, axes, 0, 0, tiled=True)  21.3 us
    all_gather x1, blocking collectives, body(): panels = spread(lax.all_gather(left_basis, 'h', tiled=True), 'z', 8)  9.28 us
    all_gather x1, blocking collectives, body(): returned = lax.all_gather(half, 'c', axis=1, tiled=True).reshape(768, 512)  5.35 us
    ppermute x1, starting transfers between devices, body(): blocks = sort(keep, lax.ppermute(send, 'c', SWAP))  4.91 us
    dot_general x1, matrix products, body(): jnp.einsum('rk,fkn->frn', projected, basis, preferred_element_type=f32)  4.74 us
  transfers between devices with their start and end apart: 9, of which 7 were waited for; matrix products, arithmetic and copies ran while one was open for 3% of the time, Pallas kernels for 0%

profile of v4, /device:TPU:1, one launch (start us, length us, event | category | flops | bytes accessed | tf_op | source)
XLA Modules:
  0.0 221.0 jit_solution(7478319255481401936)
XLA Ops:
  7.9 9.3 %all_gather.18 = bf16[96,896]{1,0:T(8,128)(2,1)S(1)} all-gather(bf16[48,896]{1,0:T(8,128)(2,1)} %param.6), channel_id=1, replica_groups=mesh['x'=4,'y'=4,'c'=2,'z'=8,'h'=2] {'h'}, dimensions={0}, use_global_device_ids=true | all-gather | bytes 258048 | tf_op jit(solution)/shard_map/all_gather | solution.py:81
  17.2 1.2 broadcast_in_dim.10
  18.4 10.2 %all-to-all-start = ((bf16[8,96,896]{2,1,0:T(8,128)(2,1)}), bf16[8,96,896]{2,1,0:T(8,128)(2,1)S(1)}, u32[]{:S(2)}, u32[]{:S(2)}) async-start(bf16[8,96,896]{2,1,0:T(8,128)(2,1)} %broadcast_in_dim.10), calls=%async_computation | async-start | bytes 2752512 | tf_op jit(solution)/shard_map/all_to_all | solution.py:56
  28.6 4.9 %collective-permute-start = (f32[2,24,256]{2,1,0:T(8,128)S(1)}, f32[2,24,256]{2,1,0:T(8,128)S(1)}, u32[]{:S(2)}, u32[]{:S(2)}) collective-permute-start(f32[2,24,256]{2,1,0:T(8,128)S(1)} %broadcast_select_fusion.2), channel_id=1, source_target_pairs={{0,16},{16,0},{1,17},{17,1},{2,18},{18,2},{3,19},{19,3},{4,20},{20... | collective-permute-start | bytes 147464 | tf_op jit(solution)/shard_map/ppermute | solution.py:77
  35.1 29.6 %all-to-all-done = bf16[8,96,896]{2,1,0:T(8,128)(2,1)S(1)} async-done(((bf16[8,96,896]{2,1,0:T(8,128)(2,1)}), bf16[8,96,896]{2,1,0:T(8,128)(2,1)S(1)}, u32[]{:S(2)}, u32[]{:S(2)}) %all-to-all-start) | async-done | bytes 1376288 | tf_op jit(solution)/shard_map/all_to_all | solution.py:56
  64.7 1.0 fusion.1
  65.8 2.6 %collective-permute-start.2 = (bf16[16,24,512]{2,1,0:T(8,128)(2,1)S(1)}, bf16[16,24,512]{2,1,0:T(8,128)(2,1)S(1)}, u32[]{:S(2)}, u32[]{:S(2)}) collective-permute-start(bf16[16,24,512]{2,1,0:T(8,128)(2,1)S(1)} %fusion.7), channel_id=1, source_target_pairs={{0,16},{16,0},{1,17},{17,1},{2,18},{18,2},{3,19},{19,3},{4,20},{20... | collective-permute-start | bytes 1179656 | tf_op jit(solution)/shard_map/ppermute | solution.py:86
  68.4 1.3 collective-permute-done.2
  70.0 22.8 %all_to_all.30 = bf16[16,24,512]{2,1,0:T(8,128)(2,1)S(1)} all-to-all(bf16[16,24,512]{2,1,0:T(8,128)(2,1)S(1)} %fusion.6), channel_id=1, replica_groups=mesh['x'=4,'y'=4,'c'=2,'z'=8,'h'=2] {'x','y'}, dimensions={0} | all-to-all | bytes 786432 | tf_op jit(solution)/shard_map/all_to_all | solution.py:60
  92.8 4.5 %all-gather.5.cloned.1.call-done = bf16[16384,256]{1,0:T(8,128)(2,1)} async-done(((bf16[512,256]{1,0:T(8,128)(2,1)}), bf16[16384,256]{1,0:T(8,128)(2,1)}) %all-gather.5.cloned.1.call-update) | async-done | bytes 8388624 | tf_op jit(solution)/shard_map/all_gather | solution.py:73
  97.3 4.7 %convolution_convert_fusion = bf16[24,32,256]{2,0,1:T(8,128)(2,1)S(1)} fusion(bf16[32,512,256]{2,1,0:T(8,128)(2,1)} %bitcast.121, bf16[16,24,512]{2,1,0:T(8,128)(2,1)S(1)} %all_to_all.30), kind=kOutput, calls=%fused_computation.2 | convolution fusion | flops 201916416 | bytes 9175040 | tf_op jit(solution)/shard_map/rk,fkn->frn/dot_general | solution.py:89
  102.1 23.7 %all_to_all.31 = bf16[16,2,24,256]{3,2,1,0:T(8,128)(2,1)S(1)} all-to-all(bf16[16,2,24,256]{3,2,1,0:T(8,128)(2,1)S(1)} %bitcast.124), channel_id=1, replica_groups=mesh['x'=4,'y'=4,'c'=2,'z'=8,'h'=2] {'z','h'}, dimensions={0} | all-to-all | bytes 786432 | tf_op jit(solution)/shard_map/all_to_all | solution.py:60
  125.9 21.3 %all_to_all.32 = bf16[16,2,24,256]{3,2,1,0:T(8,128)(2,1)S(1)} all-to-all(bf16[16,2,24,256]{3,2,1,0:T(8,128)(2,1)S(1)} %broadcast_in_dim.12), channel_id=1, replica_groups=mesh['x'=4,'y'=4,'c'=2,'z'=8,'h'=2] {'z','h'}, dimensions={0} | all-to-all | bytes 786432 | tf_op jit(solution)/shard_map/all_to_all | solution.py:56
  147.2 2.3 %fusion = bf16[24,512]{1,0:T(8,128)(2,1)S(1)} fusion(bf16[32,24,256]{2,1,0:T(8,128)(2,1)S(1)} %bitcast.123, bf16[32,512,256]{2,1,0:T(8,128)(2,1)S(1)} %bitcast.122), kind=kOutput, calls=%fused_computation.4 | convolution fusion | flops 201338880 | bytes 8806400 | tf_op jit(solution)/shard_map/dot_general | solution.py:95
  150.3 10.3 %all-to-all-start.4 = ((bf16[16,24,512]{2,1,0:T(8,128)(2,1)}), bf16[16,24,512]{2,1,0:T(8,128)(2,1)S(1)}, u32[]{:S(2)}, u32[]{:S(2)}) async-start(bf16[16,24,512]{2,1,0:T(8,128)(2,1)} %broadcast_in_dim.13), calls=%async_computation.4 | async-start | bytes 786432 | tf_op jit(solution)/shard_map/all_to_all | solution.py:56
  161.3 13.7 %all-to-all-done.4 = bf16[16,24,512]{2,1,0:T(8,128)(2,1)S(1)} async-done(((bf16[16,24,512]{2,1,0:T(8,128)(2,1)}), bf16[16,24,512]{2,1,0:T(8,128)(2,1)S(1)}, u32[]{:S(2)}, u32[]{:S(2)}) %all-to-all-start.4) | async-done | bytes 393248 | tf_op jit(solution)/shard_map/all_to_all | solution.py:56
  175.0 5.3 %all_gather.21 = bf16[16,48,512]{2,1,0:T(8,128)(2,1)S(1)} all-gather(bf16[16,24,512]{2,1,0:T(8,128)(2,1)S(1)} %all-to-all-done.4), channel_id=1, replica_groups=mesh['x'=4,'y'=4,'c'=2,'z'=8,'h'=2] {'c'}, dimensions={1}, use_global_device_ids=true | all-gather | bytes 1179648 | tf_op jit(solution)/shard_map/all_gather | solution.py:100
  180.4 2.2 multiply_reduce_fusion
  182.6 1.8 all-gather.2
  185.2 9.2 %all-to-all-start.5 = ((f32[256,2,128]{2,1,0:T(2,128)}), f32[256,2,128]{2,1,0:T(2,128)S(1)}, u32[]{:S(2)}, u32[]{:S(2)}) async-start(f32[256,2,128]{2,1,0:T(2,128)} %broadcast_in_dim.14), calls=%async_computation.5 | async-start | bytes 524288 | tf_op jit(solution)/shard_map/all_to_all | solution.py:56
  194.4 2.2 %collective-permute-start.4 = (f32[2,24,256]{2,1,0:T(8,128)S(1)}, f32[2,24,256]{2,1,0:T(8,128)S(1)}, u32[]{:S(2)}, u32[]{:S(2)}) collective-permute-start(f32[2,24,256]{2,1,0:T(8,128)S(1)} %select_bitcast_fusion), channel_id=1, source_target_pairs={{0,16},{16,0},{1,17},{17,1},{2,18},{18,2},{3,19},{19,3},{4,20},{20... | collective-permute-start | bytes 147464 | tf_op jit(solution)/shard_map/ppermute | solution.py:110
  196.6 0.9 collective-permute-done.4
  198.2 11.1 %all-to-all-done.5.sums_ref = f32[256,2,128]{2,1,0:T(2,128)S(1)} async-done(((f32[256,2,128]{2,1,0:T(2,128)}), f32[256,2,128]{2,1,0:T(2,128)S(1)}, u32[]{:S(2)}, u32[]{:S(2)}) %all-to-all-start.5) | async-done | bytes 262176 | tf_op jit(solution)/shard_map/all_to_all | solution.py:56
  210.0 4.2 %shard_map.76 = f32[896,512]{1,0:T(8,128)} custom-call(f32[256,2,128]{2,1,0:T(2,128)} %copy-done.2, f32[896,512]{1,0:T(8,128)} %get-tuple-element.18.unscaled_ref), custom_call_target="tpu_custom_call" | custom-call | flops 458752 | bytes 3670016 | tf_op jit(solution)/shard_map/pallas_call | solution.py:34
  (37 shorter events, 6.4 us)
Async XLA Ops:
  7.2 90.2 %all-gather.5.cloned.1.call-start = ((), (), s32[]{:S(2)}) async-start(), calls=%async_computation.6 | async-start | bytes 8650752 | tf_op jit(solution)/shard_map/all_gather | solution.py:73
  17.2 11.4 %copy-start.3 = (f32[48,256]{1,0:T(8,128)S(1)}, f32[48,256]{1,0:T(8,128)}, u32[]{:S(2)}) copy-start(f32[48,256]{1,0:T(8,128)} %param.9) | copy-start | bytes 147460
  17.2 11.4 %copy-start.4 = (f32[48,256]{1,0:T(8,128)S(1)}, f32[48,256]{1,0:T(8,128)}, u32[]{:S(2)}) copy-start(f32[48,256]{1,0:T(8,128)} %param.8) | copy-start | bytes 147460
  18.4 15.1 %copy-start.1 = (f32[896,512]{1,0:T(8,128)S(1)}, f32[896,512]{1,0:T(8,128)}, u32[]{:S(2)}) copy-start(f32[896,512]{1,0:T(8,128)} %param.5) | copy-start | bytes 5505028
  18.4 46.3 %all-to-all-start = ((bf16[8,96,896]{2,1,0:T(8,128)(2,1)}), bf16[8,96,896]{2,1,0:T(8,128)(2,1)S(1)}, u32[]{:S(2)}, u32[]{:S(2)}) async-start(bf16[8,96,896]{2,1,0:T(8,128)(2,1)} %broadcast_in_dim.10), calls=%async_computation | async-start | bytes 2752512 | tf_op jit(solution)/shard_map/all_to_all | solution.py:56
  28.6 5.8 %collective-permute-start = (f32[2,24,256]{2,1,0:T(8,128)S(1)}, f32[2,24,256]{2,1,0:T(8,128)S(1)}, u32[]{:S(2)}, u32[]{:S(2)}) collective-permute-start(f32[2,24,256]{2,1,0:T(8,128)S(1)} %broadcast_select_fusion.2), channel_id=1, source_target_pairs={{0,16},{16,0},{1,17},{17,1},{2,18},{18,2},{3,19},{19,3},{4,20},{20... | collective-permute-start | bytes 147464 | tf_op jit(solution)/shard_map/ppermute | solution.py:77
  34.4 0.7 collective-permute-start.1
  65.8 4.0 %collective-permute-start.2 = (bf16[16,24,512]{2,1,0:T(8,128)(2,1)S(1)}, bf16[16,24,512]{2,1,0:T(8,128)(2,1)S(1)}, u32[]{:S(2)}, u32[]{:S(2)}) collective-permute-start(bf16[16,24,512]{2,1,0:T(8,128)(2,1)S(1)} %fusion.7), channel_id=1, source_target_pairs={{0,16},{16,0},{1,17},{17,1},{2,18},{18,2},{3,19},{19,3},{4,20},{20... | collective-permute-start | bytes 1179656 | tf_op jit(solution)/shard_map/ppermute | solution.py:86
  97.3 49.9 %copy-start = (bf16[16384,256]{1,0:T(8,128)(2,1)S(1)}, bf16[16384,256]{1,0:T(8,128)(2,1)}, u32[]{:S(2)}) copy-start(bf16[16384,256]{1,0:T(8,128)(2,1)} %all-gather.5.cloned.1.call-done) | copy-start | bytes 25165828
  150.3 24.7 %all-to-all-start.4 = ((bf16[16,24,512]{2,1,0:T(8,128)(2,1)}), bf16[16,24,512]{2,1,0:T(8,128)(2,1)S(1)}, u32[]{:S(2)}, u32[]{:S(2)}) async-start(bf16[16,24,512]{2,1,0:T(8,128)(2,1)} %broadcast_in_dim.13), calls=%async_computation.4 | async-start | bytes 786432 | tf_op jit(solution)/shard_map/all_to_all | solution.py:56
  160.6 33.7 %collective-permute-start.3 = (f32[2,2,24,256]{3,2,1,0:T(8,128)S(1)}, f32[2,2,24,256]{3,2,1,0:T(8,128)S(1)}, u32[]{:S(2)}, u32[]{:S(2)}) collective-permute-start(f32[2,2,24,256]{3,2,1,0:T(8,128)S(1)} %pad_maximum_fusion.1), channel_id=1, source_target_pairs={{0,0},{1,32},{2,64},{3,96},{4,128},{5,160},{6,192},{7,224},{8,256}... | collective-permute-start | bytes 294920 | tf_op jit(solution)/shard_map/ppermute | solution.py:108
  185.2 24.1 %all-to-all-start.5 = ((f32[256,2,128]{2,1,0:T(2,128)}), f32[256,2,128]{2,1,0:T(2,128)S(1)}, u32[]{:S(2)}, u32[]{:S(2)}) async-start(f32[256,2,128]{2,1,0:T(2,128)} %broadcast_in_dim.14), calls=%async_computation.5 | async-start | bytes 524288 | tf_op jit(solution)/shard_map/all_to_all | solution.py:56
  194.4 3.1 %collective-permute-start.4 = (f32[2,24,256]{2,1,0:T(8,128)S(1)}, f32[2,24,256]{2,1,0:T(8,128)S(1)}, u32[]{:S(2)}, u32[]{:S(2)}) collective-permute-start(f32[2,24,256]{2,1,0:T(8,128)S(1)} %select_bitcast_fusion), channel_id=1, source_target_pairs={{0,16},{16,0},{1,17},{17,1},{2,18},{18,2},{3,19},{19,3},{4,20},{20... | collective-permute-start | bytes 147464 | tf_op jit(solution)/shard_map/ppermute | solution.py:110
  209.3 0.7 copy-start.2
Sparse Core Ops, SparseCore 0:
  10.1 87.1 all-gather.4

commit v5 on v4

--- a/solution.py
+++ b/solution.py
@@ -33,12 +33,12 @@
     rows, columns = unscaled.shape
     return pl.pallas_call(
         scale_kernel,
-        grid=(4,),
+        grid=(2,),
         in_specs=[
             pl.BlockSpec(sums.shape, lambda i: (0, 0, 0)),
-            pl.BlockSpec((rows // 4, columns), lambda i: (i, 0)),
+            pl.BlockSpec((rows // 2, columns), lambda i: (i, 0)),
         ],
-        out_specs=pl.BlockSpec((rows // 4, columns), lambda i: (i, 0)),
+        out_specs=pl.BlockSpec((rows // 2, columns), lambda i: (i, 0)),
         out_shape=jax.ShapeDtypeStruct(unscaled.shape, f32),
         scratch_shapes=[pltpu.VMEM((1, columns), f32)],
         cost_estimate=pl.CostEstimate(
@@ -49,6 +49,12 @@
 
 def lanes(values):
     return jnp.sum(jnp.sum(values * values, axis=0).reshape(-1, 128), axis=0)
+
+
+def adam(moment, variance, rotated):
+    new_moment = beta_first * moment + (1.0 - beta_first) * rotated
+    new_variance = beta_second * variance + (1.0 - beta_second) * rotated * rotated
+    return new_moment, new_variance, new_moment / (jnp.sqrt(new_variance) + adam_eps)
 
 
 def spread(block, axes, count):
@@ -75,22 +81,22 @@
     moments = jnp.stack([moment, variance])
     keep, send = sort(moments[:, :24], moments[:, 24:])
     blocks = sort(keep, lax.ppermute(send, "c", SWAP))
-    moments = lax.ppermute(jnp.stack(blocks, axis=1), ("x", "y", "z", "h"), TURN)
+    moments = jnp.stack(blocks, axis=1)
 
     grad_b = gradient.astype(bf16)
     panels = spread(lax.all_gather(left_basis, "h", tiled=True), "z", 8)
     panels, moments, grad_lanes = lax.optimization_barrier((panels, moments, lanes(gradient)))
+    moments = lax.ppermute(moments, ("x", "y", "z", "h"), TURN)
     panels = panels.reshape(768, 896)
     partial_value = jnp.dot(panels, grad_b, preferred_element_type=f32).reshape(16, 2, 24, 512)
     keep, send = sort(partial_value[:, 0], partial_value[:, 1])
     keep += lax.ppermute(send.astype(bf16), "c", SWAP).astype(f32)
     projected = collect(keep.astype(bf16), ("x", "y")).astype(bf16)
+    projected, moments = lax.optimization_barrier((projected, moments))
 
     rotated = jnp.einsum("rk,fkn->frn", projected, basis, preferred_element_type=f32)
     rotated = collect(rotated.astype(bf16).reshape(16, 2, 24, 256), B)
-    new_moment = beta_first * moments[0] + (1.0 - beta_first) * rotated
-    new_variance = beta_second * moments[1] + (1.0 - beta_second) * rotated * rotated
-    direction = (new_moment / (jnp.sqrt(new_variance) + adam_eps)).astype(bf16)
+    direction = (adam(moments[0], moments[1], rotated)[2]).astype(bf16)
     direction = spread(direction, B, 16).reshape(32, 24, 256)
     returned = lax.dot_general(
         direction, basis, (((0, 2), (0, 2)), ((), ())), preferred_element_type=f32
@@ -102,13 +108,14 @@
         panels, returned, (((0,), (0,)), ((), ())), preferred_element_type=f32
     )
     sums = jnp.stack([grad_lanes, lanes(unscaled)])
-    sums = jnp.sum(lax.all_gather(sums, "c"), axis=0)
-    update = scale(spread(sums, ("x", "y", "z", "h"), 256), unscaled)
+    sums = jnp.sum(spread(sums, ("x", "c"), 8), axis=0)
+    update = scale(spread(sums, ("y", "z", "h"), 64), unscaled)
 
-    moments = lax.ppermute(jnp.stack([new_moment, new_variance]), ("x", "y", "z", "h"), TURN)
-    keep, send = sort(moments[:, 0], moments[:, 1])
-    moments = jnp.concatenate(sort(keep, lax.ppermute(send, "c", SWAP)), axis=1)
-    return (update, moments[0], moments[1])
+    rotated = lax.ppermute(rotated, ("x", "y", "z", "h"), TURN)
+    keep, send = sort(rotated[0], rotated[1])
+    rotated = jnp.concatenate(sort(keep, lax.ppermute(send, "c", SWAP)))
+    new_moment, new_variance, _ = adam(moment, variance, rotated)
+    return (update, new_moment, new_variance)
 
 
 def solution(mesh):

time: 222 us -> 222 us (level)
  blocking collectives: 84.3 us -> 61.2 us
  starting transfers between devices: 40.8 us -> 55.9 us
  waiting for transfers between devices: 62.5 us -> 71 us
    all_to_all x2 -> x1, blocking collectives: 46.5 us -> 26.4 us  [collect(): got = lax.all_to_all(parts, axes, 0, 0, tiled=True)]
    all_to_all x0 -> x1, waiting for transfers between devices: none -> 13.1 us  [collect(): got = lax.all_to_all(parts, axes, 0, 0, tiled=True)]
    all_to_all x0 -> x1, starting transfers between devices: none -> 8.79 us  [collect(): got = lax.all_to_all(parts, axes, 0, 0, tiled=True)]
    all_to_all x3 -> x4, starting transfers between devices: 29.6 us -> 35.3 us  [spread(): return lax.all_to_all(copies, axes, 0, 0, tiled=True)]
    all_gather x1, waiting for transfers between devices: 4.54 us -> 0.02 us  [body(): basis = lax.all_gather(right_basis, F)]
    all_to_all x3 -> x4, waiting for transfers between devices: 54.4 us -> 55.2 us  [spread(): return lax.all_to_all(copies, axes, 0, 0, tiled=True)]
  transfers between devices with their start and end apart: 9 -> 11, of which waited for: 7 -> 7; matrix products, arithmetic and copies ran while one was open for 3% -> 3% of each run, Pallas kernels for 0% -> 0%
where the time goes in v5:
time: 222 us; the launch traced here: 221 us
  waiting for transfers between devices  71 us (32%)
  blocking collectives  61.2 us (28%)
  starting transfers between devices  55.9 us (25%)
  between operations  14.2 us (6%)
  matrix products  10.2 us (5%)
  local copies, waits for them, and re-layouts  3.89 us (2%)
  Pallas kernels  2.7 us (1%)
    all_to_all x4, waiting for transfers between devices, spread(): return lax.all_to_all(copies, axes, 0, 0, tiled=True)  55.2 us
    all_to_all x4, starting transfers between devices, spread(): return lax.all_to_all(copies, axes, 0, 0, tiled=True)  35.3 us
    all_to_all x1, blocking collectives, collect(): got = lax.all_to_all(parts, axes, 0, 0, tiled=True)  26.4 us
    all_to_all x1, blocking collectives, spread(): return lax.all_to_all(copies, axes, 0, 0, tiled=True)  21.3 us
    all_to_all x1, waiting for transfers between devices, collect(): got = lax.all_to_all(parts, axes, 0, 0, tiled=True)  13.1 us
    all_gather x1, blocking collectives, body(): panels = spread(lax.all_gather(left_basis, 'h', tiled=True), 'z', 8)  9.28 us
    all_to_all x1, starting transfers between devices, collect(): got = lax.all_to_all(parts, axes, 0, 0, tiled=True)  8.79 us
    ppermute x1, starting transfers between devices, body(): blocks = sort(keep, lax.ppermute(send, 'c', SWAP))  4.91 us
  transfers between devices with their start and end apart: 11, of which 7 were waited for; matrix products, arithmetic and copies ran while one was open for 3% of the time, Pallas kernels for 0%

profile of v5, /device:TPU:1, one launch (start us, length us, event | category | flops | bytes accessed | tf_op | source)
XLA Modules:
  0.0 221.3 jit_solution(16762806487986683376)
XLA Ops:
  7.9 9.3 %all_gather.12 = bf16[96,896]{1,0:T(8,128)(2,1)S(1)} all-gather(bf16[48,896]{1,0:T(8,128)(2,1)} %param.6), channel_id=1, replica_groups=mesh['x'=4,'y'=4,'c'=2,'z'=8,'h'=2] {'h'}, dimensions={0}, use_global_device_ids=true | all-gather | bytes 258048 | tf_op jit(solution)/shard_map/all_gather | solution.py:87
  17.2 1.2 broadcast_in_dim.12
  18.4 10.2 %all-to-all-start = ((bf16[8,96,896]{2,1,0:T(8,128)(2,1)}), bf16[8,96,896]{2,1,0:T(8,128)(2,1)S(1)}, u32[]{:S(2)}, u32[]{:S(2)}) async-start(bf16[8,96,896]{2,1,0:T(8,128)(2,1)} %broadcast_in_dim.12), calls=%async_computation | async-start | bytes 2752512 | tf_op jit(solution)/shard_map/all_to_all | solution.py:62
  28.6 4.9 %collective-permute-start = (f32[2,24,256]{2,1,0:T(8,128)S(1)}, f32[2,24,256]{2,1,0:T(8,128)S(1)}, u32[]{:S(2)}, u32[]{:S(2)}) collective-permute-start(f32[2,24,256]{2,1,0:T(8,128)S(1)} %broadcast_select_fusion), channel_id=1, source_target_pairs={{0,16},{16,0},{1,17},{17,1},{2,18},{18,2},{3,19},{19,3},{4,20},{20... | collective-permute-start | bytes 147464 | tf_op jit(solution)/shard_map/ppermute | solution.py:83
  34.4 30.3 %all-to-all-done = bf16[8,96,896]{2,1,0:T(8,128)(2,1)S(1)} async-done(((bf16[8,96,896]{2,1,0:T(8,128)(2,1)}), bf16[8,96,896]{2,1,0:T(8,128)(2,1)S(1)}, u32[]{:S(2)}, u32[]{:S(2)}) %all-to-all-start) | async-done | bytes 1376288 | tf_op jit(solution)/shard_map/all_to_all | solution.py:62
  64.7 1.0 fusion.1
  65.8 2.5 %collective-permute-start.1 = (bf16[16,24,512]{2,1,0:T(8,128)(2,1)S(1)}, bf16[16,24,512]{2,1,0:T(8,128)(2,1)S(1)}, u32[]{:S(2)}, u32[]{:S(2)}) collective-permute-start(bf16[16,24,512]{2,1,0:T(8,128)(2,1)S(1)} %fusion.7), channel_id=1, source_target_pairs={{0,16},{16,0},{1,17},{17,1},{2,18},{18,2},{3,19},{19,3},{4,20},{20... | collective-permute-start | bytes 1179656 | tf_op jit(solution)/shard_map/ppermute | solution.py:93
  68.3 1.3 collective-permute-done.1
  70.5 8.8 %all-to-all-start.1 = ((bf16[16,24,512]{2,1,0:T(8,128)(2,1)}), bf16[16,24,512]{2,1,0:T(8,128)(2,1)S(1)}, u32[]{:S(2)}, u32[]{:S(2)}) async-start(bf16[16,24,512]{2,1,0:T(8,128)(2,1)} %fusion.6), calls=%async_computation.1 | async-start | bytes 786432 | tf_op jit(solution)/shard_map/all_to_all | solution.py:66
  80.0 13.1 %all-to-all-done.1 = bf16[16,24,512]{2,1,0:T(8,128)(2,1)S(1)} async-done(((bf16[16,24,512]{2,1,0:T(8,128)(2,1)}), bf16[16,24,512]{2,1,0:T(8,128)(2,1)S(1)}, u32[]{:S(2)}, u32[]{:S(2)}) %all-to-all-start.1) | async-done | bytes 393248 | tf_op jit(solution)/shard_map/all_to_all | solution.py:66
  93.2 4.7 %convolution_convert_fusion = bf16[24,32,256]{2,0,1:T(8,128)(2,1)S(1)} fusion(bf16[32,512,256]{2,1,0:T(8,128)(2,1)} %bitcast.74, bf16[24,512]{1,0:T(8,128)(2,1)S(1)} %fusion.17), kind=kOutput, calls=%fused_computation.2 | convolution fusion | flops 201523200 | bytes 8806400 | tf_op jit(solution)/shard_map/rk,fkn->frn/dot_general | solution.py:97
  97.9 26.4 %all_to_all.35 = bf16[16,2,24,256]{3,2,1,0:T(8,128)(2,1)S(1)} all-to-all(bf16[16,2,24,256]{3,2,1,0:T(8,128)(2,1)S(1)} %bitcast.77), channel_id=1, replica_groups=mesh['x'=4,'y'=4,'c'=2,'z'=8,'h'=2] {'z','h'}, dimensions={0} | all-to-all | bytes 786432 | tf_op jit(solution)/shard_map/all_to_all | solution.py:66
  124.4 21.3 %all_to_all.36 = bf16[16,2,24,256]{3,2,1,0:T(8,128)(2,1)S(1)} all-to-all(bf16[16,2,24,256]{3,2,1,0:T(8,128)(2,1)S(1)} %broadcast_in_dim.14), channel_id=1, replica_groups=mesh['x'=4,'y'=4,'c'=2,'z'=8,'h'=2] {'z','h'}, dimensions={0} | all-to-all | bytes 786432 | tf_op jit(solution)/shard_map/all_to_all | solution.py:62
  145.7 2.3 %fusion = bf16[24,512]{1,0:T(8,128)(2,1)S(1)} fusion(bf16[32,24,256]{2,1,0:T(8,128)(2,1)S(1)} %bitcast.76, bf16[32,512,256]{2,1,0:T(8,128)(2,1)S(1)} %bitcast.75), kind=kOutput, calls=%fused_computation.4 | convolution fusion | flops 201338880 | bytes 8806400 | tf_op jit(solution)/shard_map/dot_general | solution.py:101
  148.8 9.2 %all-to-all-start.4 = ((bf16[16,24,512]{2,1,0:T(8,128)(2,1)}), bf16[16,24,512]{2,1,0:T(8,128)(2,1)S(1)}, u32[]{:S(2)}, u32[]{:S(2)}) async-start(bf16[16,24,512]{2,1,0:T(8,128)(2,1)} %broadcast_in_dim.15), calls=%async_computation.4 | async-start | bytes 786432 | tf_op jit(solution)/shard_map/all_to_all | solution.py:62
  158.7 3.1 %collective-permute-start.4 = (f32[24,256]{1,0:T(8,128)S(1)}, f32[24,256]{1,0:T(8,128)S(1)}, u32[]{:S(2)}, u32[]{:S(2)}) collective-permute-start(f32[24,256]{1,0:T(8,128)S(1)} %select_bitcast_fusion.2), channel_id=1, source_target_pairs={{0,16},{16,0},{1,17},{17,1},{2,18},{18,2},{3,19},{19,3},{4,20},{20... | collective-permute-start | bytes 73736 | tf_op jit(solution)/shard_map/ppermute | solution.py:116
  161.8 10.1 %all-to-all-done.4 = bf16[16,24,512]{2,1,0:T(8,128)(2,1)S(1)} async-done(((bf16[16,24,512]{2,1,0:T(8,128)(2,1)}), bf16[16,24,512]{2,1,0:T(8,128)(2,1)S(1)}, u32[]{:S(2)}, u32[]{:S(2)}) %all-to-all-start.4) | async-done | bytes 393248 | tf_op jit(solution)/shard_map/all_to_all | solution.py:62
  171.9 4.3 %all_gather.15 = bf16[16,48,512]{2,1,0:T(8,128)(2,1)S(1)} all-gather(bf16[16,24,512]{2,1,0:T(8,128)(2,1)S(1)} %all-to-all-done.4), channel_id=1, replica_groups=mesh['x'=4,'y'=4,'c'=2,'z'=8,'h'=2] {'c'}, dimensions={1}, use_global_device_ids=true | all-gather | bytes 1179648 | tf_op jit(solution)/shard_map/all_gather | solution.py:106
  176.2 2.2 multiply_reduce_fusion
  179.0 4.8 %all-to-all-start.5 = ((f32[8,2,128]{2,1,0:T(2,128)}), f32[8,2,128]{2,1,0:T(2,128)S(1)}, u32[]{:S(2)}, u32[]{:S(2)}) async-start(f32[8,2,128]{2,1,0:T(2,128)} %broadcast_in_dim.16), calls=%async_computation.5 | async-start | bytes 16384 | tf_op jit(solution)/shard_map/all_to_all | solution.py:62
  183.8 4.6 %all-to-all-done.5 = f32[8,2,128]{2,1,0:T(2,128)S(1)} async-done(((f32[8,2,128]{2,1,0:T(2,128)}), f32[8,2,128]{2,1,0:T(2,128)S(1)}, u32[]{:S(2)}, u32[]{:S(2)}) %all-to-all-start.5) | async-done | bytes 8224 | tf_op jit(solution)/shard_map/all_to_all | solution.py:62
  189.0 11.2 %all-to-all-start.6 = ((f32[64,2,128]{2,1,0:T(2,128)}), f32[64,2,128]{2,1,0:T(2,128)S(1)}, u32[]{:S(2)}, u32[]{:S(2)}) async-start(f32[64,2,128]{2,1,0:T(2,128)} %broadcast_in_dim.17), calls=%async_computation.6 | async-start | bytes 131072 | tf_op jit(solution)/shard_map/all_to_all | solution.py:62
  200.9 10.2 %all-to-all-done.6.sums_ref = f32[64,2,128]{2,1,0:T(2,128)S(1)} async-done(((f32[64,2,128]{2,1,0:T(2,128)}), f32[64,2,128]{2,1,0:T(2,128)S(1)}, u32[]{:S(2)}, u32[]{:S(2)}) %all-to-all-start.6) | async-done | bytes 65568 | tf_op jit(solution)/shard_map/all_to_all | solution.py:62
  211.7 2.7 %shard_map.76 = f32[896,512]{1,0:T(8,128)} custom-call(f32[64,2,128]{2,1,0:T(2,128)} %copy-done.4, f32[896,512]{1,0:T(8,128)} %get-tuple-element.22.unscaled_ref), custom_call_target="tpu_custom_call" | custom-call | flops 458752 | bytes 3670016 | tf_op jit(solution)/shard_map/pallas_call | solution.py:34
  (38 shorter events, 7.6 us)
Async XLA Ops:
  7.2 86.0 %all-gather.3.cloned.1.call-start = ((), (), s32[]{:S(2)}) async-start(), calls=%async_computation.7 | async-start | bytes 8650752 | tf_op jit(solution)/shard_map/all_gather | solution.py:79
  17.2 11.4 %copy-start.2 = (f32[48,256]{1,0:T(8,128)S(1)}, f32[48,256]{1,0:T(8,128)}, u32[]{:S(2)}) copy-start(f32[48,256]{1,0:T(8,128)} %param.9) | copy-start | bytes 147460
  17.2 11.4 %copy-start.3 = (f32[48,256]{1,0:T(8,128)S(1)}, f32[48,256]{1,0:T(8,128)}, u32[]{:S(2)}) copy-start(f32[48,256]{1,0:T(8,128)} %param.8) | copy-start | bytes 147460
  18.4 15.1 %copy-start.1 = (f32[896,512]{1,0:T(8,128)S(1)}, f32[896,512]{1,0:T(8,128)}, u32[]{:S(2)}) copy-start(f32[896,512]{1,0:T(8,128)} %param.5) | copy-start | bytes 5505028
  18.4 46.3 %all-to-all-start = ((bf16[8,96,896]{2,1,0:T(8,128)(2,1)}), bf16[8,96,896]{2,1,0:T(8,128)(2,1)S(1)}, u32[]{:S(2)}, u32[]{:S(2)}) async-start(bf16[8,96,896]{2,1,0:T(8,128)(2,1)} %broadcast_in_dim.12), calls=%async_computation | async-start | bytes 2752512 | tf_op jit(solution)/shard_map/all_to_all | solution.py:62
  28.6 5.8 %collective-permute-start = (f32[2,24,256]{2,1,0:T(8,128)S(1)}, f32[2,24,256]{2,1,0:T(8,128)S(1)}, u32[]{:S(2)}, u32[]{:S(2)}) collective-permute-start(f32[2,24,256]{2,1,0:T(8,128)S(1)} %broadcast_select_fusion), channel_id=1, source_target_pairs={{0,16},{16,0},{1,17},{17,1},{2,18},{18,2},{3,19},{19,3},{4,20},{20... | collective-permute-start | bytes 147464 | tf_op jit(solution)/shard_map/ppermute | solution.py:83
  65.8 3.8 %collective-permute-start.1 = (bf16[16,24,512]{2,1,0:T(8,128)(2,1)S(1)}, bf16[16,24,512]{2,1,0:T(8,128)(2,1)S(1)}, u32[]{:S(2)}, u32[]{:S(2)}) collective-permute-start(bf16[16,24,512]{2,1,0:T(8,128)(2,1)S(1)} %fusion.7), channel_id=1, source_target_pairs={{0,16},{16,0},{1,17},{17,1},{2,18},{18,2},{3,19},{19,3},{4,20},{20... | collective-permute-start | bytes 1179656 | tf_op jit(solution)/shard_map/ppermute | solution.py:93
  70.5 22.5 %all-to-all-start.1 = ((bf16[16,24,512]{2,1,0:T(8,128)(2,1)}), bf16[16,24,512]{2,1,0:T(8,128)(2,1)S(1)}, u32[]{:S(2)}, u32[]{:S(2)}) async-start(bf16[16,24,512]{2,1,0:T(8,128)(2,1)} %fusion.6), calls=%async_computation.1 | async-start | bytes 786432 | tf_op jit(solution)/shard_map/all_to_all | solution.py:66
  79.3 13.8 %collective-permute-start.2 = (f32[2,2,24,256]{3,2,1,0:T(8,128)S(1)}, f32[2,2,24,256]{3,2,1,0:T(8,128)S(1)}, u32[]{:S(2)}, u32[]{:S(2)}) collective-permute-start(f32[2,2,24,256]{3,2,1,0:T(8,128)S(1)} %pad_maximum_fusion), channel_id=1, source_target_pairs={{0,0},{1,32},{2,64},{3,96},{4,128},{5,160},{6,192},{7,224},{8,256}... | collective-permute-start | bytes 294920 | tf_op jit(solution)/shard_map/ppermute | solution.py:89
  93.2 52.5 %copy-start = (bf16[16384,256]{1,0:T(8,128)(2,1)S(1)}, bf16[16384,256]{1,0:T(8,128)(2,1)}, u32[]{:S(2)}) copy-start(bf16[16384,256]{1,0:T(8,128)(2,1)} %all-gather.3.cloned.1.call-done) | copy-start | bytes 25165828
  148.8 23.1 %all-to-all-start.4 = ((bf16[16,24,512]{2,1,0:T(8,128)(2,1)}), bf16[16,24,512]{2,1,0:T(8,128)(2,1)S(1)}, u32[]{:S(2)}, u32[]{:S(2)}) async-start(bf16[16,24,512]{2,1,0:T(8,128)(2,1)} %broadcast_in_dim.15), calls=%async_computation.4 | async-start | bytes 786432 | tf_op jit(solution)/shard_map/all_to_all | solution.py:62
  158.0 0.7 collective-permute-start.3
  158.7 25.1 %collective-permute-start.4 = (f32[24,256]{1,0:T(8,128)S(1)}, f32[24,256]{1,0:T(8,128)S(1)}, u32[]{:S(2)}, u32[]{:S(2)}) collective-permute-start(f32[24,256]{1,0:T(8,128)S(1)} %select_bitcast_fusion.2), channel_id=1, source_target_pairs={{0,16},{16,0},{1,17},{17,1},{2,18},{18,2},{3,19},{19,3},{4,20},{20... | collective-permute-start | bytes 73736 | tf_op jit(solution)/shard_map/ppermute | solution.py:116
  179.0 9.4 %all-to-all-start.5 = ((f32[8,2,128]{2,1,0:T(2,128)}), f32[8,2,128]{2,1,0:T(2,128)S(1)}, u32[]{:S(2)}, u32[]{:S(2)}) async-start(f32[8,2,128]{2,1,0:T(2,128)} %broadcast_in_dim.16), calls=%async_computation.5 | async-start | bytes 16384 | tf_op jit(solution)/shard_map/all_to_all | solution.py:62
  189.0 22.1 %all-to-all-start.6 = ((f32[64,2,128]{2,1,0:T(2,128)}), f32[64,2,128]{2,1,0:T(2,128)S(1)}, u32[]{:S(2)}, u32[]{:S(2)}) async-start(f32[64,2,128]{2,1,0:T(2,128)} %broadcast_in_dim.17), calls=%async_computation.6 | async-start | bytes 131072 | tf_op jit(solution)/shard_map/all_to_all | solution.py:62
  211.1 0.6 copy-start.4
Sparse Core Ops, SparseCore 0:
  10.1 79.8 all-gather.2

commit v6 on v5

--- a/solution.py
+++ b/solution.py
@@ -98,11 +98,17 @@
     rotated = collect(rotated.astype(bf16).reshape(16, 2, 24, 256), B)
     direction = (adam(moments[0], moments[1], rotated)[2]).astype(bf16)
     direction = spread(direction, B, 16).reshape(32, 24, 256)
+    rotated = lax.ppermute(rotated, ("x", "y", "z", "h"), TURN)
+    direction, rotated = lax.optimization_barrier((direction, rotated))
     returned = lax.dot_general(
         direction, basis, (((0, 2), (0, 2)), ((), ())), preferred_element_type=f32
     )
 
     half = spread(returned.astype(bf16), ("x", "y"), 16)
+    keep, send = sort(rotated[0], rotated[1])
+    rotated = jnp.concatenate(sort(keep, lax.ppermute(send, "c", SWAP)))
+    new_moment, new_variance, _ = adam(moment, variance, rotated)
+    half, new_moment, new_variance = lax.optimization_barrier((half, new_moment, new_variance))
     returned = lax.all_gather(half, "c", axis=1, tiled=True).reshape(768, 512)
     unscaled = lax.dot_general(
         panels, returned, (((0,), (0,)), ((), ())), preferred_element_type=f32
@@ -110,11 +116,6 @@
     sums = jnp.stack([grad_lanes, lanes(unscaled)])
     sums = jnp.sum(spread(sums, ("x", "c"), 8), axis=0)
     update = scale(spread(sums, ("y", "z", "h"), 64), unscaled)
-
-    rotated = lax.ppermute(rotated, ("x", "y", "z", "h"), TURN)
-    keep, send = sort(rotated[0], rotated[1])
-    rotated = jnp.concatenate(sort(keep, lax.ppermute(send, "c", SWAP)))
-    new_moment, new_variance, _ = adam(moment, variance, rotated)
     return (update, new_moment, new_variance)
 
 

time: 222 us -> 218 us (0.982)
  starting transfers between devices: 55.9 us -> 49.2 us
  blocking collectives: 61.2 us -> 64.4 us
  matrix products: 10.2 us -> 13.4 us
  waiting for transfers between devices: 71 us -> 68.4 us
    all_to_all x4 -> x3, starting transfers between devices: 35.3 us -> 28.7 us  [spread(): return lax.all_to_all(copies, axes, 0, 0, tiled=True)]
    all_to_all x1 -> x2, blocking collectives: 21.3 us -> 25.2 us  [spread(): return lax.all_to_all(copies, axes, 0, 0, tiled=True)]
    all_to_all x4 -> x3, waiting for transfers between devices: 55.2 us -> 51.9 us  [spread(): return lax.all_to_all(copies, axes, 0, 0, tiled=True)]
    dot_general x1, matrix products: 2.3 us -> 5.68 us  [body(): lax.dot_general(direction, basis, (((0, 2), (0, 2)), ((), ())), preferred...]
  transfers between devices with their start and end apart: 11 -> 10, of which waited for: 7 -> 7; matrix products, arithmetic and copies ran while one was open for 3% -> 2% of each run, Pallas kernels for 0% -> 0%
where the time goes in v6:
time: 218 us; the launch traced here: 217 us
  waiting for transfers between devices  68.4 us (31%)
  blocking collectives  64.4 us (30%)
  starting transfers between devices  49.2 us (23%)
  between operations  14.2 us (7%)
  matrix products  13.4 us (6%)
  local copies, waits for them, and re-layouts  2.79 us (1%)
  Pallas kernels  2.7 us (1%)
    all_to_all x3, waiting for transfers between devices, spread(): return lax.all_to_all(copies, axes, 0, 0, tiled=True)  51.9 us
    all_to_all x3, starting transfers between devices, spread(): return lax.all_to_all(copies, axes, 0, 0, tiled=True)  28.7 us
    all_to_all x1, blocking collectives, collect(): got = lax.all_to_all(parts, axes, 0, 0, tiled=True)  26.3 us
    all_to_all x2, blocking collectives, spread(): return lax.all_to_all(copies, axes, 0, 0, tiled=True)  25.2 us
    all_to_all x1, waiting for transfers between devices, collect(): got = lax.all_to_all(parts, axes, 0, 0, tiled=True)  13.1 us
    all_gather x1, blocking collectives, body(): panels = spread(lax.all_gather(left_basis, 'h', tiled=True), 'z', 8)  9.28 us
    all_to_all x1, starting transfers between devices, collect(): got = lax.all_to_all(parts, axes, 0, 0, tiled=True)  8.79 us
    dot_general x1, matrix products, body(): lax.dot_general(direction, basis, (((0, 2), (0, 2)), ((), ())), preferred...  5.68 us
  transfers between devices with their start and end apart: 10, of which 7 were waited for; matrix products, arithmetic and copies ran while one was open for 2% of the time, Pallas kernels for 0%

profile of v6, /device:TPU:1, one launch (start us, length us, event | category | flops | bytes accessed | tf_op | source)
XLA Modules:
  0.0 217.3 jit_solution(633425152235270388)
XLA Ops:
  7.9 9.3 %all_gather.12 = bf16[96,896]{1,0:T(8,128)(2,1)S(1)} all-gather(bf16[48,896]{1,0:T(8,128)(2,1)} %param.6), channel_id=1, replica_groups=mesh['x'=4,'y'=4,'c'=2,'z'=8,'h'=2] {'h'}, dimensions={0}, use_global_device_ids=true | all-gather | bytes 258048 | tf_op jit(solution)/shard_map/all_gather | solution.py:87
  17.2 1.2 broadcast_in_dim.12
  18.4 10.2 %all-to-all-start = ((bf16[8,96,896]{2,1,0:T(8,128)(2,1)}), bf16[8,96,896]{2,1,0:T(8,128)(2,1)S(1)}, u32[]{:S(2)}, u32[]{:S(2)}) async-start(bf16[8,96,896]{2,1,0:T(8,128)(2,1)} %broadcast_in_dim.12), calls=%async_computation | async-start | bytes 2752512 | tf_op jit(solution)/shard_map/all_to_all | solution.py:62
  28.6 4.9 %collective-permute-start = (f32[2,24,256]{2,1,0:T(8,128)S(1)}, f32[2,24,256]{2,1,0:T(8,128)S(1)}, u32[]{:S(2)}, u32[]{:S(2)}) collective-permute-start(f32[2,24,256]{2,1,0:T(8,128)S(1)} %broadcast_select_fusion), channel_id=1, source_target_pairs={{0,16},{16,0},{1,17},{17,1},{2,18},{18,2},{3,19},{19,3},{4,20},{20... | collective-permute-start | bytes 147464 | tf_op jit(solution)/shard_map/ppermute | solution.py:83
  34.4 30.3 %all-to-all-done = bf16[8,96,896]{2,1,0:T(8,128)(2,1)S(1)} async-done(((bf16[8,96,896]{2,1,0:T(8,128)(2,1)}), bf16[8,96,896]{2,1,0:T(8,128)(2,1)S(1)}, u32[]{:S(2)}, u32[]{:S(2)}) %all-to-all-start) | async-done | bytes 1376288 | tf_op jit(solution)/shard_map/all_to_all | solution.py:62
  64.7 1.0 fusion.1
  65.8 2.5 %collective-permute-start.1 = (bf16[16,24,512]{2,1,0:T(8,128)(2,1)S(1)}, bf16[16,24,512]{2,1,0:T(8,128)(2,1)S(1)}, u32[]{:S(2)}, u32[]{:S(2)}) collective-permute-start(bf16[16,24,512]{2,1,0:T(8,128)(2,1)S(1)} %fusion.7), channel_id=1, source_target_pairs={{0,16},{16,0},{1,17},{17,1},{2,18},{18,2},{3,19},{19,3},{4,20},{20... | collective-permute-start | bytes 1179656 | tf_op jit(solution)/shard_map/ppermute | solution.py:93
  68.3 1.3 collective-permute-done.1
  69.6 1.0 fusion.6
  70.5 8.8 %all-to-all-start.1 = ((bf16[16,24,512]{2,1,0:T(8,128)(2,1)}), bf16[16,24,512]{2,1,0:T(8,128)(2,1)S(1)}, u32[]{:S(2)}, u32[]{:S(2)}) async-start(bf16[16,24,512]{2,1,0:T(8,128)(2,1)} %fusion.6), calls=%async_computation.1 | async-start | bytes 786432 | tf_op jit(solution)/shard_map/all_to_all | solution.py:66
  80.0 13.1 %all-to-all-done.1 = bf16[16,24,512]{2,1,0:T(8,128)(2,1)S(1)} async-done(((bf16[16,24,512]{2,1,0:T(8,128)(2,1)}), bf16[16,24,512]{2,1,0:T(8,128)(2,1)S(1)}, u32[]{:S(2)}, u32[]{:S(2)}) %all-to-all-start.1) | async-done | bytes 393248 | tf_op jit(solution)/shard_map/all_to_all | solution.py:66
  93.2 4.6 %convolution_convert_fusion = bf16[24,32,256]{2,0,1:T(8,128)(2,1)S(1)} fusion(bf16[32,512,256]{2,1,0:T(8,128)(2,1)} %bitcast.74, bf16[24,512]{1,0:T(8,128)(2,1)S(1)} %fusion.17), kind=kOutput, calls=%fused_computation.2 | convolution fusion | flops 201523200 | bytes 8806400 | tf_op jit(solution)/shard_map/rk,fkn->frn/dot_general | solution.py:97
  97.7 26.3 %all_to_all.35 = bf16[16,2,24,256]{3,2,1,0:T(8,128)(2,1)S(1)} all-to-all(bf16[16,2,24,256]{3,2,1,0:T(8,128)(2,1)S(1)} %bitcast.77), channel_id=1, replica_groups=mesh['x'=4,'y'=4,'c'=2,'z'=8,'h'=2] {'z','h'}, dimensions={0} | all-to-all | bytes 786432 | tf_op jit(solution)/shard_map/all_to_all | solution.py:66
  124.9 8.1 %all-to-all-start.3 = ((bf16[16,2,24,256]{3,2,1,0:T(8,128)(2,1)}), bf16[16,2,24,256]{3,2,1,0:T(8,128)(2,1)S(1)}, u32[]{:S(2)}, u32[]{:S(2)}) async-start(bf16[16,2,24,256]{3,2,1,0:T(8,128)(2,1)} %broadcast_in_dim.14), calls=%async_computation.3 | async-start | bytes 786432 | tf_op jit(solution)/shard_map/all_to_all | solution.py:62
  133.7 13.1 %all-to-all-done.3 = bf16[16,2,24,256]{3,2,1,0:T(8,128)(2,1)S(1)} async-done(((bf16[16,2,24,256]{3,2,1,0:T(8,128)(2,1)}), bf16[16,2,24,256]{3,2,1,0:T(8,128)(2,1)S(1)}, u32[]{:S(2)}, u32[]{:S(2)}) %all-to-all-start.3) | async-done | bytes 393248 | tf_op jit(solution)/shard_map/all_to_all | solution.py:62
  146.8 5.7 %fusion = bf16[24,512]{1,0:T(8,128)(2,1)S(1)} fusion(bf16[32,24,256]{2,1,0:T(8,128)(2,1)S(1)} %bitcast.76, bf16[32,512,256]{2,1,0:T(8,128)(2,1)} %bitcast.75), kind=kOutput, calls=%fused_computation.4 | convolution fusion | flops 201338880 | bytes 8806400 | tf_op jit(solution)/shard_map/dot_general | solution.py:103
  153.3 10.4 %all-to-all-start.4 = ((bf16[16,24,512]{2,1,0:T(8,128)(2,1)}), bf16[16,24,512]{2,1,0:T(8,128)(2,1)S(1)}, u32[]{:S(2)}, u32[]{:S(2)}) async-start(bf16[16,24,512]{2,1,0:T(8,128)(2,1)} %broadcast_in_dim.15), calls=%async_computation.4 | async-start | bytes 786432 | tf_op jit(solution)/shard_map/all_to_all | solution.py:62
  163.7 3.0 %collective-permute-start.4 = (f32[24,256]{1,0:T(8,128)S(1)}, f32[24,256]{1,0:T(8,128)S(1)}, u32[]{:S(2)}, u32[]{:S(2)}) collective-permute-start(f32[24,256]{1,0:T(8,128)S(1)} %select_bitcast_fusion.2), channel_id=1, source_target_pairs={{0,16},{16,0},{1,17},{17,1},{2,18},{18,2},{3,19},{19,3},{4,20},{20... | collective-permute-start | bytes 73736 | tf_op jit(solution)/shard_map/ppermute | solution.py:109
  168.2 8.4 %all-to-all-done.4 = bf16[16,24,512]{2,1,0:T(8,128)(2,1)S(1)} async-done(((bf16[16,24,512]{2,1,0:T(8,128)(2,1)}), bf16[16,24,512]{2,1,0:T(8,128)(2,1)S(1)}, u32[]{:S(2)}, u32[]{:S(2)}) %all-to-all-start.4) | async-done | bytes 393248 | tf_op jit(solution)/shard_map/all_to_all | solution.py:62
  176.6 3.7 %all_gather.15 = bf16[16,48,512]{2,1,0:T(8,128)(2,1)S(1)} all-gather(bf16[16,24,512]{2,1,0:T(8,128)(2,1)S(1)} %all-to-all-done.4), channel_id=1, replica_groups=mesh['x'=4,'y'=4,'c'=2,'z'=8,'h'=2] {'c'}, dimensions={1}, use_global_device_ids=true | all-gather | bytes 1179648 | tf_op jit(solution)/shard_map/all_gather | solution.py:112
  180.3 2.2 multiply_reduce_fusion
  182.5 7.3 %all_to_all.36 = f32[8,2,128]{2,1,0:T(2,128)S(1)} all-to-all(f32[8,2,128]{2,1,0:T(2,128)S(1)} %broadcast_in_dim.16), channel_id=1, replica_groups=mesh['x'=4,'y'=4,'c'=2,'z'=8,'h'=2] {'x','c'}, dimensions={0} | all-to-all | bytes 16384 | tf_op jit(solution)/shard_map/all_to_all | solution.py:62
  189.9 17.8 %all_to_all.37.sums_ref = f32[64,2,128]{2,1,0:T(2,128)} all-to-all(f32[64,2,128]{2,1,0:T(2,128)S(1)} %broadcast_in_dim.17), channel_id=1, replica_groups=mesh['x'=4,'y'=4,'c'=2,'z'=8,'h'=2] {'y','z','h'}, dimensions={0} | all-to-all | bytes 131072 | tf_op jit(solution)/shard_map/all_to_all | solution.py:62
  207.7 2.7 %shard_map.76 = f32[896,512]{1,0:T(8,128)} custom-call(f32[64,2,128]{2,1,0:T(2,128)} %all_to_all.37.sums_ref, f32[896,512]{1,0:T(8,128)} %get-tuple-element.32.unscaled_ref), custom_call_target="tpu_custom_call" | custom-call | flops 458752 | bytes 3670016 | tf_op jit(solution)/shard_map/pallas_call | solution.py:34
  (33 shorter events, 6.3 us)
Async XLA Ops:
  7.2 86.0 %all-gather.3.cloned.1.call-start = ((), (), s32[]{:S(2)}) async-start(), calls=%async_computation.7 | async-start | bytes 8650752 | tf_op jit(solution)/shard_map/all_gather | solution.py:79
  17.2 11.4 %copy-start.1 = (f32[48,256]{1,0:T(8,128)S(1)}, f32[48,256]{1,0:T(8,128)}, u32[]{:S(2)}) copy-start(f32[48,256]{1,0:T(8,128)} %param.9) | copy-start | bytes 147460
  17.2 11.4 %copy-start.2 = (f32[48,256]{1,0:T(8,128)S(1)}, f32[48,256]{1,0:T(8,128)}, u32[]{:S(2)}) copy-start(f32[48,256]{1,0:T(8,128)} %param.8) | copy-start | bytes 147460
  18.4 15.1 %copy-start = (f32[896,512]{1,0:T(8,128)S(1)}, f32[896,512]{1,0:T(8,128)}, u32[]{:S(2)}) copy-start(f32[896,512]{1,0:T(8,128)} %param.5) | copy-start | bytes 5505028
  18.4 46.3 %all-to-all-start = ((bf16[8,96,896]{2,1,0:T(8,128)(2,1)}), bf16[8,96,896]{2,1,0:T(8,128)(2,1)S(1)}, u32[]{:S(2)}, u32[]{:S(2)}) async-start(bf16[8,96,896]{2,1,0:T(8,128)(2,1)} %broadcast_in_dim.12), calls=%async_computation | async-start | bytes 2752512 | tf_op jit(solution)/shard_map/all_to_all | solution.py:62
  28.6 5.8 %collective-permute-start = (f32[2,24,256]{2,1,0:T(8,128)S(1)}, f32[2,24,256]{2,1,0:T(8,128)S(1)}, u32[]{:S(2)}, u32[]{:S(2)}) collective-permute-start(f32[2,24,256]{2,1,0:T(8,128)S(1)} %broadcast_select_fusion), channel_id=1, source_target_pairs={{0,16},{16,0},{1,17},{17,1},{2,18},{18,2},{3,19},{19,3},{4,20},{20... | collective-permute-start | bytes 147464 | tf_op jit(solution)/shard_map/ppermute | solution.py:83
  65.8 3.8 %collective-permute-start.1 = (bf16[16,24,512]{2,1,0:T(8,128)(2,1)S(1)}, bf16[16,24,512]{2,1,0:T(8,128)(2,1)S(1)}, u32[]{:S(2)}, u32[]{:S(2)}) collective-permute-start(bf16[16,24,512]{2,1,0:T(8,128)(2,1)S(1)} %fusion.7), channel_id=1, source_target_pairs={{0,16},{16,0},{1,17},{17,1},{2,18},{18,2},{3,19},{19,3},{4,20},{20... | collective-permute-start | bytes 1179656 | tf_op jit(solution)/shard_map/ppermute | solution.py:93
  70.5 22.5 %all-to-all-start.1 = ((bf16[16,24,512]{2,1,0:T(8,128)(2,1)}), bf16[16,24,512]{2,1,0:T(8,128)(2,1)S(1)}, u32[]{:S(2)}, u32[]{:S(2)}) async-start(bf16[16,24,512]{2,1,0:T(8,128)(2,1)} %fusion.6), calls=%async_computation.1 | async-start | bytes 786432 | tf_op jit(solution)/shard_map/all_to_all | solution.py:66
  79.3 13.8 %collective-permute-start.2 = (f32[2,2,24,256]{3,2,1,0:T(8,128)S(1)}, f32[2,2,24,256]{3,2,1,0:T(8,128)S(1)}, u32[]{:S(2)}, u32[]{:S(2)}) collective-permute-start(f32[2,2,24,256]{3,2,1,0:T(8,128)S(1)} %pad_maximum_fusion), channel_id=1, source_target_pairs={{0,0},{1,32},{2,64},{3,96},{4,128},{5,160},{6,192},{7,224},{8,256}... | collective-permute-start | bytes 294920 | tf_op jit(solution)/shard_map/ppermute | solution.py:89
  124.9 22.0 %all-to-all-start.3 = ((bf16[16,2,24,256]{3,2,1,0:T(8,128)(2,1)}), bf16[16,2,24,256]{3,2,1,0:T(8,128)(2,1)S(1)}, u32[]{:S(2)}, u32[]{:S(2)}) async-start(bf16[16,2,24,256]{3,2,1,0:T(8,128)(2,1)} %broadcast_in_dim.14), calls=%async_computation.3 | async-start | bytes 786432 | tf_op jit(solution)/shard_map/all_to_all | solution.py:62
  133.0 0.7 collective-permute-start.3
  153.3 23.3 %all-to-all-start.4 = ((bf16[16,24,512]{2,1,0:T(8,128)(2,1)}), bf16[16,24,512]{2,1,0:T(8,128)(2,1)S(1)}, u32[]{:S(2)}, u32[]{:S(2)}) async-start(bf16[16,24,512]{2,1,0:T(8,128)(2,1)} %broadcast_in_dim.15), calls=%async_computation.4 | async-start | bytes 786432 | tf_op jit(solution)/shard_map/all_to_all | solution.py:62
  163.7 3.8 %collective-permute-start.4 = (f32[24,256]{1,0:T(8,128)S(1)}, f32[24,256]{1,0:T(8,128)S(1)}, u32[]{:S(2)}, u32[]{:S(2)}) collective-permute-start(f32[24,256]{1,0:T(8,128)S(1)} %select_bitcast_fusion.2), channel_id=1, source_target_pairs={{0,16},{16,0},{1,17},{17,1},{2,18},{18,2},{3,19},{19,3},{4,20},{20... | collective-permute-start | bytes 73736 | tf_op jit(solution)/shard_map/ppermute | solution.py:109
Sparse Core Ops, SparseCore 0:
  10.1 79.8 all-gather.2

commit v7 on v5

--- a/solution.py
+++ b/solution.py
@@ -103,17 +103,18 @@
     )
 
     half = spread(returned.astype(bf16), ("x", "y"), 16)
+    keep, send = sort(rotated[0], rotated[1])
+    rotated = jnp.concatenate(sort(keep, lax.ppermute(send, "c", SWAP)))
+    half, rotated = lax.optimization_barrier((half, rotated))
     returned = lax.all_gather(half, "c", axis=1, tiled=True).reshape(768, 512)
     unscaled = lax.dot_general(
         panels, returned, (((0,), (0,)), ((), ())), preferred_element_type=f32
     )
     sums = jnp.stack([grad_lanes, lanes(unscaled)])
     sums = jnp.sum(spread(sums, ("x", "c"), 8), axis=0)
+    sums, rotated = lax.optimization_barrier((sums, rotated))
     update = scale(spread(sums, ("y", "z", "h"), 64), unscaled)
-
     rotated = lax.ppermute(rotated, ("x", "y", "z", "h"), TURN)
-    keep, send = sort(rotated[0], rotated[1])
-    rotated = jnp.concatenate(sort(keep, lax.ppermute(send, "c", SWAP)))
     new_moment, new_variance, _ = adam(moment, variance, rotated)
     return (update, new_moment, new_variance)
 

time: 222 us -> 220 us (level)
  blocking collectives: 61.2 us -> 68 us
  waiting for transfers between devices: 71 us -> 66 us
  starting transfers between devices: 55.9 us -> 53 us
    all_to_all x1 -> x2, blocking collectives: 21.3 us -> 28.6 us  [spread(): return lax.all_to_all(copies, axes, 0, 0, tiled=True)]
    all_to_all x4 -> x3, waiting for transfers between devices: 55.2 us -> 49.4 us  [spread(): return lax.all_to_all(copies, axes, 0, 0, tiled=True)]
    all_to_all x4 -> x3, starting transfers between devices: 35.3 us -> 32.4 us  [spread(): return lax.all_to_all(copies, axes, 0, 0, tiled=True)]
  transfers between devices with their start and end apart: 11 -> 10, of which waited for: 7 -> 7; matrix products, arithmetic and copies ran while one was open for 3% -> 2% of each run, Pallas kernels for 0% -> 0%
where the time goes in v7:
time: 220 us
  blocking collectives  68 us (31%)
  waiting for transfers between devices  66 us (30%)
  starting transfers between devices  53 us (24%)
  between operations  14.2 us (6%)
  matrix products  10.2 us (5%)
  local copies, waits for them, and re-layouts  3.29 us (1%)
  Pallas kernels  2.7 us (1%)
    all_to_all x3, waiting for transfers between devices, spread(): return lax.all_to_all(copies, axes, 0, 0, tiled=True)  49.4 us
    all_to_all x3, starting transfers between devices, spread(): return lax.all_to_all(copies, axes, 0, 0, tiled=True)  32.4 us
    all_to_all x2, blocking collectives, spread(): return lax.all_to_all(copies, axes, 0, 0, tiled=True)  28.6 us
    all_to_all x1, blocking collectives, collect(): got = lax.all_to_all(parts, axes, 0, 0, tiled=True)  26.4 us
    all_to_all x1, waiting for transfers between devices, collect(): got = lax.all_to_all(parts, axes, 0, 0, tiled=True)  13.1 us
    all_gather x1, blocking collectives, body(): panels = spread(lax.all_gather(left_basis, 'h', tiled=True), 'z', 8)  9.28 us
    all_to_all x1, starting transfers between devices, collect(): got = lax.all_to_all(parts, axes, 0, 0, tiled=True)  8.79 us
    ppermute x1, starting transfers between devices, body(): blocks = sort(keep, lax.ppermute(send, 'c', SWAP))  4.91 us
  transfers between devices with their start and end apart: 10, of which 7 were waited for; matrix products, arithmetic and copies ran while one was open for 2% of the time, Pallas kernels for 0%

profile of v7, /device:TPU:1, one launch (start us, length us, event | category | flops | bytes accessed | tf_op | source)
XLA Modules:
  0.0 219.6 jit_solution(16663180896158877759)
XLA Ops:
  7.9 9.3 %all_gather.12 = bf16[96,896]{1,0:T(8,128)(2,1)S(1)} all-gather(bf16[48,896]{1,0:T(8,128)(2,1)} %param.6), channel_id=1, replica_groups=mesh['x'=4,'y'=4,'c'=2,'z'=8,'h'=2] {'h'}, dimensions={0}, use_global_device_ids=true | all-gather | bytes 258048 | tf_op jit(solution)/shard_map/all_gather | solution.py:87
  17.2 1.2 broadcast_in_dim.12
  18.4 10.2 %all-to-all-start = ((bf16[8,96,896]{2,1,0:T(8,128)(2,1)}), bf16[8,96,896]{2,1,0:T(8,128)(2,1)S(1)}, u32[]{:S(2)}, u32[]{:S(2)}) async-start(bf16[8,96,896]{2,1,0:T(8,128)(2,1)} %broadcast_in_dim.12), calls=%async_computation | async-start | bytes 2752512 | tf_op jit(solution)/shard_map/all_to_all | solution.py:62
  28.6 4.9 %collective-permute-start = (f32[2,24,256]{2,1,0:T(8,128)S(1)}, f32[2,24,256]{2,1,0:T(8,128)S(1)}, u32[]{:S(2)}, u32[]{:S(2)}) collective-permute-start(f32[2,24,256]{2,1,0:T(8,128)S(1)} %broadcast_select_fusion), channel_id=1, source_target_pairs={{0,16},{16,0},{1,17},{17,1},{2,18},{18,2},{3,19},{19,3},{4,20},{20... | collective-permute-start | bytes 147464 | tf_op jit(solution)/shard_map/ppermute | solution.py:83
  34.4 30.3 %all-to-all-done = bf16[8,96,896]{2,1,0:T(8,128)(2,1)S(1)} async-done(((bf16[8,96,896]{2,1,0:T(8,128)(2,1)}), bf16[8,96,896]{2,1,0:T(8,128)(2,1)S(1)}, u32[]{:S(2)}, u32[]{:S(2)}) %all-to-all-start) | async-done | bytes 1376288 | tf_op jit(solution)/shard_map/all_to_all | solution.py:62
  64.7 1.0 fusion.1
  65.8 2.5 %collective-permute-start.1 = (bf16[16,24,512]{2,1,0:T(8,128)(2,1)S(1)}, bf16[16,24,512]{2,1,0:T(8,128)(2,1)S(1)}, u32[]{:S(2)}, u32[]{:S(2)}) collective-permute-start(bf16[16,24,512]{2,1,0:T(8,128)(2,1)S(1)} %fusion.7), channel_id=1, source_target_pairs={{0,16},{16,0},{1,17},{17,1},{2,18},{18,2},{3,19},{19,3},{4,20},{20... | collective-permute-start | bytes 1179656 | tf_op jit(solution)/shard_map/ppermute | solution.py:93
  68.3 1.3 collective-permute-done.1
  69.6 1.0 fusion.6
  70.5 8.8 %all-to-all-start.1 = ((bf16[16,24,512]{2,1,0:T(8,128)(2,1)}), bf16[16,24,512]{2,1,0:T(8,128)(2,1)S(1)}, u32[]{:S(2)}, u32[]{:S(2)}) async-start(bf16[16,24,512]{2,1,0:T(8,128)(2,1)} %fusion.6), calls=%async_computation.1 | async-start | bytes 786432 | tf_op jit(solution)/shard_map/all_to_all | solution.py:66
  80.0 13.1 %all-to-all-done.1 = bf16[16,24,512]{2,1,0:T(8,128)(2,1)S(1)} async-done(((bf16[16,24,512]{2,1,0:T(8,128)(2,1)}), bf16[16,24,512]{2,1,0:T(8,128)(2,1)S(1)}, u32[]{:S(2)}, u32[]{:S(2)}) %all-to-all-start.1) | async-done | bytes 393248 | tf_op jit(solution)/shard_map/all_to_all | solution.py:66
  93.2 4.7 %convolution_convert_fusion = bf16[24,32,256]{2,0,1:T(8,128)(2,1)S(1)} fusion(bf16[32,512,256]{2,1,0:T(8,128)(2,1)} %bitcast.73, bf16[24,512]{1,0:T(8,128)(2,1)S(1)} %fusion.17), kind=kOutput, calls=%fused_computation.2 | convolution fusion | flops 201523200 | bytes 8806400 | tf_op jit(solution)/shard_map/rk,fkn->frn/dot_general | solution.py:97
  97.9 26.4 %all_to_all.35 = bf16[16,2,24,256]{3,2,1,0:T(8,128)(2,1)S(1)} all-to-all(bf16[16,2,24,256]{3,2,1,0:T(8,128)(2,1)S(1)} %bitcast.76), channel_id=1, replica_groups=mesh['x'=4,'y'=4,'c'=2,'z'=8,'h'=2] {'z','h'}, dimensions={0} | all-to-all | bytes 786432 | tf_op jit(solution)/shard_map/all_to_all | solution.py:66
  124.4 21.3 %all_to_all.36 = bf16[16,2,24,256]{3,2,1,0:T(8,128)(2,1)S(1)} all-to-all(bf16[16,2,24,256]{3,2,1,0:T(8,128)(2,1)S(1)} %broadcast_in_dim.14), channel_id=1, replica_groups=mesh['x'=4,'y'=4,'c'=2,'z'=8,'h'=2] {'z','h'}, dimensions={0} | all-to-all | bytes 786432 | tf_op jit(solution)/shard_map/all_to_all | solution.py:62
  145.7 2.3 %fusion = bf16[24,512]{1,0:T(8,128)(2,1)S(1)} fusion(bf16[32,24,256]{2,1,0:T(8,128)(2,1)S(1)} %bitcast.75, bf16[32,512,256]{2,1,0:T(8,128)(2,1)S(1)} %bitcast.74), kind=kOutput, calls=%fused_computation.4 | convolution fusion | flops 201338880 | bytes 8806400 | tf_op jit(solution)/shard_map/dot_general | solution.py:101
  148.8 9.2 %all-to-all-start.4 = ((bf16[16,24,512]{2,1,0:T(8,128)(2,1)}), bf16[16,24,512]{2,1,0:T(8,128)(2,1)S(1)}, u32[]{:S(2)}, u32[]{:S(2)}) async-start(bf16[16,24,512]{2,1,0:T(8,128)(2,1)} %broadcast_in_dim.15), calls=%async_computation.4 | async-start | bytes 786432 | tf_op jit(solution)/shard_map/all_to_all | solution.py:62
  158.0 3.1 %collective-permute-start.3 = (f32[24,256]{1,0:T(8,128)S(1)}, f32[24,256]{1,0:T(8,128)S(1)}, u32[]{:S(2)}, u32[]{:S(2)}) collective-permute-start(f32[24,256]{1,0:T(8,128)S(1)} %select_bitcast_fusion.2), channel_id=1, source_target_pairs={{0,16},{16,0},{1,17},{17,1},{2,18},{18,2},{3,19},{19,3},{4,20},{20... | collective-permute-start | bytes 73736 | tf_op jit(solution)/shard_map/ppermute | solution.py:107
  161.9 8.9 %all-to-all-done.4 = bf16[16,24,512]{2,1,0:T(8,128)(2,1)S(1)} async-done(((bf16[16,24,512]{2,1,0:T(8,128)(2,1)}), bf16[16,24,512]{2,1,0:T(8,128)(2,1)S(1)}, u32[]{:S(2)}, u32[]{:S(2)}) %all-to-all-start.4) | async-done | bytes 393248 | tf_op jit(solution)/shard_map/all_to_all | solution.py:62
  170.9 3.7 %all_gather.15 = bf16[16,48,512]{2,1,0:T(8,128)(2,1)S(1)} all-gather(bf16[16,24,512]{2,1,0:T(8,128)(2,1)S(1)} %all-to-all-done.4), channel_id=1, replica_groups=mesh['x'=4,'y'=4,'c'=2,'z'=8,'h'=2] {'c'}, dimensions={1}, use_global_device_ids=true | all-gather | bytes 1179648 | tf_op jit(solution)/shard_map/all_gather | solution.py:109
  174.6 2.2 multiply_reduce_fusion
  176.8 7.3 %all_to_all.37 = f32[8,2,128]{2,1,0:T(2,128)S(1)} all-to-all(f32[8,2,128]{2,1,0:T(2,128)S(1)} %broadcast_in_dim.16), channel_id=1, replica_groups=mesh['x'=4,'y'=4,'c'=2,'z'=8,'h'=2] {'x','c'}, dimensions={0} | all-to-all | bytes 16384 | tf_op jit(solution)/shard_map/all_to_all | solution.py:62
  185.5 13.0 %all-to-all-start.6 = ((f32[64,2,128]{2,1,0:T(2,128)}), f32[64,2,128]{2,1,0:T(2,128)S(1)}, u32[]{:S(2)}, u32[]{:S(2)}) async-start(f32[64,2,128]{2,1,0:T(2,128)} %broadcast_in_dim.17), calls=%async_computation.6 | async-start | bytes 131072 | tf_op jit(solution)/shard_map/all_to_all | solution.py:62
  199.2 10.2 %all-to-all-done.6.sums_ref = f32[64,2,128]{2,1,0:T(2,128)S(1)} async-done(((f32[64,2,128]{2,1,0:T(2,128)}), f32[64,2,128]{2,1,0:T(2,128)S(1)}, u32[]{:S(2)}, u32[]{:S(2)}) %all-to-all-start.6) | async-done | bytes 65568 | tf_op jit(solution)/shard_map/all_to_all | solution.py:62
  210.0 2.7 %shard_map.76 = f32[896,512]{1,0:T(8,128)} custom-call(f32[64,2,128]{2,1,0:T(2,128)} %copy-done.4, f32[896,512]{1,0:T(8,128)} %get-tuple-element.30.unscaled_ref), custom_call_target="tpu_custom_call" | custom-call | flops 458752 | bytes 3670016 | tf_op jit(solution)/shard_map/pallas_call | solution.py:34
  (38 shorter events, 6.8 us)
Async XLA Ops:
  7.2 86.0 %all-gather.3.cloned.1.call-start = ((), (), s32[]{:S(2)}) async-start(), calls=%async_computation.7 | async-start | bytes 8650752 | tf_op jit(solution)/shard_map/all_gather | solution.py:79
  17.2 11.4 %copy-start.2 = (f32[48,256]{1,0:T(8,128)S(1)}, f32[48,256]{1,0:T(8,128)}, u32[]{:S(2)}) copy-start(f32[48,256]{1,0:T(8,128)} %param.9) | copy-start | bytes 147460
  17.2 11.4 %copy-start.3 = (f32[48,256]{1,0:T(8,128)S(1)}, f32[48,256]{1,0:T(8,128)}, u32[]{:S(2)}) copy-start(f32[48,256]{1,0:T(8,128)} %param.8) | copy-start | bytes 147460
  18.4 15.1 %copy-start.1 = (f32[896,512]{1,0:T(8,128)S(1)}, f32[896,512]{1,0:T(8,128)}, u32[]{:S(2)}) copy-start(f32[896,512]{1,0:T(8,128)} %param.5) | copy-start | bytes 5505028
  18.4 46.3 %all-to-all-start = ((bf16[8,96,896]{2,1,0:T(8,128)(2,1)}), bf16[8,96,896]{2,1,0:T(8,128)(2,1)S(1)}, u32[]{:S(2)}, u32[]{:S(2)}) async-start(bf16[8,96,896]{2,1,0:T(8,128)(2,1)} %broadcast_in_dim.12), calls=%async_computation | async-start | bytes 2752512 | tf_op jit(solution)/shard_map/all_to_all | solution.py:62
  28.6 5.8 %collective-permute-start = (f32[2,24,256]{2,1,0:T(8,128)S(1)}, f32[2,24,256]{2,1,0:T(8,128)S(1)}, u32[]{:S(2)}, u32[]{:S(2)}) collective-permute-start(f32[2,24,256]{2,1,0:T(8,128)S(1)} %broadcast_select_fusion), channel_id=1, source_target_pairs={{0,16},{16,0},{1,17},{17,1},{2,18},{18,2},{3,19},{19,3},{4,20},{20... | collective-permute-start | bytes 147464 | tf_op jit(solution)/shard_map/ppermute | solution.py:83
  65.8 3.8 %collective-permute-start.1 = (bf16[16,24,512]{2,1,0:T(8,128)(2,1)S(1)}, bf16[16,24,512]{2,1,0:T(8,128)(2,1)S(1)}, u32[]{:S(2)}, u32[]{:S(2)}) collective-permute-start(bf16[16,24,512]{2,1,0:T(8,128)(2,1)S(1)} %fusion.7), channel_id=1, source_target_pairs={{0,16},{16,0},{1,17},{17,1},{2,18},{18,2},{3,19},{19,3},{4,20},{20... | collective-permute-start | bytes 1179656 | tf_op jit(solution)/shard_map/ppermute | solution.py:93
  70.5 22.5 %all-to-all-start.1 = ((bf16[16,24,512]{2,1,0:T(8,128)(2,1)}), bf16[16,24,512]{2,1,0:T(8,128)(2,1)S(1)}, u32[]{:S(2)}, u32[]{:S(2)}) async-start(bf16[16,24,512]{2,1,0:T(8,128)(2,1)} %fusion.6), calls=%async_computation.1 | async-start | bytes 786432 | tf_op jit(solution)/shard_map/all_to_all | solution.py:66
  79.3 13.8 %collective-permute-start.2 = (f32[2,2,24,256]{3,2,1,0:T(8,128)S(1)}, f32[2,2,24,256]{3,2,1,0:T(8,128)S(1)}, u32[]{:S(2)}, u32[]{:S(2)}) collective-permute-start(f32[2,2,24,256]{3,2,1,0:T(8,128)S(1)} %pad_maximum_fusion), channel_id=1, source_target_pairs={{0,0},{1,32},{2,64},{3,96},{4,128},{5,160},{6,192},{7,224},{8,256}... | collective-permute-start | bytes 294920 | tf_op jit(solution)/shard_map/ppermute | solution.py:89
  93.2 52.5 %copy-start = (bf16[16384,256]{1,0:T(8,128)(2,1)S(1)}, bf16[16384,256]{1,0:T(8,128)(2,1)}, u32[]{:S(2)}) copy-start(bf16[16384,256]{1,0:T(8,128)(2,1)} %all-gather.3.cloned.1.call-done) | copy-start | bytes 25165828
  148.8 22.1 %all-to-all-start.4 = ((bf16[16,24,512]{2,1,0:T(8,128)(2,1)}), bf16[16,24,512]{2,1,0:T(8,128)(2,1)S(1)}, u32[]{:S(2)}, u32[]{:S(2)}) async-start(bf16[16,24,512]{2,1,0:T(8,128)(2,1)} %broadcast_in_dim.15), calls=%async_computation.4 | async-start | bytes 786432 | tf_op jit(solution)/shard_map/all_to_all | solution.py:62
  158.0 3.9 %collective-permute-start.3 = (f32[24,256]{1,0:T(8,128)S(1)}, f32[24,256]{1,0:T(8,128)S(1)}, u32[]{:S(2)}, u32[]{:S(2)}) collective-permute-start(f32[24,256]{1,0:T(8,128)S(1)} %select_bitcast_fusion.2), channel_id=1, source_target_pairs={{0,16},{16,0},{1,17},{17,1},{2,18},{18,2},{3,19},{19,3},{4,20},{20... | collective-permute-start | bytes 73736 | tf_op jit(solution)/shard_map/ppermute | solution.py:107
  184.2 14.4 %collective-permute-start.4 = (f32[48,256]{1,0:T(8,128)S(1)}, f32[48,256]{1,0:T(8,128)S(1)}, u32[]{:S(2)}, u32[]{:S(2)}) collective-permute-start(f32[48,256]{1,0:T(8,128)S(1)} %pad_maximum_fusion.2), channel_id=1, source_target_pairs={{0,0},{1,32},{2,64},{3,96},{4,128},{5,160},{6,192},{7,224},{8,256}... | collective-permute-start | bytes 147464 | tf_op jit(solution)/shard_map/ppermute | solution.py:117
  185.5 23.9 %all-to-all-start.6 = ((f32[64,2,128]{2,1,0:T(2,128)}), f32[64,2,128]{2,1,0:T(2,128)S(1)}, u32[]{:S(2)}, u32[]{:S(2)}) async-start(f32[64,2,128]{2,1,0:T(2,128)} %broadcast_in_dim.17), calls=%async_computation.6 | async-start | bytes 131072 | tf_op jit(solution)/shard_map/all_to_all | solution.py:62
  209.4 0.6 copy-start.4
Sparse Core Ops, SparseCore 0:
  10.1 79.8 all-gather.2

commit v8 on v6

--- a/solution.py
+++ b/solution.py
@@ -14,35 +14,41 @@
 B = ("z", "h")
 SWAP = [(0, 1), (1, 0)]
 TURN = [(16 * i + j, 16 * j + i) for i in range(16) for j in range(16)]
+PARTS = 4
 f32 = jnp.float32
 bf16 = jnp.bfloat16
 
 
-def scale_kernel(sums_ref, unscaled_ref, update_ref, factor_ref):
-    @pl.when(pl.program_id(0) == 0)
-    def _():
-        total = jnp.sum(sums_ref[...], axis=0)
-        total = jnp.sum(total, axis=1, keepdims=True)
-        root = jnp.sqrt(total)
-        factor_ref[...] = jnp.broadcast_to(root[0:1] / (root[1:2] + graft_eps), factor_ref.shape)
-
-    update_ref[...] = unscaled_ref[...] * factor_ref[...]
+def scale_kernel(sums_ref, unscaled_ref, update_ref, scaled_ref, done_ref):
+    total = jnp.sum(sums_ref[...], axis=0)
+    root = jnp.sqrt(jnp.sum(total, axis=1, keepdims=True))
+    factor = root[0:1] / (root[1:2] + graft_eps)
+    size = scaled_ref.shape[0] // PARTS
+    copies = []
+    for part in range(PARTS):
+        rows = pl.ds(part * size, size)
+        scaled_ref[rows] = unscaled_ref[rows] * factor
+        copies.append(
+            pltpu.make_async_copy(scaled_ref.at[rows], update_ref.at[rows], done_ref.at[part])
+        )
+        copies[-1].start()
+    for copy in copies:
+        copy.wait()
 
 
 def scale(sums, unscaled):
-    rows, columns = unscaled.shape
     return pl.pallas_call(
         scale_kernel,
-        grid=(2,),
-        in_specs=[
-            pl.BlockSpec(sums.shape, lambda i: (0, 0, 0)),
-            pl.BlockSpec((rows // 2, columns), lambda i: (i, 0)),
+        in_specs=[pl.BlockSpec(memory_space=pltpu.VMEM)] * 2,
+        out_specs=pl.BlockSpec(memory_space=pl.ANY),
+        out_shape=jax.ShapeDtypeStruct(unscaled.shape, f32),
+        scratch_shapes=[
+            pltpu.VMEM(unscaled.shape, f32),
+            pltpu.SemaphoreType.DMA((PARTS,)),
         ],
-        out_specs=pl.BlockSpec((rows // 2, columns), lambda i: (i, 0)),
-        out_shape=jax.ShapeDtypeStruct(unscaled.shape, f32),
-        scratch_shapes=[pltpu.VMEM((1, columns), f32)],
+        compiler_params=pltpu.CompilerParams(vmem_limit_bytes=16 * 2**20),
         cost_estimate=pl.CostEstimate(
-            flops=rows * columns, bytes_accessed=8 * rows * columns, transcendentals=0
+            flops=unscaled.size, bytes_accessed=8 * unscaled.size, transcendentals=0
         ),
     )(sums, unscaled)
 
@@ -98,13 +104,12 @@
     rotated = collect(rotated.astype(bf16).reshape(16, 2, 24, 256), B)
     direction = (adam(moments[0], moments[1], rotated)[2]).astype(bf16)
     direction = spread(direction, B, 16).reshape(32, 24, 256)
-    rotated = lax.ppermute(rotated, ("x", "y", "z", "h"), TURN)
-    direction, rotated = lax.optimization_barrier((direction, rotated))
     returned = lax.dot_general(
         direction, basis, (((0, 2), (0, 2)), ((), ())), preferred_element_type=f32
     )
 
     half = spread(returned.astype(bf16), ("x", "y"), 16)
+    rotated = lax.ppermute(rotated, ("x", "y", "z", "h"), TURN)
     keep, send = sort(rotated[0], rotated[1])
     rotated = jnp.concatenate(sort(keep, lax.ppermute(send, "c", SWAP)))
     new_moment, new_variance, _ = adam(moment, variance, rotated)

time: 218 us -> 214 us (0.982)
  transfers between devices with their start and end apart: 10 -> 10, of which waited for: 7 -> 7; matrix products, arithmetic and copies ran while one was open for 2% -> 5% of each run, Pallas kernels for 0% -> 0%
where the time goes in v8:
time: 214 us; the launch traced here: 213 us
  waiting for transfers between devices  68 us (32%)
  blocking collectives  63.2 us (30%)
  starting transfers between devices  48.9 us (23%)
  between operations  14.2 us (7%)
  matrix products  12.2 us (6%)
  local copies, waits for them, and re-layouts  2.79 us (1%)
  other arithmetic  2.14 us (1%)
    all_to_all x3, waiting for transfers between devices, spread(): return lax.all_to_all(copies, axes, 0, 0, tiled=True)  51.4 us
    all_to_all x3, starting transfers between devices, spread(): return lax.all_to_all(copies, axes, 0, 0, tiled=True)  27.9 us
    all_to_all x1, blocking collectives, collect(): got = lax.all_to_all(parts, axes, 0, 0, tiled=True)  26.3 us
    all_to_all x2, blocking collectives, spread(): return lax.all_to_all(copies, axes, 0, 0, tiled=True)  24 us
    all_to_all x1, waiting for transfers between devices, collect(): got = lax.all_to_all(parts, axes, 0, 0, tiled=True)  13.1 us
    all_gather x1, blocking collectives, body(): panels = spread(lax.all_gather(left_basis, 'h', tiled=True), 'z', 8)  9.28 us
    all_to_all x1, starting transfers between devices, collect(): got = lax.all_to_all(parts, axes, 0, 0, tiled=True)  8.79 us
    dot_general x1, matrix products, body(): lax.dot_general(direction, basis, (((0, 2), (0, 2)), ((), ())), preferred...  5.68 us
  transfers between devices with their start and end apart: 10, of which 7 were waited for; matrix products, arithmetic and copies ran while one was open for 5% of the time, Pallas kernels for 0%

profile of v8, /device:TPU:1, one launch (start us, length us, event | category | flops | bytes accessed | tf_op | source)
XLA Modules:
  0.0 212.9 jit_solution(12377501310361797636)
XLA Ops:
  7.9 9.3 %all_gather.12 = bf16[96,896]{1,0:T(8,128)(2,1)S(1)} all-gather(bf16[48,896]{1,0:T(8,128)(2,1)} %param.6), channel_id=1, replica_groups=mesh['x'=4,'y'=4,'c'=2,'z'=8,'h'=2] {'h'}, dimensions={0}, use_global_device_ids=true | all-gather | bytes 258048 | tf_op jit(solution)/shard_map/all_gather | solution.py:93
  17.2 1.2 broadcast_in_dim.12
  18.4 10.2 %all-to-all-start = ((bf16[8,96,896]{2,1,0:T(8,128)(2,1)}), bf16[8,96,896]{2,1,0:T(8,128)(2,1)S(1)}, u32[]{:S(2)}, u32[]{:S(2)}) async-start(bf16[8,96,896]{2,1,0:T(8,128)(2,1)} %broadcast_in_dim.12), calls=%async_computation | async-start | bytes 2752512 | tf_op jit(solution)/shard_map/all_to_all | solution.py:68
  28.6 4.9 %collective-permute-start = (f32[2,24,256]{2,1,0:T(8,128)S(1)}, f32[2,24,256]{2,1,0:T(8,128)S(1)}, u32[]{:S(2)}, u32[]{:S(2)}) collective-permute-start(f32[2,24,256]{2,1,0:T(8,128)S(1)} %broadcast_select_fusion), channel_id=1, source_target_pairs={{0,16},{16,0},{1,17},{17,1},{2,18},{18,2},{3,19},{19,3},{4,20},{20... | collective-permute-start | bytes 147464 | tf_op jit(solution)/shard_map/ppermute | solution.py:89
  34.4 30.3 %all-to-all-done = bf16[8,96,896]{2,1,0:T(8,128)(2,1)S(1)} async-done(((bf16[8,96,896]{2,1,0:T(8,128)(2,1)}), bf16[8,96,896]{2,1,0:T(8,128)(2,1)S(1)}, u32[]{:S(2)}, u32[]{:S(2)}) %all-to-all-start) | async-done | bytes 1376288 | tf_op jit(solution)/shard_map/all_to_all | solution.py:68
  64.7 1.0 fusion.1
  65.8 2.5 %collective-permute-start.1 = (bf16[16,24,512]{2,1,0:T(8,128)(2,1)S(1)}, bf16[16,24,512]{2,1,0:T(8,128)(2,1)S(1)}, u32[]{:S(2)}, u32[]{:S(2)}) collective-permute-start(bf16[16,24,512]{2,1,0:T(8,128)(2,1)S(1)} %fusion.7), channel_id=1, source_target_pairs={{0,16},{16,0},{1,17},{17,1},{2,18},{18,2},{3,19},{19,3},{4,20},{20... | collective-permute-start | bytes 1179656 | tf_op jit(solution)/shard_map/ppermute | solution.py:99
  68.3 1.3 collective-permute-done.1
  69.6 1.0 fusion.6
  70.5 8.8 %all-to-all-start.1 = ((bf16[16,24,512]{2,1,0:T(8,128)(2,1)}), bf16[16,24,512]{2,1,0:T(8,128)(2,1)S(1)}, u32[]{:S(2)}, u32[]{:S(2)}) async-start(bf16[16,24,512]{2,1,0:T(8,128)(2,1)} %fusion.6), calls=%async_computation.1 | async-start | bytes 786432 | tf_op jit(solution)/shard_map/all_to_all | solution.py:72
  80.0 13.1 %all-to-all-done.1 = bf16[16,24,512]{2,1,0:T(8,128)(2,1)S(1)} async-done(((bf16[16,24,512]{2,1,0:T(8,128)(2,1)}), bf16[16,24,512]{2,1,0:T(8,128)(2,1)S(1)}, u32[]{:S(2)}, u32[]{:S(2)}) %all-to-all-start.1) | async-done | bytes 393248 | tf_op jit(solution)/shard_map/all_to_all | solution.py:72
  93.2 4.6 %convolution_convert_fusion = bf16[24,32,256]{2,0,1:T(8,128)(2,1)S(1)} fusion(bf16[32,512,256]{2,1,0:T(8,128)(2,1)} %bitcast.74, bf16[24,512]{1,0:T(8,128)(2,1)S(1)} %fusion.17), kind=kOutput, calls=%fused_computation.2 | convolution fusion | flops 201523200 | bytes 8806400 | tf_op jit(solution)/shard_map/rk,fkn->frn/dot_general | solution.py:103
  97.7 26.3 %all_to_all.35 = bf16[16,2,24,256]{3,2,1,0:T(8,128)(2,1)S(1)} all-to-all(bf16[16,2,24,256]{3,2,1,0:T(8,128)(2,1)S(1)} %bitcast.77), channel_id=1, replica_groups=mesh['x'=4,'y'=4,'c'=2,'z'=8,'h'=2] {'z','h'}, dimensions={0} | all-to-all | bytes 786432 | tf_op jit(solution)/shard_map/all_to_all | solution.py:72
  124.9 8.1 %all-to-all-start.3 = ((bf16[16,2,24,256]{3,2,1,0:T(8,128)(2,1)}), bf16[16,2,24,256]{3,2,1,0:T(8,128)(2,1)S(1)}, u32[]{:S(2)}, u32[]{:S(2)}) async-start(bf16[16,2,24,256]{3,2,1,0:T(8,128)(2,1)} %broadcast_in_dim.14), calls=%async_computation.3 | async-start | bytes 786432 | tf_op jit(solution)/shard_map/all_to_all | solution.py:68
  133.7 13.2 %all-to-all-done.3 = bf16[16,2,24,256]{3,2,1,0:T(8,128)(2,1)S(1)} async-done(((bf16[16,2,24,256]{3,2,1,0:T(8,128)(2,1)}), bf16[16,2,24,256]{3,2,1,0:T(8,128)(2,1)S(1)}, u32[]{:S(2)}, u32[]{:S(2)}) %all-to-all-start.3) | async-done | bytes 393248 | tf_op jit(solution)/shard_map/all_to_all | solution.py:68
  146.8 5.7 %fusion = bf16[24,512]{1,0:T(8,128)(2,1)S(1)} fusion(bf16[32,24,256]{2,1,0:T(8,128)(2,1)S(1)} %bitcast.76, bf16[32,512,256]{2,1,0:T(8,128)(2,1)} %bitcast.75), kind=kOutput, calls=%fused_computation.4 | convolution fusion | flops 201338880 | bytes 8806400 | tf_op jit(solution)/shard_map/dot_general | solution.py:107
  153.3 9.6 %all-to-all-start.4 = ((bf16[16,24,512]{2,1,0:T(8,128)(2,1)}), bf16[16,24,512]{2,1,0:T(8,128)(2,1)S(1)}, u32[]{:S(2)}, u32[]{:S(2)}) async-start(bf16[16,24,512]{2,1,0:T(8,128)(2,1)} %broadcast_in_dim.15), calls=%async_computation.4 | async-start | bytes 786432 | tf_op jit(solution)/shard_map/all_to_all | solution.py:68
  163.0 3.4 %collective-permute-start.4 = (f32[24,256]{1,0:T(8,128)S(1)}, f32[24,256]{1,0:T(8,128)S(1)}, u32[]{:S(2)}, u32[]{:S(2)}) collective-permute-start(f32[24,256]{1,0:T(8,128)S(1)} %select_bitcast_fusion.2), channel_id=1, source_target_pairs={{0,16},{16,0},{1,17},{17,1},{2,18},{18,2},{3,19},{19,3},{4,20},{20... | collective-permute-start | bytes 73736 | tf_op jit(solution)/shard_map/ppermute | solution.py:114
  167.9 8.0 %all-to-all-done.4 = bf16[16,24,512]{2,1,0:T(8,128)(2,1)S(1)} async-done(((bf16[16,24,512]{2,1,0:T(8,128)(2,1)}), bf16[16,24,512]{2,1,0:T(8,128)(2,1)S(1)}, u32[]{:S(2)}, u32[]{:S(2)}) %all-to-all-start.4) | async-done | bytes 393248 | tf_op jit(solution)/shard_map/all_to_all | solution.py:68
  175.8 3.7 %all_gather.15 = bf16[16,48,512]{2,1,0:T(8,128)(2,1)S(1)} all-gather(bf16[16,24,512]{2,1,0:T(8,128)(2,1)S(1)} %all-to-all-done.4), channel_id=1, replica_groups=mesh['x'=4,'y'=4,'c'=2,'z'=8,'h'=2] {'c'}, dimensions={1}, use_global_device_ids=true | all-gather | bytes 1179648 | tf_op jit(solution)/shard_map/all_gather | solution.py:117
  179.6 0.9 multiply_reduce_fusion
  180.5 7.3 %all_to_all.36 = f32[8,2,128]{2,1,0:T(2,128)S(1)} all-to-all(f32[8,2,128]{2,1,0:T(2,128)S(1)} %broadcast_in_dim.16), channel_id=1, replica_groups=mesh['x'=4,'y'=4,'c'=2,'z'=8,'h'=2] {'x','c'}, dimensions={0} | all-to-all | bytes 16384 | tf_op jit(solution)/shard_map/all_to_all | solution.py:68
  187.9 16.6 %all_to_all.37.sums_ref = f32[64,2,128]{2,1,0:T(2,128)S(1)} all-to-all(f32[64,2,128]{2,1,0:T(2,128)S(1)} %broadcast_in_dim.17), channel_id=1, replica_groups=mesh['x'=4,'y'=4,'c'=2,'z'=8,'h'=2] {'y','z','h'}, dimensions={0} | all-to-all | bytes 131072 | tf_op jit(solution)/shard_map/all_to_all | solution.py:68
  204.5 1.5 shard_map.76
  (33 shorter events, 6.3 us)
Async XLA Ops:
  7.2 86.0 %all-gather.3.cloned.1.call-start = ((), (), s32[]{:S(2)}) async-start(), calls=%async_computation.7 | async-start | bytes 8650752 | tf_op jit(solution)/shard_map/all_gather | solution.py:85
  17.2 11.4 %copy-start.1 = (f32[48,256]{1,0:T(8,128)S(1)}, f32[48,256]{1,0:T(8,128)}, u32[]{:S(2)}) copy-start(f32[48,256]{1,0:T(8,128)} %param.9) | copy-start | bytes 147460
  17.2 11.4 %copy-start.2 = (f32[48,256]{1,0:T(8,128)S(1)}, f32[48,256]{1,0:T(8,128)}, u32[]{:S(2)}) copy-start(f32[48,256]{1,0:T(8,128)} %param.8) | copy-start | bytes 147460
  18.4 15.1 %copy-start = (f32[896,512]{1,0:T(8,128)S(1)}, f32[896,512]{1,0:T(8,128)}, u32[]{:S(2)}) copy-start(f32[896,512]{1,0:T(8,128)} %param.5) | copy-start | bytes 5505028
  18.4 46.3 %all-to-all-start = ((bf16[8,96,896]{2,1,0:T(8,128)(2,1)}), bf16[8,96,896]{2,1,0:T(8,128)(2,1)S(1)}, u32[]{:S(2)}, u32[]{:S(2)}) async-start(bf16[8,96,896]{2,1,0:T(8,128)(2,1)} %broadcast_in_dim.12), calls=%async_computation | async-start | bytes 2752512 | tf_op jit(solution)/shard_map/all_to_all | solution.py:68
  28.6 5.8 %collective-permute-start = (f32[2,24,256]{2,1,0:T(8,128)S(1)}, f32[2,24,256]{2,1,0:T(8,128)S(1)}, u32[]{:S(2)}, u32[]{:S(2)}) collective-permute-start(f32[2,24,256]{2,1,0:T(8,128)S(1)} %broadcast_select_fusion), channel_id=1, source_target_pairs={{0,16},{16,0},{1,17},{17,1},{2,18},{18,2},{3,19},{19,3},{4,20},{20... | collective-permute-start | bytes 147464 | tf_op jit(solution)/shard_map/ppermute | solution.py:89
  65.8 3.8 %collective-permute-start.1 = (bf16[16,24,512]{2,1,0:T(8,128)(2,1)S(1)}, bf16[16,24,512]{2,1,0:T(8,128)(2,1)S(1)}, u32[]{:S(2)}, u32[]{:S(2)}) collective-permute-start(bf16[16,24,512]{2,1,0:T(8,128)(2,1)S(1)} %fusion.7), channel_id=1, source_target_pairs={{0,16},{16,0},{1,17},{17,1},{2,18},{18,2},{3,19},{19,3},{4,20},{20... | collective-permute-start | bytes 1179656 | tf_op jit(solution)/shard_map/ppermute | solution.py:99
  70.5 22.5 %all-to-all-start.1 = ((bf16[16,24,512]{2,1,0:T(8,128)(2,1)}), bf16[16,24,512]{2,1,0:T(8,128)(2,1)S(1)}, u32[]{:S(2)}, u32[]{:S(2)}) async-start(bf16[16,24,512]{2,1,0:T(8,128)(2,1)} %fusion.6), calls=%async_computation.1 | async-start | bytes 786432 | tf_op jit(solution)/shard_map/all_to_all | solution.py:72
  79.3 13.8 %collective-permute-start.2 = (f32[2,2,24,256]{3,2,1,0:T(8,128)S(1)}, f32[2,2,24,256]{3,2,1,0:T(8,128)S(1)}, u32[]{:S(2)}, u32[]{:S(2)}) collective-permute-start(f32[2,2,24,256]{3,2,1,0:T(8,128)S(1)} %pad_maximum_fusion), channel_id=1, source_target_pairs={{0,0},{1,32},{2,64},{3,96},{4,128},{5,160},{6,192},{7,224},{8,256}... | collective-permute-start | bytes 294920 | tf_op jit(solution)/shard_map/ppermute | solution.py:95
  124.9 22.0 %all-to-all-start.3 = ((bf16[16,2,24,256]{3,2,1,0:T(8,128)(2,1)}), bf16[16,2,24,256]{3,2,1,0:T(8,128)(2,1)S(1)}, u32[]{:S(2)}, u32[]{:S(2)}) async-start(bf16[16,2,24,256]{3,2,1,0:T(8,128)(2,1)} %broadcast_in_dim.14), calls=%async_computation.3 | async-start | bytes 786432 | tf_op jit(solution)/shard_map/all_to_all | solution.py:68
  133.0 29.9 %collective-permute-start.3 = (f32[2,24,256]{2,1,0:T(8,128)S(1)}, f32[2,24,256]{2,1,0:T(8,128)S(1)}, u32[]{:S(2)}, u32[]{:S(2)}) collective-permute-start(f32[2,24,256]{2,1,0:T(8,128)S(1)} %bitcast.85), channel_id=1, source_target_pairs={{0,0},{1,32},{2,64},{3,96},{4,128},{5,160},{6,192},{7,224},{8,256}... | collective-permute-start | bytes 147464 | tf_op jit(solution)/shard_map/ppermute | solution.py:112
  153.3 22.5 %all-to-all-start.4 = ((bf16[16,24,512]{2,1,0:T(8,128)(2,1)}), bf16[16,24,512]{2,1,0:T(8,128)(2,1)S(1)}, u32[]{:S(2)}, u32[]{:S(2)}) async-start(bf16[16,24,512]{2,1,0:T(8,128)(2,1)} %broadcast_in_dim.15), calls=%async_computation.4 | async-start | bytes 786432 | tf_op jit(solution)/shard_map/all_to_all | solution.py:68
  163.0 4.2 %collective-permute-start.4 = (f32[24,256]{1,0:T(8,128)S(1)}, f32[24,256]{1,0:T(8,128)S(1)}, u32[]{:S(2)}, u32[]{:S(2)}) collective-permute-start(f32[24,256]{1,0:T(8,128)S(1)} %select_bitcast_fusion.2), channel_id=1, source_target_pairs={{0,16},{16,0},{1,17},{17,1},{2,18},{18,2},{3,19},{19,3},{4,20},{20... | collective-permute-start | bytes 73736 | tf_op jit(solution)/shard_map/ppermute | solution.py:114
Sparse Core Ops, SparseCore 0:
  10.1 79.8 all-gather.2

commit v9 on v8

--- a/solution.py
+++ b/solution.py
@@ -15,8 +15,62 @@
 SWAP = [(0, 1), (1, 0)]
 TURN = [(16 * i + j, 16 * j + i) for i in range(16) for j in range(16)]
 PARTS = 4
+PIECES = 8
 f32 = jnp.float32
 bf16 = jnp.bfloat16
+
+
+def fetch(basis_ref, held_ref, landed_ref):
+    size = held_ref.shape[0] // PIECES
+    copies = []
+    for piece in range(PIECES):
+        blocks = pl.ds(piece * size, size)
+        copies.append(
+            pltpu.make_async_copy(basis_ref.at[blocks], held_ref.at[blocks], landed_ref.at[piece])
+        )
+        copies[-1].start()
+    return copies, size
+
+
+def rotate_kernel(rows_ref, basis_ref, out_ref, held_ref, landed_ref):
+    copies, size = fetch(basis_ref, held_ref, landed_ref)
+    rows = rows_ref[...]
+    for piece, copy in enumerate(copies):
+        copy.wait()
+        for block in range(piece * size, (piece + 1) * size):
+            product = jnp.dot(rows, held_ref[block], preferred_element_type=f32)
+            out_ref[block] = product.astype(bf16)
+
+
+def back_kernel(direction_ref, basis_ref, out_ref, held_ref, landed_ref):
+    copies, size = fetch(basis_ref, held_ref, landed_ref)
+    total = jnp.zeros(out_ref.shape[1:], f32)
+    for piece, copy in enumerate(copies):
+        copy.wait()
+        for block in range(piece * size, (piece + 1) * size):
+            total += lax.dot_general(
+                direction_ref[block],
+                held_ref[block],
+                (((1,), (1,)), ((), ())),
+                preferred_element_type=f32,
+            )
+    total = total.astype(bf16)
+    for target in range(out_ref.shape[0]):
+        out_ref[target] = total
+
+
+def with_basis(kernel, left, basis, shape):
+    return pl.pallas_call(
+        kernel,
+        in_specs=[pl.BlockSpec(memory_space=pltpu.VMEM), pl.BlockSpec(memory_space=pl.ANY)],
+        out_specs=pl.BlockSpec(memory_space=pltpu.VMEM),
+        out_shape=jax.ShapeDtypeStruct(shape, bf16),
+        scratch_shapes=[pltpu.VMEM(basis.shape, bf16), pltpu.SemaphoreType.DMA((PIECES,))],
+        compiler_params=pltpu.CompilerParams(vmem_limit_bytes=24 * 2**20),
+        cost_estimate=pl.CostEstimate(
+            flops=48 * basis.size, bytes_accessed=2 * basis.size, transcendentals=0
+        ),
+    )(left, basis)
 
 
 def scale_kernel(sums_ref, unscaled_ref, update_ref, scaled_ref, done_ref):
@@ -100,15 +154,12 @@
     projected = collect(keep.astype(bf16), ("x", "y")).astype(bf16)
     projected, moments = lax.optimization_barrier((projected, moments))
 
-    rotated = jnp.einsum("rk,fkn->frn", projected, basis, preferred_element_type=f32)
-    rotated = collect(rotated.astype(bf16).reshape(16, 2, 24, 256), B)
+    rotated = with_basis(rotate_kernel, projected, basis, (32, 24, 256))
+    rotated = collect(rotated.reshape(16, 2, 24, 256), B)
     direction = (adam(moments[0], moments[1], rotated)[2]).astype(bf16)
     direction = spread(direction, B, 16).reshape(32, 24, 256)
-    returned = lax.dot_general(
-        direction, basis, (((0, 2), (0, 2)), ((), ())), preferred_element_type=f32
-    )
-
-    half = spread(returned.astype(bf16), ("x", "y"), 16)
+    returned = with_basis(back_kernel, direction, basis, (16, 24, 512))
+    half = lax.all_to_all(returned, ("x", "y"), 0, 0, tiled=True)
     rotated = lax.ppermute(rotated, ("x", "y", "z", "h"), TURN)
     keep, send = sort(rotated[0], rotated[1])
     rotated = jnp.concatenate(sort(keep, lax.ppermute(send, "c", SWAP)))

time: 214 us -> 216 us (level)
  matrix products: 12.2 us -> 1.93 us
  Pallas kernels: 1.48 us -> 8.42 us
  local copies, waits for them, and re-layouts: 2.79 us -> 8.75 us
    dot_general x2 -> x0, matrix products: 10.3 us -> none  [the longest x1 5.68 us: body(): lax.dot_general(direction, basis, (((0, 2), (0, 2)), ((), ())), preferred...]
    all_to_all x3 -> x2, starting transfers between devices: 27.9 us -> 18.3 us  [spread(): return lax.all_to_all(copies, axes, 0, 0, tiled=True)]
    all_to_all x0 -> x1, starting transfers between devices: none -> 9.41 us  [body(): half = lax.all_to_all(returned, ('x', 'y'), 0, 0, tiled=True)]
    all_to_all x0 -> x1, waiting for transfers between devices: none -> 8.1 us  [body(): half = lax.all_to_all(returned, ('x', 'y'), 0, 0, tiled=True)]
    all_to_all x3 -> x2, waiting for transfers between devices: 51.4 us -> 43.5 us  [spread(): return lax.all_to_all(copies, axes, 0, 0, tiled=True)]
    pallas_call x0 -> x2, Pallas kernels: none -> 6.94 us  [with_basis(): pl.pallas_call(kernel, in_specs=[pl.BlockSpec(memory_space=pltpu.VMEM), p...]
    unnamed x6 -> x10, local copies, waits for them, and re-layouts: 0.01 us -> 6.77 us
  transfers between devices with their start and end apart: 10 -> 10, of which waited for: 7 -> 7; matrix products, arithmetic and copies ran while one was open for 5% -> 2% of each run, Pallas kernels for 0% -> 2%
where the time goes in v9:
time: 216 us
  waiting for transfers between devices  68.1 us (32%)
  blocking collectives  63.4 us (29%)
  starting transfers between devices  48.5 us (22%)
  between operations  14.2 us (7%)
  local copies, waits for them, and re-layouts  8.75 us (4%)
  Pallas kernels  8.42 us (4%)
  other arithmetic  2.16 us (1%)
    all_to_all x2, waiting for transfers between devices, spread(): return lax.all_to_all(copies, axes, 0, 0, tiled=True)  43.5 us
    all_to_all x1, blocking collectives, collect(): got = lax.all_to_all(parts, axes, 0, 0, tiled=True)  26.2 us
    all_to_all x2, blocking collectives, spread(): return lax.all_to_all(copies, axes, 0, 0, tiled=True)  24.1 us
    all_to_all x2, starting transfers between devices, spread(): return lax.all_to_all(copies, axes, 0, 0, tiled=True)  18.3 us
    all_to_all x1, waiting for transfers between devices, collect(): got = lax.all_to_all(parts, axes, 0, 0, tiled=True)  13.1 us
    all_to_all x1, starting transfers between devices, body(): half = lax.all_to_all(returned, ('x', 'y'), 0, 0, tiled=True)  9.41 us
    all_gather x1, blocking collectives, body(): panels = spread(lax.all_gather(left_basis, 'h', tiled=True), 'z', 8)  9.28 us
    all_to_all x1, starting transfers between devices, collect(): got = lax.all_to_all(parts, axes, 0, 0, tiled=True)  8.79 us
  transfers between devices with their start and end apart: 10, of which 7 were waited for; matrix products, arithmetic and copies ran while one was open for 2% of the time, Pallas kernels for 2%

profile of v9, /device:TPU:1, one launch (start us, length us, event | category | flops | bytes accessed | tf_op | source)
XLA Modules:
  0.0 215.5 jit_solution(14924455857501606367)
XLA Ops:
  7.9 9.3 %all_gather.12 = bf16[96,896]{1,0:T(8,128)(2,1)S(1)} all-gather(bf16[48,896]{1,0:T(8,128)(2,1)} %param.6), channel_id=1, replica_groups=mesh['x'=4,'y'=4,'c'=2,'z'=8,'h'=2] {'h'}, dimensions={0}, use_global_device_ids=true | all-gather | bytes 258048 | tf_op jit(solution)/shard_map/all_gather | solution.py:147
  17.2 1.2 broadcast_in_dim.10
  18.4 10.2 %all-to-all-start = ((bf16[8,96,896]{2,1,0:T(8,128)(2,1)}), bf16[8,96,896]{2,1,0:T(8,128)(2,1)S(1)}, u32[]{:S(2)}, u32[]{:S(2)}) async-start(bf16[8,96,896]{2,1,0:T(8,128)(2,1)} %broadcast_in_dim.10), calls=%async_computation | async-start | bytes 2752512 | tf_op jit(solution)/shard_map/all_to_all | solution.py:122
  28.6 4.9 %collective-permute-start = (f32[2,24,256]{2,1,0:T(8,128)S(1)}, f32[2,24,256]{2,1,0:T(8,128)S(1)}, u32[]{:S(2)}, u32[]{:S(2)}) collective-permute-start(f32[2,24,256]{2,1,0:T(8,128)S(1)} %broadcast_select_fusion), channel_id=1, source_target_pairs={{0,16},{16,0},{1,17},{17,1},{2,18},{18,2},{3,19},{19,3},{4,20},{20... | collective-permute-start | bytes 147464 | tf_op jit(solution)/shard_map/ppermute | solution.py:143
  34.4 30.3 %all-to-all-done = bf16[8,96,896]{2,1,0:T(8,128)(2,1)S(1)} async-done(((bf16[8,96,896]{2,1,0:T(8,128)(2,1)}), bf16[8,96,896]{2,1,0:T(8,128)(2,1)S(1)}, u32[]{:S(2)}, u32[]{:S(2)}) %all-to-all-start) | async-done | bytes 1376288 | tf_op jit(solution)/shard_map/all_to_all | solution.py:122
  64.7 1.0 fusion
  65.8 2.5 %collective-permute-start.1 = (bf16[16,24,512]{2,1,0:T(8,128)(2,1)S(1)}, bf16[16,24,512]{2,1,0:T(8,128)(2,1)S(1)}, u32[]{:S(2)}, u32[]{:S(2)}) collective-permute-start(bf16[16,24,512]{2,1,0:T(8,128)(2,1)S(1)} %fusion.5), channel_id=1, source_target_pairs={{0,16},{16,0},{1,17},{17,1},{2,18},{18,2},{3,19},{19,3},{4,20},{20... | collective-permute-start | bytes 1179656 | tf_op jit(solution)/shard_map/ppermute | solution.py:153
  68.2 1.3 collective-permute-done.1
  70.6 8.8 %all-to-all-start.1 = ((bf16[16,24,512]{2,1,0:T(8,128)(2,1)}), bf16[16,24,512]{2,1,0:T(8,128)(2,1)S(1)}, u32[]{:S(2)}, u32[]{:S(2)}) async-start(bf16[16,24,512]{2,1,0:T(8,128)(2,1)} %fusion.4), calls=%async_computation.1 | async-start | bytes 786432 | tf_op jit(solution)/shard_map/all_to_all | solution.py:126
  80.0 13.1 %all-to-all-done.1 = bf16[16,24,512]{2,1,0:T(8,128)(2,1)S(1)} async-done(((bf16[16,24,512]{2,1,0:T(8,128)(2,1)}), bf16[16,24,512]{2,1,0:T(8,128)(2,1)S(1)}, u32[]{:S(2)}, u32[]{:S(2)}) %all-to-all-start.1) | async-done | bytes 393248 | tf_op jit(solution)/shard_map/all_to_all | solution.py:126
  93.2 3.4 %copy-done = bf16[16384,256]{1,0:T(8,128)(2,1)S(1)} copy-done((bf16[16384,256]{1,0:T(8,128)(2,1)S(1)}, bf16[16384,256]{1,0:T(8,128)(2,1)}, u32[]{:S(2)}) %copy-start) | copy-done | bytes 8388632
  96.6 2.9 %shard_map.76 = bf16[32,24,256]{2,1,0:T(8,128)(2,1)S(1)} custom-call(bf16[24,512]{1,0:T(8,128)(2,1)S(1)} %fusion.14.rows_ref, bf16[32,512,256]{2,1,0:T(8,128)(2,1)S(1)} %bitcast.41), custom_call_target="tpu_custom_call" | custom-call | flops 201326592 | bytes 8388608 | tf_op jit(solution)/shard_map/pallas_call | solution.py:63
  99.5 26.2 %all_to_all.35 = bf16[16,2,24,256]{3,2,1,0:T(8,128)(2,1)S(1)} all-to-all(bf16[16,2,24,256]{3,2,1,0:T(8,128)(2,1)S(1)} %bitcast.44), channel_id=1, replica_groups=mesh['x'=4,'y'=4,'c'=2,'z'=8,'h'=2] {'z','h'}, dimensions={0} | all-to-all | bytes 786432 | tf_op jit(solution)/shard_map/all_to_all | solution.py:126
  126.6 8.1 %all-to-all-start.3 = ((bf16[16,2,24,256]{3,2,1,0:T(8,128)(2,1)}), bf16[16,2,24,256]{3,2,1,0:T(8,128)(2,1)S(1)}, u32[]{:S(2)}, u32[]{:S(2)}) async-start(bf16[16,2,24,256]{3,2,1,0:T(8,128)(2,1)} %broadcast_in_dim.12), calls=%async_computation.3 | async-start | bytes 786432 | tf_op jit(solution)/shard_map/all_to_all | solution.py:122
  135.4 13.2 %all-to-all-done.3 = bf16[16,2,24,256]{3,2,1,0:T(8,128)(2,1)S(1)} async-done(((bf16[16,2,24,256]{3,2,1,0:T(8,128)(2,1)}), bf16[16,2,24,256]{3,2,1,0:T(8,128)(2,1)S(1)}, u32[]{:S(2)}, u32[]{:S(2)}) %all-to-all-start.3) | async-done | bytes 393248 | tf_op jit(solution)/shard_map/all_to_all | solution.py:122
  148.6 3.4 %copy-done.1 = bf16[16384,256]{1,0:T(8,128)(2,1)S(1)} copy-done((bf16[16384,256]{1,0:T(8,128)(2,1)S(1)}, bf16[16384,256]{1,0:T(8,128)(2,1)}, u32[]{:S(2)}) %copy-start.1) | copy-done | bytes 8388632
  152.0 4.0 %shard_map.77 = bf16[16,24,512]{2,1,0:T(8,128)(2,1)} custom-call(bf16[32,24,256]{2,1,0:T(8,128)(2,1)S(1)} %bitcast.43, bf16[32,512,256]{2,1,0:T(8,128)(2,1)S(1)} %bitcast.42), custom_call_target="tpu_custom_call" | custom-call | flops 201326592 | bytes 8388608 | tf_op jit(solution)/shard_map/pallas_call | solution.py:63
  156.0 9.4 %all-to-all-start.4 = ((bf16[16,24,512]{2,1,0:T(8,128)(2,1)}), bf16[16,24,512]{2,1,0:T(8,128)(2,1)S(1)}, u32[]{:S(2)}, u32[]{:S(2)}) async-start(bf16[16,24,512]{2,1,0:T(8,128)(2,1)} %shard_map.77), calls=%async_computation.4 | async-start | bytes 786432 | tf_op jit(solution)/shard_map/all_to_all | solution.py:162
  165.4 3.3 %collective-permute-start.4 = (f32[24,256]{1,0:T(8,128)S(1)}, f32[24,256]{1,0:T(8,128)S(1)}, u32[]{:S(2)}, u32[]{:S(2)}) collective-permute-start(f32[24,256]{1,0:T(8,128)S(1)} %select_bitcast_fusion.2), channel_id=1, source_target_pairs={{0,16},{16,0},{1,17},{17,1},{2,18},{18,2},{3,19},{19,3},{4,20},{20... | collective-permute-start | bytes 73736 | tf_op jit(solution)/shard_map/ppermute | solution.py:165
  170.2 8.1 %all-to-all-done.4 = bf16[16,24,512]{2,1,0:T(8,128)(2,1)S(1)} async-done(((bf16[16,24,512]{2,1,0:T(8,128)(2,1)}), bf16[16,24,512]{2,1,0:T(8,128)(2,1)S(1)}, u32[]{:S(2)}, u32[]{:S(2)}) %all-to-all-start.4) | async-done | bytes 393248 | tf_op jit(solution)/shard_map/all_to_all | solution.py:162
  178.3 3.7 %all_gather.15 = bf16[16,48,512]{2,1,0:T(8,128)(2,1)S(1)} all-gather(bf16[16,24,512]{2,1,0:T(8,128)(2,1)S(1)} %all-to-all-done.4), channel_id=1, replica_groups=mesh['x'=4,'y'=4,'c'=2,'z'=8,'h'=2] {'c'}, dimensions={1}, use_global_device_ids=true | all-gather | bytes 1179648 | tf_op jit(solution)/shard_map/all_gather | solution.py:168
  183.0 7.3 %all_to_all.36 = f32[8,2,128]{2,1,0:T(2,128)S(1)} all-to-all(f32[8,2,128]{2,1,0:T(2,128)S(1)} %broadcast_in_dim.13), channel_id=1, replica_groups=mesh['x'=4,'y'=4,'c'=2,'z'=8,'h'=2] {'x','c'}, dimensions={0} | all-to-all | bytes 16384 | tf_op jit(solution)/shard_map/all_to_all | solution.py:122
  190.4 16.8 %all_to_all.37.sums_ref = f32[64,2,128]{2,1,0:T(2,128)S(1)} all-to-all(f32[64,2,128]{2,1,0:T(2,128)S(1)} %broadcast_in_dim.14), channel_id=1, replica_groups=mesh['x'=4,'y'=4,'c'=2,'z'=8,'h'=2] {'y','z','h'}, dimensions={0} | all-to-all | bytes 131072 | tf_op jit(solution)/shard_map/all_to_all | solution.py:122
  207.2 1.5 shard_map.78
  (36 shorter events, 7.4 us)
Async XLA Ops:
  7.2 86.0 %all-gather.3.cloned.1.call-start = ((), (), s32[]{:S(2)}) async-start(), calls=%async_computation.7 | async-start | bytes 8650752 | tf_op jit(solution)/shard_map/all_gather | solution.py:139
  18.4 10.2 %copy-start.3 = (f32[48,256]{1,0:T(8,128)S(1)}, f32[48,256]{1,0:T(8,128)}, u32[]{:S(2)}) copy-start(f32[48,256]{1,0:T(8,128)} %param.9) | copy-start | bytes 147460
  18.4 10.2 %copy-start.4 = (f32[48,256]{1,0:T(8,128)S(1)}, f32[48,256]{1,0:T(8,128)}, u32[]{:S(2)}) copy-start(f32[48,256]{1,0:T(8,128)} %param.8) | copy-start | bytes 147460
  18.4 15.1 %copy-start.2 = (f32[896,512]{1,0:T(8,128)S(1)}, f32[896,512]{1,0:T(8,128)}, u32[]{:S(2)}) copy-start(f32[896,512]{1,0:T(8,128)} %param.5) | copy-start | bytes 5505028
  18.4 46.3 %all-to-all-start = ((bf16[8,96,896]{2,1,0:T(8,128)(2,1)}), bf16[8,96,896]{2,1,0:T(8,128)(2,1)S(1)}, u32[]{:S(2)}, u32[]{:S(2)}) async-start(bf16[8,96,896]{2,1,0:T(8,128)(2,1)} %broadcast_in_dim.10), calls=%async_computation | async-start | bytes 2752512 | tf_op jit(solution)/shard_map/all_to_all | solution.py:122
  28.6 5.8 %collective-permute-start = (f32[2,24,256]{2,1,0:T(8,128)S(1)}, f32[2,24,256]{2,1,0:T(8,128)S(1)}, u32[]{:S(2)}, u32[]{:S(2)}) collective-permute-start(f32[2,24,256]{2,1,0:T(8,128)S(1)} %broadcast_select_fusion), channel_id=1, source_target_pairs={{0,16},{16,0},{1,17},{17,1},{2,18},{18,2},{3,19},{19,3},{4,20},{20... | collective-permute-start | bytes 147464 | tf_op jit(solution)/shard_map/ppermute | solution.py:143
  65.8 3.8 %collective-permute-start.1 = (bf16[16,24,512]{2,1,0:T(8,128)(2,1)S(1)}, bf16[16,24,512]{2,1,0:T(8,128)(2,1)S(1)}, u32[]{:S(2)}, u32[]{:S(2)}) collective-permute-start(bf16[16,24,512]{2,1,0:T(8,128)(2,1)S(1)} %fusion.5), channel_id=1, source_target_pairs={{0,16},{16,0},{1,17},{17,1},{2,18},{18,2},{3,19},{19,3},{4,20},{20... | collective-permute-start | bytes 1179656 | tf_op jit(solution)/shard_map/ppermute | solution.py:153
  70.6 22.5 %all-to-all-start.1 = ((bf16[16,24,512]{2,1,0:T(8,128)(2,1)}), bf16[16,24,512]{2,1,0:T(8,128)(2,1)S(1)}, u32[]{:S(2)}, u32[]{:S(2)}) async-start(bf16[16,24,512]{2,1,0:T(8,128)(2,1)} %fusion.4), calls=%async_computation.1 | async-start | bytes 786432 | tf_op jit(solution)/shard_map/all_to_all | solution.py:126
  79.4 13.8 %collective-permute-start.2 = (f32[2,2,24,256]{3,2,1,0:T(8,128)S(1)}, f32[2,2,24,256]{3,2,1,0:T(8,128)S(1)}, u32[]{:S(2)}, u32[]{:S(2)}) collective-permute-start(f32[2,2,24,256]{3,2,1,0:T(8,128)S(1)} %pad_maximum_fusion), channel_id=1, source_target_pairs={{0,0},{1,32},{2,64},{3,96},{4,128},{5,160},{6,192},{7,224},{8,256}... | collective-permute-start | bytes 294920 | tf_op jit(solution)/shard_map/ppermute | solution.py:149
  93.2 3.4 %copy-start = (bf16[16384,256]{1,0:T(8,128)(2,1)S(1)}, bf16[16384,256]{1,0:T(8,128)(2,1)}, u32[]{:S(2)}) copy-start(bf16[16384,256]{1,0:T(8,128)(2,1)} %all-gather.3.cloned.1.call-done) | copy-start | bytes 25165828
  126.6 22.0 %all-to-all-start.3 = ((bf16[16,2,24,256]{3,2,1,0:T(8,128)(2,1)}), bf16[16,2,24,256]{3,2,1,0:T(8,128)(2,1)S(1)}, u32[]{:S(2)}, u32[]{:S(2)}) async-start(bf16[16,2,24,256]{3,2,1,0:T(8,128)(2,1)} %broadcast_in_dim.12), calls=%async_computation.3 | async-start | bytes 786432 | tf_op jit(solution)/shard_map/all_to_all | solution.py:122
  134.8 30.6 %collective-permute-start.3 = (f32[2,24,256]{2,1,0:T(8,128)S(1)}, f32[2,24,256]{2,1,0:T(8,128)S(1)}, u32[]{:S(2)}, u32[]{:S(2)}) collective-permute-start(f32[2,24,256]{2,1,0:T(8,128)S(1)} %bitcast.52), channel_id=1, source_target_pairs={{0,0},{1,32},{2,64},{3,96},{4,128},{5,160},{6,192},{7,224},{8,256}... | collective-permute-start | bytes 147464 | tf_op jit(solution)/shard_map/ppermute | solution.py:163
  148.6 3.4 %copy-start.1 = (bf16[16384,256]{1,0:T(8,128)(2,1)S(1)}, bf16[16384,256]{1,0:T(8,128)(2,1)}, u32[]{:S(2)}) copy-start(bf16[16384,256]{1,0:T(8,128)(2,1)} %all-gather.3.cloned.1.call-done) | copy-start | bytes 25165828
  156.0 22.3 %all-to-all-start.4 = ((bf16[16,24,512]{2,1,0:T(8,128)(2,1)}), bf16[16,24,512]{2,1,0:T(8,128)(2,1)S(1)}, u32[]{:S(2)}, u32[]{:S(2)}) async-start(bf16[16,24,512]{2,1,0:T(8,128)(2,1)} %shard_map.77), calls=%async_computation.4 | async-start | bytes 786432 | tf_op jit(solution)/shard_map/all_to_all | solution.py:162
  165.4 4.1 %collective-permute-start.4 = (f32[24,256]{1,0:T(8,128)S(1)}, f32[24,256]{1,0:T(8,128)S(1)}, u32[]{:S(2)}, u32[]{:S(2)}) collective-permute-start(f32[24,256]{1,0:T(8,128)S(1)} %select_bitcast_fusion.2), channel_id=1, source_target_pairs={{0,16},{16,0},{1,17},{17,1},{2,18},{18,2},{3,19},{19,3},{4,20},{20... | collective-permute-start | bytes 73736 | tf_op jit(solution)/shard_map/ppermute | solution.py:165
Sparse Core Ops, SparseCore 0:
  10.1 79.8 all-gather.2

commit v10 on v9

--- a/solution.py
+++ b/solution.py
@@ -66,7 +66,7 @@
         out_specs=pl.BlockSpec(memory_space=pltpu.VMEM),
         out_shape=jax.ShapeDtypeStruct(shape, bf16),
         scratch_shapes=[pltpu.VMEM(basis.shape, bf16), pltpu.SemaphoreType.DMA((PIECES,))],
-        compiler_params=pltpu.CompilerParams(vmem_limit_bytes=24 * 2**20),
+        compiler_params=pltpu.CompilerParams(vmem_limit_bytes=57 * 2**20),
         cost_estimate=pl.CostEstimate(
             flops=48 * basis.size, bytes_accessed=2 * basis.size, transcendentals=0
         ),

time: 216 us -> 215 us (level)
  local copies, waits for them, and re-layouts: 8.75 us -> 2.74 us
  Pallas kernels: 8.42 us -> 12.4 us
    unnamed x10 -> x8, local copies, waits for them, and re-layouts: 6.77 us -> 0.76 us
    pallas_call x2, Pallas kernels: 6.94 us -> 11 us  [with_basis(): pl.pallas_call(kernel, in_specs=[pl.BlockSpec(memory_space=pltpu.VMEM), p...]
  transfers between devices with their start and end apart: 10 -> 10, of which waited for: 7 -> 7; matrix products, arithmetic and copies ran while one was open for 2% -> 2% of each run, Pallas kernels for 2% -> 3%
where the time goes in v10:
time: 215 us; the launch traced here: 214 us
  waiting for transfers between devices  68.1 us (32%)
  blocking collectives  62.9 us (29%)
  starting transfers between devices  48.6 us (23%)
  between operations  14.2 us (7%)
  Pallas kernels  12.4 us (6%)
  other arithmetic  2.77 us (1%)
  local copies, waits for them, and re-layouts  2.74 us (1%)
    all_to_all x2, waiting for transfers between devices, spread(): return lax.all_to_all(copies, axes, 0, 0, tiled=True)  43.5 us
    all_to_all x1, blocking collectives, collect(): got = lax.all_to_all(parts, axes, 0, 0, tiled=True)  25.9 us
    all_to_all x2, blocking collectives, spread(): return lax.all_to_all(copies, axes, 0, 0, tiled=True)  24 us
    all_to_all x2, starting transfers between devices, spread(): return lax.all_to_all(copies, axes, 0, 0, tiled=True)  18.3 us
    all_to_all x1, waiting for transfers between devices, collect(): got = lax.all_to_all(parts, axes, 0, 0, tiled=True)  13.1 us
    pallas_call x2, Pallas kernels, with_basis(): pl.pallas_call(kernel, in_specs=[pl.BlockSpec(memory_space=pltpu.VMEM), p...  11 us
    all_to_all x1, starting transfers between devices, body(): half = lax.all_to_all(returned, ('x', 'y'), 0, 0, tiled=True)  9.5 us
    all_gather x1, blocking collectives, body(): panels = spread(lax.all_gather(left_basis, 'h', tiled=True), 'z', 8)  9.28 us
  transfers between devices with their start and end apart: 10, of which 7 were waited for; matrix products, arithmetic and copies ran while one was open for 2% of the time, Pallas kernels for 3%

profile of v10, /device:TPU:1, one launch (start us, length us, event | category | flops | bytes accessed | tf_op | source)
XLA Modules:
  0.0 213.7 jit_solution(17498535866279640153)
XLA Ops:
  7.9 9.3 %all_gather.12 = bf16[96,896]{1,0:T(8,128)(2,1)S(1)} all-gather(bf16[48,896]{1,0:T(8,128)(2,1)} %param.6), channel_id=1, replica_groups=mesh['x'=4,'y'=4,'c'=2,'z'=8,'h'=2] {'h'}, dimensions={0}, use_global_device_ids=true | all-gather | bytes 258048 | tf_op jit(solution)/shard_map/all_gather | solution.py:147
  17.2 1.2 broadcast_in_dim.10
  18.4 10.2 %all-to-all-start = ((bf16[8,96,896]{2,1,0:T(8,128)(2,1)}), bf16[8,96,896]{2,1,0:T(8,128)(2,1)S(1)}, u32[]{:S(2)}, u32[]{:S(2)}) async-start(bf16[8,96,896]{2,1,0:T(8,128)(2,1)} %broadcast_in_dim.10), calls=%async_computation | async-start | bytes 2752512 | tf_op jit(solution)/shard_map/all_to_all | solution.py:122
  28.6 4.9 %collective-permute-start = (f32[2,24,256]{2,1,0:T(8,128)S(1)}, f32[2,24,256]{2,1,0:T(8,128)S(1)}, u32[]{:S(2)}, u32[]{:S(2)}) collective-permute-start(f32[2,24,256]{2,1,0:T(8,128)S(1)} %broadcast_select_fusion), channel_id=1, source_target_pairs={{0,16},{16,0},{1,17},{17,1},{2,18},{18,2},{3,19},{19,3},{4,20},{20... | collective-permute-start | bytes 147464 | tf_op jit(solution)/shard_map/ppermute | solution.py:143
  34.4 30.3 %all-to-all-done = bf16[8,96,896]{2,1,0:T(8,128)(2,1)S(1)} async-done(((bf16[8,96,896]{2,1,0:T(8,128)(2,1)}), bf16[8,96,896]{2,1,0:T(8,128)(2,1)S(1)}, u32[]{:S(2)}, u32[]{:S(2)}) %all-to-all-start) | async-done | bytes 1376288 | tf_op jit(solution)/shard_map/all_to_all | solution.py:122
  64.7 1.0 fusion
  65.8 2.5 %collective-permute-start.1 = (bf16[16,24,512]{2,1,0:T(8,128)(2,1)S(1)}, bf16[16,24,512]{2,1,0:T(8,128)(2,1)S(1)}, u32[]{:S(2)}, u32[]{:S(2)}) collective-permute-start(bf16[16,24,512]{2,1,0:T(8,128)(2,1)S(1)} %fusion.5), channel_id=1, source_target_pairs={{0,16},{16,0},{1,17},{17,1},{2,18},{18,2},{3,19},{19,3},{4,20},{20... | collective-permute-start | bytes 1179656 | tf_op jit(solution)/shard_map/ppermute | solution.py:153
  68.2 1.3 collective-permute-done.1
  69.6 1.0 fusion.4
  70.6 8.8 %all-to-all-start.1 = ((bf16[16,24,512]{2,1,0:T(8,128)(2,1)}), bf16[16,24,512]{2,1,0:T(8,128)(2,1)S(1)}, u32[]{:S(2)}, u32[]{:S(2)}) async-start(bf16[16,24,512]{2,1,0:T(8,128)(2,1)} %fusion.4), calls=%async_computation.1 | async-start | bytes 786432 | tf_op jit(solution)/shard_map/all_to_all | solution.py:126
  80.0 13.1 %all-to-all-done.1 = bf16[16,24,512]{2,1,0:T(8,128)(2,1)S(1)} async-done(((bf16[16,24,512]{2,1,0:T(8,128)(2,1)}), bf16[16,24,512]{2,1,0:T(8,128)(2,1)S(1)}, u32[]{:S(2)}, u32[]{:S(2)}) %all-to-all-start.1) | async-done | bytes 393248 | tf_op jit(solution)/shard_map/all_to_all | solution.py:126
  93.8 5.2 %shard_map.76 = bf16[32,24,256]{2,1,0:T(8,128)(2,1)} custom-call(bf16[24,512]{1,0:T(8,128)(2,1)} %fusion.14.rows_ref, bf16[32,512,256]{2,1,0:T(8,128)(2,1)} %bitcast.41), custom_call_target="tpu_custom_call" | custom-call | flops 201326592 | bytes 8388608 | tf_op jit(solution)/shard_map/pallas_call | solution.py:63
  99.0 25.9 %all_to_all.35 = bf16[16,2,24,256]{3,2,1,0:T(8,128)(2,1)S(1)} all-to-all(bf16[16,2,24,256]{3,2,1,0:T(8,128)(2,1)} %bitcast.46), channel_id=1, replica_groups=mesh['x'=4,'y'=4,'c'=2,'z'=8,'h'=2] {'z','h'}, dimensions={0} | all-to-all | bytes 786432 | tf_op jit(solution)/shard_map/all_to_all | solution.py:126
  125.8 8.1 %all-to-all-start.3 = ((bf16[16,2,24,256]{3,2,1,0:T(8,128)(2,1)}), bf16[16,2,24,256]{3,2,1,0:T(8,128)(2,1)S(1)}, u32[]{:S(2)}, u32[]{:S(2)}) async-start(bf16[16,2,24,256]{3,2,1,0:T(8,128)(2,1)} %broadcast_in_dim.12), calls=%async_computation.3 | async-start | bytes 786432 | tf_op jit(solution)/shard_map/all_to_all | solution.py:122
  134.6 13.2 %all-to-all-done.3 = bf16[16,2,24,256]{3,2,1,0:T(8,128)(2,1)S(1)} async-done(((bf16[16,2,24,256]{3,2,1,0:T(8,128)(2,1)}), bf16[16,2,24,256]{3,2,1,0:T(8,128)(2,1)S(1)}, u32[]{:S(2)}, u32[]{:S(2)}) %all-to-all-start.3) | async-done | bytes 393248 | tf_op jit(solution)/shard_map/all_to_all | solution.py:122
  148.5 5.7 %shard_map.77 = bf16[16,24,512]{2,1,0:T(8,128)(2,1)} custom-call(bf16[32,24,256]{2,1,0:T(8,128)(2,1)} %bitcast.45, bf16[32,512,256]{2,1,0:T(8,128)(2,1)} %bitcast.42), custom_call_target="tpu_custom_call" | custom-call | flops 201326592 | bytes 8388608 | tf_op jit(solution)/shard_map/pallas_call | solution.py:63
  154.2 9.5 %all-to-all-start.4 = ((bf16[16,24,512]{2,1,0:T(8,128)(2,1)}), bf16[16,24,512]{2,1,0:T(8,128)(2,1)S(1)}, u32[]{:S(2)}, u32[]{:S(2)}) async-start(bf16[16,24,512]{2,1,0:T(8,128)(2,1)} %shard_map.77), calls=%async_computation.4 | async-start | bytes 786432 | tf_op jit(solution)/shard_map/all_to_all | solution.py:162
  163.7 3.3 %collective-permute-start.4 = (f32[24,256]{1,0:T(8,128)S(1)}, f32[24,256]{1,0:T(8,128)S(1)}, u32[]{:S(2)}, u32[]{:S(2)}) collective-permute-start(f32[24,256]{1,0:T(8,128)S(1)} %select_bitcast_fusion.2), channel_id=1, source_target_pairs={{0,16},{16,0},{1,17},{17,1},{2,18},{18,2},{3,19},{19,3},{4,20},{20... | collective-permute-start | bytes 73736 | tf_op jit(solution)/shard_map/ppermute | solution.py:165
  168.5 8.1 %all-to-all-done.4 = bf16[16,24,512]{2,1,0:T(8,128)(2,1)S(1)} async-done(((bf16[16,24,512]{2,1,0:T(8,128)(2,1)}), bf16[16,24,512]{2,1,0:T(8,128)(2,1)S(1)}, u32[]{:S(2)}, u32[]{:S(2)}) %all-to-all-start.4) | async-done | bytes 393248 | tf_op jit(solution)/shard_map/all_to_all | solution.py:162
  176.6 3.7 %all_gather.15 = bf16[16,48,512]{2,1,0:T(8,128)(2,1)S(1)} all-gather(bf16[16,24,512]{2,1,0:T(8,128)(2,1)S(1)} %all-to-all-done.4), channel_id=1, replica_groups=mesh['x'=4,'y'=4,'c'=2,'z'=8,'h'=2] {'c'}, dimensions={1}, use_global_device_ids=true | all-gather | bytes 1179648 | tf_op jit(solution)/shard_map/all_gather | solution.py:168
  180.3 0.9 multiply_reduce_fusion
  181.3 7.3 %all_to_all.36 = f32[8,2,128]{2,1,0:T(2,128)S(1)} all-to-all(f32[8,2,128]{2,1,0:T(2,128)S(1)} %broadcast_in_dim.13), channel_id=1, replica_groups=mesh['x'=4,'y'=4,'c'=2,'z'=8,'h'=2] {'x','c'}, dimensions={0} | all-to-all | bytes 16384 | tf_op jit(solution)/shard_map/all_to_all | solution.py:122
  188.7 16.7 %all_to_all.37.sums_ref = f32[64,2,128]{2,1,0:T(2,128)S(1)} all-to-all(f32[64,2,128]{2,1,0:T(2,128)S(1)} %broadcast_in_dim.14), channel_id=1, replica_groups=mesh['x'=4,'y'=4,'c'=2,'z'=8,'h'=2] {'y','z','h'}, dimensions={0} | all-to-all | bytes 131072 | tf_op jit(solution)/shard_map/all_to_all | solution.py:122
  205.4 1.5 shard_map.78
  (34 shorter events, 6.9 us)
Async XLA Ops:
  7.2 86.6 %all-gather.3.cloned.1.call-start = ((), (), s32[]{:S(2)}) async-start(), calls=%async_computation.7 | async-start | bytes 8650752 | tf_op jit(solution)/shard_map/all_gather | solution.py:139
  18.4 10.2 %copy-start.2 = (f32[48,256]{1,0:T(8,128)S(1)}, f32[48,256]{1,0:T(8,128)}, u32[]{:S(2)}) copy-start(f32[48,256]{1,0:T(8,128)} %param.9) | copy-start | bytes 147460
  18.4 10.2 %copy-start.3 = (f32[48,256]{1,0:T(8,128)S(1)}, f32[48,256]{1,0:T(8,128)}, u32[]{:S(2)}) copy-start(f32[48,256]{1,0:T(8,128)} %param.8) | copy-start | bytes 147460
  18.4 15.1 %copy-start = (f32[896,512]{1,0:T(8,128)S(1)}, f32[896,512]{1,0:T(8,128)}, u32[]{:S(2)}) copy-start(f32[896,512]{1,0:T(8,128)} %param.5) | copy-start | bytes 5505028
  18.4 46.3 %all-to-all-start = ((bf16[8,96,896]{2,1,0:T(8,128)(2,1)}), bf16[8,96,896]{2,1,0:T(8,128)(2,1)S(1)}, u32[]{:S(2)}, u32[]{:S(2)}) async-start(bf16[8,96,896]{2,1,0:T(8,128)(2,1)} %broadcast_in_dim.10), calls=%async_computation | async-start | bytes 2752512 | tf_op jit(solution)/shard_map/all_to_all | solution.py:122
  28.6 5.8 %collective-permute-start = (f32[2,24,256]{2,1,0:T(8,128)S(1)}, f32[2,24,256]{2,1,0:T(8,128)S(1)}, u32[]{:S(2)}, u32[]{:S(2)}) collective-permute-start(f32[2,24,256]{2,1,0:T(8,128)S(1)} %broadcast_select_fusion), channel_id=1, source_target_pairs={{0,16},{16,0},{1,17},{17,1},{2,18},{18,2},{3,19},{19,3},{4,20},{20... | collective-permute-start | bytes 147464 | tf_op jit(solution)/shard_map/ppermute | solution.py:143
  65.8 3.8 %collective-permute-start.1 = (bf16[16,24,512]{2,1,0:T(8,128)(2,1)S(1)}, bf16[16,24,512]{2,1,0:T(8,128)(2,1)S(1)}, u32[]{:S(2)}, u32[]{:S(2)}) collective-permute-start(bf16[16,24,512]{2,1,0:T(8,128)(2,1)S(1)} %fusion.5), channel_id=1, source_target_pairs={{0,16},{16,0},{1,17},{17,1},{2,18},{18,2},{3,19},{19,3},{4,20},{20... | collective-permute-start | bytes 1179656 | tf_op jit(solution)/shard_map/ppermute | solution.py:153
  70.6 22.5 %all-to-all-start.1 = ((bf16[16,24,512]{2,1,0:T(8,128)(2,1)}), bf16[16,24,512]{2,1,0:T(8,128)(2,1)S(1)}, u32[]{:S(2)}, u32[]{:S(2)}) async-start(bf16[16,24,512]{2,1,0:T(8,128)(2,1)} %fusion.4), calls=%async_computation.1 | async-start | bytes 786432 | tf_op jit(solution)/shard_map/all_to_all | solution.py:126
  79.4 14.4 %collective-permute-start.2 = (f32[2,2,24,256]{3,2,1,0:T(8,128)S(1)}, f32[2,2,24,256]{3,2,1,0:T(8,128)S(1)}, u32[]{:S(2)}, u32[]{:S(2)}) collective-permute-start(f32[2,2,24,256]{3,2,1,0:T(8,128)S(1)} %pad_maximum_fusion), channel_id=1, source_target_pairs={{0,0},{1,32},{2,64},{3,96},{4,128},{5,160},{6,192},{7,224},{8,256}... | collective-permute-start | bytes 294920 | tf_op jit(solution)/shard_map/ppermute | solution.py:149
  125.8 22.0 %all-to-all-start.3 = ((bf16[16,2,24,256]{3,2,1,0:T(8,128)(2,1)}), bf16[16,2,24,256]{3,2,1,0:T(8,128)(2,1)S(1)}, u32[]{:S(2)}, u32[]{:S(2)}) async-start(bf16[16,2,24,256]{3,2,1,0:T(8,128)(2,1)} %broadcast_in_dim.12), calls=%async_computation.3 | async-start | bytes 786432 | tf_op jit(solution)/shard_map/all_to_all | solution.py:122
  133.9 29.8 %collective-permute-start.3 = (f32[2,24,256]{2,1,0:T(8,128)S(1)}, f32[2,24,256]{2,1,0:T(8,128)S(1)}, u32[]{:S(2)}, u32[]{:S(2)}) collective-permute-start(f32[2,24,256]{2,1,0:T(8,128)S(1)} %bitcast.52), channel_id=1, source_target_pairs={{0,0},{1,32},{2,64},{3,96},{4,128},{5,160},{6,192},{7,224},{8,256}... | collective-permute-start | bytes 147464 | tf_op jit(solution)/shard_map/ppermute | solution.py:163
  147.7 0.7 copy-start.1
  154.2 22.4 %all-to-all-start.4 = ((bf16[16,24,512]{2,1,0:T(8,128)(2,1)}), bf16[16,24,512]{2,1,0:T(8,128)(2,1)S(1)}, u32[]{:S(2)}, u32[]{:S(2)}) async-start(bf16[16,24,512]{2,1,0:T(8,128)(2,1)} %shard_map.77), calls=%async_computation.4 | async-start | bytes 786432 | tf_op jit(solution)/shard_map/all_to_all | solution.py:162
  163.7 4.1 %collective-permute-start.4 = (f32[24,256]{1,0:T(8,128)S(1)}, f32[24,256]{1,0:T(8,128)S(1)}, u32[]{:S(2)}, u32[]{:S(2)}) collective-permute-start(f32[24,256]{1,0:T(8,128)S(1)} %select_bitcast_fusion.2), channel_id=1, source_target_pairs={{0,16},{16,0},{1,17},{17,1},{2,18},{18,2},{3,19},{19,3},{4,20},{20... | collective-permute-start | bytes 73736 | tf_op jit(solution)/shard_map/ppermute | solution.py:165
Sparse Core Ops, SparseCore 0:
  10.1 79.8 all-gather.2

commit v11 on v8

--- a/solution.py
+++ b/solution.py
@@ -109,18 +109,19 @@
     )
 
     half = spread(returned.astype(bf16), ("x", "y"), 16)
-    rotated = lax.ppermute(rotated, ("x", "y", "z", "h"), TURN)
     keep, send = sort(rotated[0], rotated[1])
     rotated = jnp.concatenate(sort(keep, lax.ppermute(send, "c", SWAP)))
-    new_moment, new_variance, _ = adam(moment, variance, rotated)
-    half, new_moment, new_variance = lax.optimization_barrier((half, new_moment, new_variance))
+    half, rotated = lax.optimization_barrier((half, rotated))
     returned = lax.all_gather(half, "c", axis=1, tiled=True).reshape(768, 512)
     unscaled = lax.dot_general(
         panels, returned, (((0,), (0,)), ((), ())), preferred_element_type=f32
     )
     sums = jnp.stack([grad_lanes, lanes(unscaled)])
     sums = jnp.sum(spread(sums, ("x", "c"), 8), axis=0)
-    update = scale(spread(sums, ("y", "z", "h"), 64), unscaled)
+    sums, rotated = lax.optimization_barrier((spread(sums, ("y", "z", "h"), 64), rotated))
+    rotated = lax.ppermute(rotated, ("x", "y", "z", "h"), TURN)
+    update = scale(sums, unscaled)
+    new_moment, new_variance, _ = adam(moment, variance, rotated)
     return (update, new_moment, new_variance)
 
 

time: 214 us -> 221 us (1.033)
  the two profiles are of different devices: /device:TPU:1 before, /device:TPU:12 now
where the time goes in v11:
time: 221 us
  blocking collectives  84.1 us (38%)
  waiting for transfers between devices  67.1 us (30%)
  starting transfers between devices  40.6 us (18%)
  between operations  14.2 us (6%)
  matrix products  8.96 us (4%)
    all_to_all x3, blocking collectives, spread(): return lax.all_to_all(copies, axes, 0, 0, tiled=True)  46.9 us
    all_to_all x2, waiting for transfers between devices, spread(): return lax.all_to_all(copies, axes, 0, 0, tiled=True)  38.4 us
    all_to_all x1, blocking collectives, collect(): got = lax.all_to_all(parts, axes, 0, 0, tiled=True)  25.6 us
    all_to_all x2, starting transfers between devices, spread(): return lax.all_to_all(copies, axes, 0, 0, tiled=True)  16.2 us
    ppermute x1, waiting for transfers between devices, body(): rotated = lax.ppermute(rotated, ('x', 'y', 'z', 'h'), TURN)  10.2 us
    all_to_all x1, starting transfers between devices, collect(): got = lax.all_to_all(parts, axes, 0, 0, tiled=True)  9.58 us
    all_gather x1, blocking collectives, body(): panels = spread(lax.all_gather(left_basis, 'h', tiled=True), 'z', 8)  9.3 us
    all_to_all x1, waiting for transfers between devices, collect(): got = lax.all_to_all(parts, axes, 0, 0, tiled=True)  8.74 us
  transfers between devices with their start and end apart: 9, of which 8 were waited for; matrix products, arithmetic and copies ran while one was open for 2% of the time, Pallas kernels for 1%

profile of v11, /device:TPU:12, one launch (start us, length us, event | category | flops | bytes accessed | tf_op | source)
XLA Modules:
  0.0 220.7 jit_solution(8274830230101133347)
XLA Ops:
  7.9 9.3 %all_gather.12 = bf16[96,896]{1,0:T(8,128)(2,1)S(1)} all-gather(bf16[48,896]{1,0:T(8,128)(2,1)} %param.6), channel_id=1, replica_groups=mesh['x'=4,'y'=4,'c'=2,'z'=8,'h'=2] {'h'}, dimensions={0}, use_global_device_ids=true | all-gather | bytes 258048 | tf_op jit(solution)/shard_map/all_gather | solution.py:93
  17.2 1.2 broadcast_in_dim.12
  18.4 10.4 %all-to-all-start = ((bf16[8,96,896]{2,1,0:T(8,128)(2,1)}), bf16[8,96,896]{2,1,0:T(8,128)(2,1)S(1)}, u32[]{:S(2)}, u32[]{:S(2)}) async-start(bf16[8,96,896]{2,1,0:T(8,128)(2,1)} %broadcast_in_dim.12), calls=%async_computation | async-start | bytes 2752512 | tf_op jit(solution)/shard_map/all_to_all | solution.py:68
  28.9 1.9 collective-permute-start
  32.0 31.5 %all-to-all-done = bf16[8,96,896]{2,1,0:T(8,128)(2,1)S(1)} async-done(((bf16[8,96,896]{2,1,0:T(8,128)(2,1)}), bf16[8,96,896]{2,1,0:T(8,128)(2,1)S(1)}, u32[]{:S(2)}, u32[]{:S(2)}) %all-to-all-start) | async-done | bytes 1376288 | tf_op jit(solution)/shard_map/all_to_all | solution.py:68
  64.6 1.9 collective-permute-start.1
  66.5 1.7 collective-permute-done.1
  69.2 9.6 %all-to-all-start.1 = ((bf16[16,24,512]{2,1,0:T(8,128)(2,1)}), bf16[16,24,512]{2,1,0:T(8,128)(2,1)S(1)}, u32[]{:S(2)}, u32[]{:S(2)}) async-start(bf16[16,24,512]{2,1,0:T(8,128)(2,1)} %fusion.6), calls=%async_computation.1 | async-start | bytes 786432 | tf_op jit(solution)/shard_map/all_to_all | solution.py:72
  78.8 4.5 %collective-permute-start.2 = (f32[2,2,24,256]{3,2,1,0:T(8,128)S(1)}, f32[2,2,24,256]{3,2,1,0:T(8,128)S(1)}, u32[]{:S(2)}, u32[]{:S(2)}) collective-permute-start(f32[2,2,24,256]{3,2,1,0:T(8,128)S(1)} %pad_maximum_fusion), channel_id=1, source_target_pairs={{0,0},{1,32},{2,64},{3,96},{4,128},{5,160},{6,192},{7,224},{8,256}... | collective-permute-start | bytes 294920 | tf_op jit(solution)/shard_map/ppermute | solution.py:95
  83.3 8.7 %all-to-all-done.1 = bf16[16,24,512]{2,1,0:T(8,128)(2,1)S(1)} async-done(((bf16[16,24,512]{2,1,0:T(8,128)(2,1)}), bf16[16,24,512]{2,1,0:T(8,128)(2,1)S(1)}, u32[]{:S(2)}, u32[]{:S(2)}) %all-to-all-start.1) | async-done | bytes 393248 | tf_op jit(solution)/shard_map/all_to_all | solution.py:72
  92.1 5.3 %collective-permute-done.2 = f32[2,2,24,256]{3,2,1,0:T(8,128)S(1)} collective-permute-done((f32[2,2,24,256]{3,2,1,0:T(8,128)S(1)}, f32[2,2,24,256]{3,2,1,0:T(8,128)S(1)}, u32[]{:S(2)}, u32[]{:S(2)}) %collective-permute-start.2) | collective-permute-done | bytes 98336 | tf_op jit(solution)/shard_map/ppermute | solution.py:95
  97.4 4.7 %convolution_convert_fusion = bf16[24,32,256]{2,0,1:T(8,128)(2,1)S(1)} fusion(bf16[32,512,256]{2,1,0:T(8,128)(2,1)} %bitcast.73, bf16[24,512]{1,0:T(8,128)(2,1)S(1)} %fusion.17), kind=kOutput, calls=%fused_computation.2 | convolution fusion | flops 201523200 | bytes 8806400 | tf_op jit(solution)/shard_map/rk,fkn->frn/dot_general | solution.py:103
  102.1 25.6 %all_to_all.35 = bf16[16,2,24,256]{3,2,1,0:T(8,128)(2,1)S(1)} all-to-all(bf16[16,2,24,256]{3,2,1,0:T(8,128)(2,1)S(1)} %bitcast.76), channel_id=1, replica_groups=mesh['x'=4,'y'=4,'c'=2,'z'=8,'h'=2] {'z','h'}, dimensions={0} | all-to-all | bytes 786432 | tf_op jit(solution)/shard_map/all_to_all | solution.py:72
  127.8 21.3 %all_to_all.36 = bf16[16,2,24,256]{3,2,1,0:T(8,128)(2,1)S(1)} all-to-all(bf16[16,2,24,256]{3,2,1,0:T(8,128)(2,1)S(1)} %broadcast_in_dim.14), channel_id=1, replica_groups=mesh['x'=4,'y'=4,'c'=2,'z'=8,'h'=2] {'z','h'}, dimensions={0} | all-to-all | bytes 786432 | tf_op jit(solution)/shard_map/all_to_all | solution.py:68
  149.1 2.3 %fusion = bf16[24,512]{1,0:T(8,128)(2,1)S(1)} fusion(bf16[32,24,256]{2,1,0:T(8,128)(2,1)S(1)} %bitcast.75, bf16[32,512,256]{2,1,0:T(8,128)(2,1)S(1)} %bitcast.74), kind=kOutput, calls=%fused_computation.4 | convolution fusion | flops 201338880 | bytes 8806400 | tf_op jit(solution)/shard_map/dot_general | solution.py:107
  152.2 5.8 %all-to-all-start.4 = ((bf16[16,24,512]{2,1,0:T(8,128)(2,1)}), bf16[16,24,512]{2,1,0:T(8,128)(2,1)S(1)}, u32[]{:S(2)}, u32[]{:S(2)}) async-start(bf16[16,24,512]{2,1,0:T(8,128)(2,1)} %broadcast_in_dim.15), calls=%async_computation.4 | async-start | bytes 786432 | tf_op jit(solution)/shard_map/all_to_all | solution.py:68
  158.0 1.9 collective-permute-start.3
  161.1 6.9 %all-to-all-done.4 = bf16[16,24,512]{2,1,0:T(8,128)(2,1)S(1)} async-done(((bf16[16,24,512]{2,1,0:T(8,128)(2,1)}), bf16[16,24,512]{2,1,0:T(8,128)(2,1)S(1)}, u32[]{:S(2)}, u32[]{:S(2)}) %all-to-all-start.4) | async-done | bytes 393248 | tf_op jit(solution)/shard_map/all_to_all | solution.py:68
  168.0 2.4 %all_gather.15 = bf16[16,48,512]{2,1,0:T(8,128)(2,1)S(1)} all-gather(bf16[16,24,512]{2,1,0:T(8,128)(2,1)S(1)} %all-to-all-done.4), channel_id=1, replica_groups=mesh['x'=4,'y'=4,'c'=2,'z'=8,'h'=2] {'c'}, dimensions={1}, use_global_device_ids=true | all-gather | bytes 1179648 | tf_op jit(solution)/shard_map/all_gather | solution.py:115
  171.3 7.5 %all_to_all.37 = f32[8,2,128]{2,1,0:T(2,128)S(1)} all-to-all(f32[8,2,128]{2,1,0:T(2,128)S(1)} %broadcast_in_dim.16), channel_id=1, replica_groups=mesh['x'=4,'y'=4,'c'=2,'z'=8,'h'=2] {'x','c'}, dimensions={0} | all-to-all | bytes 16384 | tf_op jit(solution)/shard_map/all_to_all | solution.py:68
  178.9 18.1 %all_to_all.38.sums_ref = f32[64,2,128]{2,1,0:T(2,128)S(1)} all-to-all(f32[64,2,128]{2,1,0:T(2,128)S(1)} %broadcast_in_dim.17), channel_id=1, replica_groups=mesh['x'=4,'y'=4,'c'=2,'z'=8,'h'=2] {'y','z','h'}, dimensions={0} | all-to-all | bytes 131072 | tf_op jit(solution)/shard_map/all_to_all | solution.py:68
  197.0 4.5 %collective-permute-start.4 = (f32[48,256]{1,0:T(8,128)S(1)}, f32[48,256]{1,0:T(8,128)S(1)}, u32[]{:S(2)}, u32[]{:S(2)}) collective-permute-start(f32[48,256]{1,0:T(8,128)S(1)} %pad_maximum_fusion.2), channel_id=1, source_target_pairs={{0,0},{1,32},{2,64},{3,96},{4,128},{5,160},{6,192},{7,224},{8,256}... | collective-permute-start | bytes 147464 | tf_op jit(solution)/shard_map/ppermute | solution.py:122
  201.5 1.5 shard_map.76
  203.0 10.2 %collective-permute-done.4 = f32[48,256]{1,0:T(8,128)S(1)} collective-permute-done((f32[48,256]{1,0:T(8,128)S(1)}, f32[48,256]{1,0:T(8,128)S(1)}, u32[]{:S(2)}, u32[]{:S(2)}) %collective-permute-start.4) | collective-permute-done | bytes 49184 | tf_op jit(solution)/shard_map/ppermute | solution.py:122
  (35 shorter events, 7.8 us)
Async XLA Ops:
  7.2 90.2 %all-gather.3.cloned.1.call-start = ((), (), s32[]{:S(2)}) async-start(), calls=%async_computation.7 | async-start | bytes 8650752 | tf_op jit(solution)/shard_map/all_gather | solution.py:85
  17.2 11.6 %copy-start.2 = (f32[48,256]{1,0:T(8,128)S(1)}, f32[48,256]{1,0:T(8,128)}, u32[]{:S(2)}) copy-start(f32[48,256]{1,0:T(8,128)} %param.9) | copy-start | bytes 147460
  17.2 11.6 %copy-start.3 = (f32[48,256]{1,0:T(8,128)S(1)}, f32[48,256]{1,0:T(8,128)}, u32[]{:S(2)}) copy-start(f32[48,256]{1,0:T(8,128)} %param.8) | copy-start | bytes 147460
  18.4 12.4 %copy-start.1 = (f32[896,512]{1,0:T(8,128)S(1)}, f32[896,512]{1,0:T(8,128)}, u32[]{:S(2)}) copy-start(f32[896,512]{1,0:T(8,128)} %param.5) | copy-start | bytes 5505028
  18.4 45.1 %all-to-all-start = ((bf16[8,96,896]{2,1,0:T(8,128)(2,1)}), bf16[8,96,896]{2,1,0:T(8,128)(2,1)S(1)}, u32[]{:S(2)}, u32[]{:S(2)}) async-start(bf16[8,96,896]{2,1,0:T(8,128)(2,1)} %broadcast_in_dim.12), calls=%async_computation | async-start | bytes 2752512 | tf_op jit(solution)/shard_map/all_to_all | solution.py:68
  28.9 3.1 %collective-permute-start = (f32[2,24,256]{2,1,0:T(8,128)S(1)}, f32[2,24,256]{2,1,0:T(8,128)S(1)}, u32[]{:S(2)}, u32[]{:S(2)}) collective-permute-start(f32[2,24,256]{2,1,0:T(8,128)S(1)} %broadcast_select_fusion), channel_id=1, source_target_pairs={{0,16},{16,0},{1,17},{17,1},{2,18},{18,2},{3,19},{19,3},{4,20},{20... | collective-permute-start | bytes 147464 | tf_op jit(solution)/shard_map/ppermute | solution.py:89
  64.6 3.6 %collective-permute-start.1 = (bf16[16,24,512]{2,1,0:T(8,128)(2,1)S(1)}, bf16[16,24,512]{2,1,0:T(8,128)(2,1)S(1)}, u32[]{:S(2)}, u32[]{:S(2)}) collective-permute-start(bf16[16,24,512]{2,1,0:T(8,128)(2,1)S(1)} %fusion.7), channel_id=1, source_target_pairs={{0,16},{16,0},{1,17},{17,1},{2,18},{18,2},{3,19},{19,3},{4,20},{20... | collective-permute-start | bytes 1179656 | tf_op jit(solution)/shard_map/ppermute | solution.py:99
  69.2 22.8 %all-to-all-start.1 = ((bf16[16,24,512]{2,1,0:T(8,128)(2,1)}), bf16[16,24,512]{2,1,0:T(8,128)(2,1)S(1)}, u32[]{:S(2)}, u32[]{:S(2)}) async-start(bf16[16,24,512]{2,1,0:T(8,128)(2,1)} %fusion.6), calls=%async_computation.1 | async-start | bytes 786432 | tf_op jit(solution)/shard_map/all_to_all | solution.py:72
  78.8 18.6 %collective-permute-start.2 = (f32[2,2,24,256]{3,2,1,0:T(8,128)S(1)}, f32[2,2,24,256]{3,2,1,0:T(8,128)S(1)}, u32[]{:S(2)}, u32[]{:S(2)}) collective-permute-start(f32[2,2,24,256]{3,2,1,0:T(8,128)S(1)} %pad_maximum_fusion), channel_id=1, source_target_pairs={{0,0},{1,32},{2,64},{3,96},{4,128},{5,160},{6,192},{7,224},{8,256}... | collective-permute-start | bytes 294920 | tf_op jit(solution)/shard_map/ppermute | solution.py:95
  97.4 51.7 %copy-start = (bf16[16384,256]{1,0:T(8,128)(2,1)S(1)}, bf16[16384,256]{1,0:T(8,128)(2,1)}, u32[]{:S(2)}) copy-start(bf16[16384,256]{1,0:T(8,128)(2,1)} %all-gather.3.cloned.1.call-done) | copy-start | bytes 25165828
  152.2 15.8 %all-to-all-start.4 = ((bf16[16,24,512]{2,1,0:T(8,128)(2,1)}), bf16[16,24,512]{2,1,0:T(8,128)(2,1)S(1)}, u32[]{:S(2)}, u32[]{:S(2)}) async-start(bf16[16,24,512]{2,1,0:T(8,128)(2,1)} %broadcast_in_dim.15), calls=%async_computation.4 | async-start | bytes 786432 | tf_op jit(solution)/shard_map/all_to_all | solution.py:68
  158.0 3.1 %collective-permute-start.3 = (f32[24,256]{1,0:T(8,128)S(1)}, f32[24,256]{1,0:T(8,128)S(1)}, u32[]{:S(2)}, u32[]{:S(2)}) collective-permute-start(f32[24,256]{1,0:T(8,128)S(1)} %select_bitcast_fusion.2), channel_id=1, source_target_pairs={{0,16},{16,0},{1,17},{17,1},{2,18},{18,2},{3,19},{19,3},{4,20},{20... | collective-permute-start | bytes 73736 | tf_op jit(solution)/shard_map/ppermute | solution.py:113
  197.0 16.2 %collective-permute-start.4 = (f32[48,256]{1,0:T(8,128)S(1)}, f32[48,256]{1,0:T(8,128)S(1)}, u32[]{:S(2)}, u32[]{:S(2)}) collective-permute-start(f32[48,256]{1,0:T(8,128)S(1)} %pad_maximum_fusion.2), channel_id=1, source_target_pairs={{0,0},{1,32},{2,64},{3,96},{4,128},{5,160},{6,192},{7,224},{8,256}... | collective-permute-start | bytes 147464 | tf_op jit(solution)/shard_map/ppermute | solution.py:122
Sparse Core Ops, SparseCore 0:
  10.1 76.0 all-gather.2

commit v12 on v8

--- a/solution.py
+++ b/solution.py
@@ -108,17 +108,18 @@
         direction, basis, (((0, 2), (0, 2)), ((), ())), preferred_element_type=f32
     )
 
-    half = spread(returned.astype(bf16), ("x", "y"), 16)
-    rotated = lax.ppermute(rotated, ("x", "y", "z", "h"), TURN)
+    returned, rotated = lax.optimization_barrier((returned.astype(bf16), rotated))
+    half = spread(returned, ("x", "y"), 16)
     keep, send = sort(rotated[0], rotated[1])
     rotated = jnp.concatenate(sort(keep, lax.ppermute(send, "c", SWAP)))
+    rotated = lax.ppermute(rotated, ("x", "y", "z", "h"), TURN)
     new_moment, new_variance, _ = adam(moment, variance, rotated)
-    half, new_moment, new_variance = lax.optimization_barrier((half, new_moment, new_variance))
     returned = lax.all_gather(half, "c", axis=1, tiled=True).reshape(768, 512)
     unscaled = lax.dot_general(
         panels, returned, (((0,), (0,)), ((), ())), preferred_element_type=f32
     )
     sums = jnp.stack([grad_lanes, lanes(unscaled)])
+    sums, new_moment, new_variance = lax.optimization_barrier((sums, new_moment, new_variance))
     sums = jnp.sum(spread(sums, ("x", "c"), 8), axis=0)
     update = scale(spread(sums, ("y", "z", "h"), 64), unscaled)
     return (update, new_moment, new_variance)

time: 214 us -> 218 us (1.019)
  blocking collectives: 63.2 us -> 94.3 us
  waiting for transfers between devices: 68 us -> 54.4 us
  starting transfers between devices: 48.9 us -> 40 us
  matrix products: 12.2 us -> 8.96 us
    all_to_all x2 -> x3, blocking collectives: 24 us -> 54.4 us  [spread(): return lax.all_to_all(copies, axes, 0, 0, tiled=True)]
    all_to_all x3 -> x2, waiting for transfers between devices: 51.4 us -> 37.9 us  [spread(): return lax.all_to_all(copies, axes, 0, 0, tiled=True)]
    all_to_all x3 -> x2, starting transfers between devices: 27.9 us -> 19.3 us  [spread(): return lax.all_to_all(copies, axes, 0, 0, tiled=True)]
    dot_general x1, matrix products: 5.68 us -> 2.3 us  [body(): lax.dot_general(direction, basis, (((0, 2), (0, 2)), ((), ())), preferred...]
  transfers between devices with their start and end apart: 10 -> 9, of which waited for: 7 -> 6; matrix products, arithmetic and copies ran while one was open for 5% -> 2% of each run, Pallas kernels for 0% -> 0%
where the time goes in v12:
time: 218 us
  blocking collectives  94.3 us (43%)
  waiting for transfers between devices  54.4 us (25%)
  starting transfers between devices  40 us (18%)
  between operations  14.2 us (7%)
  matrix products  8.96 us (4%)
    all_to_all x3, blocking collectives, spread(): return lax.all_to_all(copies, axes, 0, 0, tiled=True)  54.4 us
    all_to_all x2, waiting for transfers between devices, spread(): return lax.all_to_all(copies, axes, 0, 0, tiled=True)  37.9 us
    all_to_all x1, blocking collectives, collect(): got = lax.all_to_all(parts, axes, 0, 0, tiled=True)  26.4 us
    all_to_all x2, starting transfers between devices, spread(): return lax.all_to_all(copies, axes, 0, 0, tiled=True)  19.3 us
    all_to_all x1, waiting for transfers between devices, collect(): got = lax.all_to_all(parts, axes, 0, 0, tiled=True)  13.1 us
    all_gather x1, blocking collectives, body(): panels = spread(lax.all_gather(left_basis, 'h', tiled=True), 'z', 8)  9.28 us
    all_to_all x1, starting transfers between devices, collect(): got = lax.all_to_all(parts, axes, 0, 0, tiled=True)  8.79 us
    ppermute x1, starting transfers between devices, body(): blocks = sort(keep, lax.ppermute(send, 'c', SWAP))  4.91 us
  transfers between devices with their start and end apart: 9, of which 6 were waited for; matrix products, arithmetic and copies ran while one was open for 2% of the time, Pallas kernels for 0%

profile of v12, /device:TPU:1, one launch (start us, length us, event | category | flops | bytes accessed | tf_op | source)
XLA Modules:
  0.0 217.6 jit_solution(7244772515789025596)
XLA Ops:
  7.9 9.3 %all_gather.12 = bf16[96,896]{1,0:T(8,128)(2,1)S(1)} all-gather(bf16[48,896]{1,0:T(8,128)(2,1)} %param.6), channel_id=1, replica_groups=mesh['x'=4,'y'=4,'c'=2,'z'=8,'h'=2] {'h'}, dimensions={0}, use_global_device_ids=true | all-gather | bytes 258048 | tf_op jit(solution)/shard_map/all_gather | solution.py:93
  17.2 1.2 broadcast_in_dim.12
  18.4 10.2 %all-to-all-start = ((bf16[8,96,896]{2,1,0:T(8,128)(2,1)}), bf16[8,96,896]{2,1,0:T(8,128)(2,1)S(1)}, u32[]{:S(2)}, u32[]{:S(2)}) async-start(bf16[8,96,896]{2,1,0:T(8,128)(2,1)} %broadcast_in_dim.12), calls=%async_computation | async-start | bytes 2752512 | tf_op jit(solution)/shard_map/all_to_all | solution.py:68
  28.6 4.9 %collective-permute-start = (f32[2,24,256]{2,1,0:T(8,128)S(1)}, f32[2,24,256]{2,1,0:T(8,128)S(1)}, u32[]{:S(2)}, u32[]{:S(2)}) collective-permute-start(f32[2,24,256]{2,1,0:T(8,128)S(1)} %broadcast_select_fusion), channel_id=1, source_target_pairs={{0,16},{16,0},{1,17},{17,1},{2,18},{18,2},{3,19},{19,3},{4,20},{20... | collective-permute-start | bytes 147464 | tf_op jit(solution)/shard_map/ppermute | solution.py:89
  34.4 30.3 %all-to-all-done = bf16[8,96,896]{2,1,0:T(8,128)(2,1)S(1)} async-done(((bf16[8,96,896]{2,1,0:T(8,128)(2,1)}), bf16[8,96,896]{2,1,0:T(8,128)(2,1)S(1)}, u32[]{:S(2)}, u32[]{:S(2)}) %all-to-all-start) | async-done | bytes 1376288 | tf_op jit(solution)/shard_map/all_to_all | solution.py:68
  64.7 1.0 fusion.1
  65.8 2.5 %collective-permute-start.1 = (bf16[16,24,512]{2,1,0:T(8,128)(2,1)S(1)}, bf16[16,24,512]{2,1,0:T(8,128)(2,1)S(1)}, u32[]{:S(2)}, u32[]{:S(2)}) collective-permute-start(bf16[16,24,512]{2,1,0:T(8,128)(2,1)S(1)} %fusion.7), channel_id=1, source_target_pairs={{0,16},{16,0},{1,17},{17,1},{2,18},{18,2},{3,19},{19,3},{4,20},{20... | collective-permute-start | bytes 1179656 | tf_op jit(solution)/shard_map/ppermute | solution.py:99
  68.3 1.3 collective-permute-done.1
  69.6 1.0 fusion.6
  70.5 8.8 %all-to-all-start.1 = ((bf16[16,24,512]{2,1,0:T(8,128)(2,1)}), bf16[16,24,512]{2,1,0:T(8,128)(2,1)S(1)}, u32[]{:S(2)}, u32[]{:S(2)}) async-start(bf16[16,24,512]{2,1,0:T(8,128)(2,1)} %fusion.6), calls=%async_computation.1 | async-start | bytes 786432 | tf_op jit(solution)/shard_map/all_to_all | solution.py:72
  80.0 13.1 %all-to-all-done.1 = bf16[16,24,512]{2,1,0:T(8,128)(2,1)S(1)} async-done(((bf16[16,24,512]{2,1,0:T(8,128)(2,1)}), bf16[16,24,512]{2,1,0:T(8,128)(2,1)S(1)}, u32[]{:S(2)}, u32[]{:S(2)}) %all-to-all-start.1) | async-done | bytes 393248 | tf_op jit(solution)/shard_map/all_to_all | solution.py:72
  93.2 4.7 %convolution_convert_fusion = bf16[24,32,256]{2,0,1:T(8,128)(2,1)S(1)} fusion(bf16[32,512,256]{2,1,0:T(8,128)(2,1)} %bitcast.74, bf16[24,512]{1,0:T(8,128)(2,1)S(1)} %fusion.17), kind=kOutput, calls=%fused_computation.2 | convolution fusion | flops 201523200 | bytes 8806400 | tf_op jit(solution)/shard_map/rk,fkn->frn/dot_general | solution.py:103
  97.9 26.4 %all_to_all.35 = bf16[16,2,24,256]{3,2,1,0:T(8,128)(2,1)S(1)} all-to-all(bf16[16,2,24,256]{3,2,1,0:T(8,128)(2,1)S(1)} %bitcast.77), channel_id=1, replica_groups=mesh['x'=4,'y'=4,'c'=2,'z'=8,'h'=2] {'z','h'}, dimensions={0} | all-to-all | bytes 786432 | tf_op jit(solution)/shard_map/all_to_all | solution.py:72
  124.4 21.3 %all_to_all.36 = bf16[16,2,24,256]{3,2,1,0:T(8,128)(2,1)S(1)} all-to-all(bf16[16,2,24,256]{3,2,1,0:T(8,128)(2,1)S(1)} %broadcast_in_dim.14), channel_id=1, replica_groups=mesh['x'=4,'y'=4,'c'=2,'z'=8,'h'=2] {'z','h'}, dimensions={0} | all-to-all | bytes 786432 | tf_op jit(solution)/shard_map/all_to_all | solution.py:68
  145.7 2.3 %fusion = bf16[24,512]{1,0:T(8,128)(2,1)S(1)} fusion(bf16[32,24,256]{2,1,0:T(8,128)(2,1)S(1)} %bitcast.76, bf16[32,512,256]{2,1,0:T(8,128)(2,1)S(1)} %bitcast.75), kind=kOutput, calls=%fused_computation.4 | convolution fusion | flops 201338880 | bytes 8806400 | tf_op jit(solution)/shard_map/dot_general | solution.py:107
  148.8 9.2 %all-to-all-start.4 = ((bf16[16,24,512]{2,1,0:T(8,128)(2,1)}), bf16[16,24,512]{2,1,0:T(8,128)(2,1)S(1)}, u32[]{:S(2)}, u32[]{:S(2)}) async-start(bf16[16,24,512]{2,1,0:T(8,128)(2,1)} %broadcast_in_dim.15), calls=%async_computation.4 | async-start | bytes 786432 | tf_op jit(solution)/shard_map/all_to_all | solution.py:68
  158.0 3.1 %collective-permute-start.3 = (f32[24,256]{1,0:T(8,128)S(1)}, f32[24,256]{1,0:T(8,128)S(1)}, u32[]{:S(2)}, u32[]{:S(2)}) collective-permute-start(f32[24,256]{1,0:T(8,128)S(1)} %select_bitcast_fusion.2), channel_id=1, source_target_pairs={{0,16},{16,0},{1,17},{17,1},{2,18},{18,2},{3,19},{19,3},{4,20},{20... | collective-permute-start | bytes 73736 | tf_op jit(solution)/shard_map/ppermute | solution.py:114
  161.1 0.8 collective-permute-done.3
  163.3 7.6 %all-to-all-done.4 = bf16[16,24,512]{2,1,0:T(8,128)(2,1)S(1)} async-done(((bf16[16,24,512]{2,1,0:T(8,128)(2,1)}), bf16[16,24,512]{2,1,0:T(8,128)(2,1)S(1)}, u32[]{:S(2)}, u32[]{:S(2)}) %all-to-all-start.4) | async-done | bytes 393248 | tf_op jit(solution)/shard_map/all_to_all | solution.py:68
  170.9 4.3 %all_gather.15 = bf16[16,48,512]{2,1,0:T(8,128)(2,1)S(1)} all-gather(bf16[16,24,512]{2,1,0:T(8,128)(2,1)S(1)} %all-to-all-done.4), channel_id=1, replica_groups=mesh['x'=4,'y'=4,'c'=2,'z'=8,'h'=2] {'c'}, dimensions={1}, use_global_device_ids=true | all-gather | bytes 1179648 | tf_op jit(solution)/shard_map/all_gather | solution.py:117
  175.1 0.9 multiply_reduce_fusion
  176.1 12.1 %all_to_all.37 = f32[8,2,128]{2,1,0:T(2,128)S(1)} all-to-all(f32[8,2,128]{2,1,0:T(2,128)S(1)} %broadcast_in_dim.16), channel_id=1, replica_groups=mesh['x'=4,'y'=4,'c'=2,'z'=8,'h'=2] {'x','c'}, dimensions={0} | all-to-all | bytes 16384 | tf_op jit(solution)/shard_map/all_to_all | solution.py:68
  188.2 21.0 %all_to_all.38.sums_ref = f32[64,2,128]{2,1,0:T(2,128)S(1)} all-to-all(f32[64,2,128]{2,1,0:T(2,128)S(1)} %broadcast_in_dim.17), channel_id=1, replica_groups=mesh['x'=4,'y'=4,'c'=2,'z'=8,'h'=2] {'y','z','h'}, dimensions={0} | all-to-all | bytes 131072 | tf_op jit(solution)/shard_map/all_to_all | solution.py:68
  209.2 1.5 shard_map.76
  (35 shorter events, 4.8 us)
Async XLA Ops:
  7.2 86.0 %all-gather.3.cloned.1.call-start = ((), (), s32[]{:S(2)}) async-start(), calls=%async_computation.7 | async-start | bytes 8650752 | tf_op jit(solution)/shard_map/all_gather | solution.py:85
  17.2 11.4 %copy-start.2 = (f32[48,256]{1,0:T(8,128)S(1)}, f32[48,256]{1,0:T(8,128)}, u32[]{:S(2)}) copy-start(f32[48,256]{1,0:T(8,128)} %param.9) | copy-start | bytes 147460
  17.2 11.4 %copy-start.3 = (f32[48,256]{1,0:T(8,128)S(1)}, f32[48,256]{1,0:T(8,128)}, u32[]{:S(2)}) copy-start(f32[48,256]{1,0:T(8,128)} %param.8) | copy-start | bytes 147460
  18.4 15.1 %copy-start.1 = (f32[896,512]{1,0:T(8,128)S(1)}, f32[896,512]{1,0:T(8,128)}, u32[]{:S(2)}) copy-start(f32[896,512]{1,0:T(8,128)} %param.5) | copy-start | bytes 5505028
  18.4 46.3 %all-to-all-start = ((bf16[8,96,896]{2,1,0:T(8,128)(2,1)}), bf16[8,96,896]{2,1,0:T(8,128)(2,1)S(1)}, u32[]{:S(2)}, u32[]{:S(2)}) async-start(bf16[8,96,896]{2,1,0:T(8,128)(2,1)} %broadcast_in_dim.12), calls=%async_computation | async-start | bytes 2752512 | tf_op jit(solution)/shard_map/all_to_all | solution.py:68
  28.6 5.8 %collective-permute-start = (f32[2,24,256]{2,1,0:T(8,128)S(1)}, f32[2,24,256]{2,1,0:T(8,128)S(1)}, u32[]{:S(2)}, u32[]{:S(2)}) collective-permute-start(f32[2,24,256]{2,1,0:T(8,128)S(1)} %broadcast_select_fusion), channel_id=1, source_target_pairs={{0,16},{16,0},{1,17},{17,1},{2,18},{18,2},{3,19},{19,3},{4,20},{20... | collective-permute-start | bytes 147464 | tf_op jit(solution)/shard_map/ppermute | solution.py:89
  65.8 3.8 %collective-permute-start.1 = (bf16[16,24,512]{2,1,0:T(8,128)(2,1)S(1)}, bf16[16,24,512]{2,1,0:T(8,128)(2,1)S(1)}, u32[]{:S(2)}, u32[]{:S(2)}) collective-permute-start(bf16[16,24,512]{2,1,0:T(8,128)(2,1)S(1)} %fusion.7), channel_id=1, source_target_pairs={{0,16},{16,0},{1,17},{17,1},{2,18},{18,2},{3,19},{19,3},{4,20},{20... | collective-permute-start | bytes 1179656 | tf_op jit(solution)/shard_map/ppermute | solution.py:99
  70.5 22.5 %all-to-all-start.1 = ((bf16[16,24,512]{2,1,0:T(8,128)(2,1)}), bf16[16,24,512]{2,1,0:T(8,128)(2,1)S(1)}, u32[]{:S(2)}, u32[]{:S(2)}) async-start(bf16[16,24,512]{2,1,0:T(8,128)(2,1)} %fusion.6), calls=%async_computation.1 | async-start | bytes 786432 | tf_op jit(solution)/shard_map/all_to_all | solution.py:72
  79.3 13.8 %collective-permute-start.2 = (f32[2,2,24,256]{3,2,1,0:T(8,128)S(1)}, f32[2,2,24,256]{3,2,1,0:T(8,128)S(1)}, u32[]{:S(2)}, u32[]{:S(2)}) collective-permute-start(f32[2,2,24,256]{3,2,1,0:T(8,128)S(1)} %pad_maximum_fusion), channel_id=1, source_target_pairs={{0,0},{1,32},{2,64},{3,96},{4,128},{5,160},{6,192},{7,224},{8,256}... | collective-permute-start | bytes 294920 | tf_op jit(solution)/shard_map/ppermute | solution.py:95
  93.2 52.5 %copy-start = (bf16[16384,256]{1,0:T(8,128)(2,1)S(1)}, bf16[16384,256]{1,0:T(8,128)(2,1)}, u32[]{:S(2)}) copy-start(bf16[16384,256]{1,0:T(8,128)(2,1)} %all-gather.3.cloned.1.call-done) | copy-start | bytes 25165828
  148.8 22.1 %all-to-all-start.4 = ((bf16[16,24,512]{2,1,0:T(8,128)(2,1)}), bf16[16,24,512]{2,1,0:T(8,128)(2,1)S(1)}, u32[]{:S(2)}, u32[]{:S(2)}) async-start(bf16[16,24,512]{2,1,0:T(8,128)(2,1)} %broadcast_in_dim.15), calls=%async_computation.4 | async-start | bytes 786432 | tf_op jit(solution)/shard_map/all_to_all | solution.py:68
  158.0 3.9 %collective-permute-start.3 = (f32[24,256]{1,0:T(8,128)S(1)}, f32[24,256]{1,0:T(8,128)S(1)}, u32[]{:S(2)}, u32[]{:S(2)}) collective-permute-start(f32[24,256]{1,0:T(8,128)S(1)} %select_bitcast_fusion.2), channel_id=1, source_target_pairs={{0,16},{16,0},{1,17},{17,1},{2,18},{18,2},{3,19},{19,3},{4,20},{20... | collective-permute-start | bytes 73736 | tf_op jit(solution)/shard_map/ppermute | solution.py:114
  161.9 0.7 collective-permute-start.4
Sparse Core Ops, SparseCore 0:
  10.1 79.8 all-gather.2

commit v13 on v10

--- a/solution.py
+++ b/solution.py
@@ -15,12 +15,13 @@
 SWAP = [(0, 1), (1, 0)]
 TURN = [(16 * i + j, 16 * j + i) for i in range(16) for j in range(16)]
 PARTS = 4
-PIECES = 8
+PIECES = 16
+AHEAD = 6
 f32 = jnp.float32
 bf16 = jnp.bfloat16
 
 
-def fetch(basis_ref, held_ref, landed_ref):
+def back_kernel(direction_ref, basis_ref, out_ref, held_ref, landed_ref):
     size = held_ref.shape[0] // PIECES
     copies = []
     for piece in range(PIECES):
@@ -28,25 +29,13 @@
         copies.append(
             pltpu.make_async_copy(basis_ref.at[blocks], held_ref.at[blocks], landed_ref.at[piece])
         )
-        copies[-1].start()
-    return copies, size
-
-
-def rotate_kernel(rows_ref, basis_ref, out_ref, held_ref, landed_ref):
-    copies, size = fetch(basis_ref, held_ref, landed_ref)
-    rows = rows_ref[...]
-    for piece, copy in enumerate(copies):
-        copy.wait()
-        for block in range(piece * size, (piece + 1) * size):
-            product = jnp.dot(rows, held_ref[block], preferred_element_type=f32)
-            out_ref[block] = product.astype(bf16)
-
-
-def back_kernel(direction_ref, basis_ref, out_ref, held_ref, landed_ref):
-    copies, size = fetch(basis_ref, held_ref, landed_ref)
+    for copy in copies[:AHEAD]:
+        copy.start()
     total = jnp.zeros(out_ref.shape[1:], f32)
     for piece, copy in enumerate(copies):
         copy.wait()
+        if piece + AHEAD < PIECES:
+            copies[piece + AHEAD].start()
         for block in range(piece * size, (piece + 1) * size):
             total += lax.dot_general(
                 direction_ref[block],
@@ -59,18 +48,18 @@
         out_ref[target] = total
 
 
-def with_basis(kernel, left, basis, shape):
+def rotate_back(direction, basis):
     return pl.pallas_call(
-        kernel,
+        back_kernel,
         in_specs=[pl.BlockSpec(memory_space=pltpu.VMEM), pl.BlockSpec(memory_space=pl.ANY)],
         out_specs=pl.BlockSpec(memory_space=pltpu.VMEM),
-        out_shape=jax.ShapeDtypeStruct(shape, bf16),
+        out_shape=jax.ShapeDtypeStruct((16, 24, 512), bf16),
         scratch_shapes=[pltpu.VMEM(basis.shape, bf16), pltpu.SemaphoreType.DMA((PIECES,))],
         compiler_params=pltpu.CompilerParams(vmem_limit_bytes=57 * 2**20),
         cost_estimate=pl.CostEstimate(
             flops=48 * basis.size, bytes_accessed=2 * basis.size, transcendentals=0
         ),
-    )(left, basis)
+    )(direction, basis)
 
 
 def scale_kernel(sums_ref, unscaled_ref, update_ref, scaled_ref, done_ref):
@@ -154,12 +143,11 @@
     projected = collect(keep.astype(bf16), ("x", "y")).astype(bf16)
     projected, moments = lax.optimization_barrier((projected, moments))
 
-    rotated = with_basis(rotate_kernel, projected, basis, (32, 24, 256))
-    rotated = collect(rotated.reshape(16, 2, 24, 256), B)
+    rotated = jnp.einsum("rk,fkn->frn", projected, basis, preferred_element_type=f32)
+    rotated = collect(rotated.astype(bf16).reshape(16, 2, 24, 256), B)
     direction = (adam(moments[0], moments[1], rotated)[2]).astype(bf16)
     direction = spread(direction, B, 16).reshape(32, 24, 256)
-    returned = with_basis(back_kernel, direction, basis, (16, 24, 512))
-    half = lax.all_to_all(returned, ("x", "y"), 0, 0, tiled=True)
+    half = lax.all_to_all(rotate_back(direction, basis), ("x", "y"), 0, 0, tiled=True)
     rotated = lax.ppermute(rotated, ("x", "y", "z", "h"), TURN)
     keep, send = sort(rotated[0], rotated[1])
     rotated = jnp.concatenate(sort(keep, lax.ppermute(send, "c", SWAP)))

time: 215 us -> 214 us (level)
  Pallas kernels: 12.4 us -> 7.67 us
  matrix products: 1.93 us -> 6.51 us
    pallas_call x2 -> x1, Pallas kernels: 11 us -> 6.19 us  [rotate_back(): pl.pallas_call(back_kernel, in_specs=[pl.BlockSpec(memory_space=pltpu.VME...]
    dot_general x0 -> x1, matrix products: none -> 4.58 us  [body(): jnp.einsum('rk,fkn->frn', projected, basis, preferred_element_type=f32)]
where the time goes in v13:
time: 214 us; the launch traced here: 213 us
  waiting for transfers between devices  68 us (32%)
  blocking collectives  63.2 us (30%)
  starting transfers between devices  48.9 us (23%)
  between operations  14.2 us (7%)
  Pallas kernels  7.67 us (4%)
  matrix products  6.51 us (3%)
  local copies, waits for them, and re-layouts  2.74 us (1%)
  other arithmetic  2.14 us (1%)
    all_to_all x2, waiting for transfers between devices, spread(): return lax.all_to_all(copies, axes, 0, 0, tiled=True)  43.5 us
    all_to_all x1, blocking collectives, collect(): got = lax.all_to_all(parts, axes, 0, 0, tiled=True)  26.3 us
    all_to_all x2, blocking collectives, spread(): return lax.all_to_all(copies, axes, 0, 0, tiled=True)  24 us
    all_to_all x2, starting transfers between devices, spread(): return lax.all_to_all(copies, axes, 0, 0, tiled=True)  18.3 us
    all_to_all x1, waiting for transfers between devices, collect(): got = lax.all_to_all(parts, axes, 0, 0, tiled=True)  13.1 us
    all_to_all x1, starting transfers between devices, body(): lax.all_to_all(rotate_back(direction, basis), ('x', 'y'), 0, 0, tiled=True)  9.63 us
    all_gather x1, blocking collectives, body(): panels = spread(lax.all_gather(left_basis, 'h', tiled=True), 'z', 8)  9.28 us
    all_to_all x1, starting transfers between devices, collect(): got = lax.all_to_all(parts, axes, 0, 0, tiled=True)  8.79 us
  transfers between devices with their start and end apart: 10, of which 7 were waited for; matrix products, arithmetic and copies ran while one was open for 2% of the time, Pallas kernels for 3%

profile of v13, /device:TPU:1, one launch (start us, length us, event | category | flops | bytes accessed | tf_op | source)
XLA Modules:
  0.0 213.4 jit_solution(372373876791243204)
XLA Ops:
  7.9 9.3 %all_gather.12 = bf16[96,896]{1,0:T(8,128)(2,1)S(1)} all-gather(bf16[48,896]{1,0:T(8,128)(2,1)} %param.6), channel_id=1, replica_groups=mesh['x'=4,'y'=4,'c'=2,'z'=8,'h'=2] {'h'}, dimensions={0}, use_global_device_ids=true | all-gather | bytes 258048 | tf_op jit(solution)/shard_map/all_gather | solution.py:136
  17.2 1.2 broadcast_in_dim.10
  18.4 10.2 %all-to-all-start = ((bf16[8,96,896]{2,1,0:T(8,128)(2,1)}), bf16[8,96,896]{2,1,0:T(8,128)(2,1)S(1)}, u32[]{:S(2)}, u32[]{:S(2)}) async-start(bf16[8,96,896]{2,1,0:T(8,128)(2,1)} %broadcast_in_dim.10), calls=%async_computation | async-start | bytes 2752512 | tf_op jit(solution)/shard_map/all_to_all | solution.py:111
  28.6 4.9 %collective-permute-start = (f32[2,24,256]{2,1,0:T(8,128)S(1)}, f32[2,24,256]{2,1,0:T(8,128)S(1)}, u32[]{:S(2)}, u32[]{:S(2)}) collective-permute-start(f32[2,24,256]{2,1,0:T(8,128)S(1)} %broadcast_select_fusion), channel_id=1, source_target_pairs={{0,16},{16,0},{1,17},{17,1},{2,18},{18,2},{3,19},{19,3},{4,20},{20... | collective-permute-start | bytes 147464 | tf_op jit(solution)/shard_map/ppermute | solution.py:132
  34.4 30.3 %all-to-all-done = bf16[8,96,896]{2,1,0:T(8,128)(2,1)S(1)} async-done(((bf16[8,96,896]{2,1,0:T(8,128)(2,1)}), bf16[8,96,896]{2,1,0:T(8,128)(2,1)S(1)}, u32[]{:S(2)}, u32[]{:S(2)}) %all-to-all-start) | async-done | bytes 1376288 | tf_op jit(solution)/shard_map/all_to_all | solution.py:111
  64.7 1.0 fusion
  65.8 2.5 %collective-permute-start.1 = (bf16[16,24,512]{2,1,0:T(8,128)(2,1)S(1)}, bf16[16,24,512]{2,1,0:T(8,128)(2,1)S(1)}, u32[]{:S(2)}, u32[]{:S(2)}) collective-permute-start(bf16[16,24,512]{2,1,0:T(8,128)(2,1)S(1)} %fusion.6), channel_id=1, source_target_pairs={{0,16},{16,0},{1,17},{17,1},{2,18},{18,2},{3,19},{19,3},{4,20},{20... | collective-permute-start | bytes 1179656 | tf_op jit(solution)/shard_map/ppermute | solution.py:142
  68.3 1.3 collective-permute-done.1
  69.6 1.0 fusion.5
  70.5 8.8 %all-to-all-start.1 = ((bf16[16,24,512]{2,1,0:T(8,128)(2,1)}), bf16[16,24,512]{2,1,0:T(8,128)(2,1)S(1)}, u32[]{:S(2)}, u32[]{:S(2)}) async-start(bf16[16,24,512]{2,1,0:T(8,128)(2,1)} %fusion.5), calls=%async_computation.1 | async-start | bytes 786432 | tf_op jit(solution)/shard_map/all_to_all | solution.py:115
  80.0 13.1 %all-to-all-done.1 = bf16[16,24,512]{2,1,0:T(8,128)(2,1)S(1)} async-done(((bf16[16,24,512]{2,1,0:T(8,128)(2,1)}), bf16[16,24,512]{2,1,0:T(8,128)(2,1)S(1)}, u32[]{:S(2)}, u32[]{:S(2)}) %all-to-all-start.1) | async-done | bytes 393248 | tf_op jit(solution)/shard_map/all_to_all | solution.py:115
  93.2 4.6 %convolution_convert_fusion = bf16[24,32,256]{2,0,1:T(8,128)(2,1)S(1)} fusion(bf16[32,512,256]{2,1,0:T(8,128)(2,1)} %bitcast.68, bf16[24,512]{1,0:T(8,128)(2,1)S(1)} %fusion.16), kind=kOutput, calls=%fused_computation.2 | convolution fusion | flops 201523200 | bytes 8806400 | tf_op jit(solution)/shard_map/rk,fkn->frn/dot_general | solution.py:146
  97.7 26.3 %all_to_all.35 = bf16[16,2,24,256]{3,2,1,0:T(8,128)(2,1)S(1)} all-to-all(bf16[16,2,24,256]{3,2,1,0:T(8,128)(2,1)S(1)} %bitcast.71), channel_id=1, replica_groups=mesh['x'=4,'y'=4,'c'=2,'z'=8,'h'=2] {'z','h'}, dimensions={0} | all-to-all | bytes 786432 | tf_op jit(solution)/shard_map/all_to_all | solution.py:115
  124.9 8.1 %all-to-all-start.3 = ((bf16[16,2,24,256]{3,2,1,0:T(8,128)(2,1)}), bf16[16,2,24,256]{3,2,1,0:T(8,128)(2,1)S(1)}, u32[]{:S(2)}, u32[]{:S(2)}) async-start(bf16[16,2,24,256]{3,2,1,0:T(8,128)(2,1)} %broadcast_in_dim.12), calls=%async_computation.3 | async-start | bytes 786432 | tf_op jit(solution)/shard_map/all_to_all | solution.py:111
  133.7 13.2 %all-to-all-done.3 = bf16[16,2,24,256]{3,2,1,0:T(8,128)(2,1)S(1)} async-done(((bf16[16,2,24,256]{3,2,1,0:T(8,128)(2,1)}), bf16[16,2,24,256]{3,2,1,0:T(8,128)(2,1)S(1)}, u32[]{:S(2)}, u32[]{:S(2)}) %all-to-all-start.3) | async-done | bytes 393248 | tf_op jit(solution)/shard_map/all_to_all | solution.py:111
  147.6 6.2 %shard_map.76 = bf16[16,24,512]{2,1,0:T(8,128)(2,1)} custom-call(bf16[32,24,256]{2,1,0:T(8,128)(2,1)} %bitcast.70, bf16[32,512,256]{2,1,0:T(8,128)(2,1)} %bitcast.69), custom_call_target="tpu_custom_call" | custom-call | flops 201326592 | bytes 8388608 | tf_op jit(solution)/shard_map/pallas_call | solution.py:52
  153.8 9.6 %all-to-all-start.4 = ((bf16[16,24,512]{2,1,0:T(8,128)(2,1)}), bf16[16,24,512]{2,1,0:T(8,128)(2,1)S(1)}, u32[]{:S(2)}, u32[]{:S(2)}) async-start(bf16[16,24,512]{2,1,0:T(8,128)(2,1)} %shard_map.76), calls=%async_computation.4 | async-start | bytes 786432 | tf_op jit(solution)/shard_map/all_to_all | solution.py:150
  163.5 3.4 %collective-permute-start.4 = (f32[24,256]{1,0:T(8,128)S(1)}, f32[24,256]{1,0:T(8,128)S(1)}, u32[]{:S(2)}, u32[]{:S(2)}) collective-permute-start(f32[24,256]{1,0:T(8,128)S(1)} %select_bitcast_fusion.2), channel_id=1, source_target_pairs={{0,16},{16,0},{1,17},{17,1},{2,18},{18,2},{3,19},{19,3},{4,20},{20... | collective-permute-start | bytes 73736 | tf_op jit(solution)/shard_map/ppermute | solution.py:153
  168.4 8.0 %all-to-all-done.4 = bf16[16,24,512]{2,1,0:T(8,128)(2,1)S(1)} async-done(((bf16[16,24,512]{2,1,0:T(8,128)(2,1)}), bf16[16,24,512]{2,1,0:T(8,128)(2,1)S(1)}, u32[]{:S(2)}, u32[]{:S(2)}) %all-to-all-start.4) | async-done | bytes 393248 | tf_op jit(solution)/shard_map/all_to_all | solution.py:150
  176.3 3.7 %all_gather.15 = bf16[16,48,512]{2,1,0:T(8,128)(2,1)S(1)} all-gather(bf16[16,24,512]{2,1,0:T(8,128)(2,1)S(1)} %all-to-all-done.4), channel_id=1, replica_groups=mesh['x'=4,'y'=4,'c'=2,'z'=8,'h'=2] {'c'}, dimensions={1}, use_global_device_ids=true | all-gather | bytes 1179648 | tf_op jit(solution)/shard_map/all_gather | solution.py:156
  180.1 0.9 multiply_reduce_fusion
  181.0 7.3 %all_to_all.36 = f32[8,2,128]{2,1,0:T(2,128)S(1)} all-to-all(f32[8,2,128]{2,1,0:T(2,128)S(1)} %broadcast_in_dim.13), channel_id=1, replica_groups=mesh['x'=4,'y'=4,'c'=2,'z'=8,'h'=2] {'x','c'}, dimensions={0} | all-to-all | bytes 16384 | tf_op jit(solution)/shard_map/all_to_all | solution.py:111
  188.4 16.6 %all_to_all.37.sums_ref = f32[64,2,128]{2,1,0:T(2,128)S(1)} all-to-all(f32[64,2,128]{2,1,0:T(2,128)S(1)} %broadcast_in_dim.14), channel_id=1, replica_groups=mesh['x'=4,'y'=4,'c'=2,'z'=8,'h'=2] {'y','z','h'}, dimensions={0} | all-to-all | bytes 131072 | tf_op jit(solution)/shard_map/all_to_all | solution.py:111
  205.0 1.5 shard_map.77
  (34 shorter events, 6.3 us)
Async XLA Ops:
  7.2 86.0 %all-gather.3.cloned.1.call-start = ((), (), s32[]{:S(2)}) async-start(), calls=%async_computation.7 | async-start | bytes 8650752 | tf_op jit(solution)/shard_map/all_gather | solution.py:128
  17.2 11.4 %copy-start.2 = (f32[48,256]{1,0:T(8,128)S(1)}, f32[48,256]{1,0:T(8,128)}, u32[]{:S(2)}) copy-start(f32[48,256]{1,0:T(8,128)} %param.9) | copy-start | bytes 147460
  17.2 11.4 %copy-start.3 = (f32[48,256]{1,0:T(8,128)S(1)}, f32[48,256]{1,0:T(8,128)}, u32[]{:S(2)}) copy-start(f32[48,256]{1,0:T(8,128)} %param.8) | copy-start | bytes 147460
  18.4 15.1 %copy-start = (f32[896,512]{1,0:T(8,128)S(1)}, f32[896,512]{1,0:T(8,128)}, u32[]{:S(2)}) copy-start(f32[896,512]{1,0:T(8,128)} %param.5) | copy-start | bytes 5505028
  18.4 46.3 %all-to-all-start = ((bf16[8,96,896]{2,1,0:T(8,128)(2,1)}), bf16[8,96,896]{2,1,0:T(8,128)(2,1)S(1)}, u32[]{:S(2)}, u32[]{:S(2)}) async-start(bf16[8,96,896]{2,1,0:T(8,128)(2,1)} %broadcast_in_dim.10), calls=%async_computation | async-start | bytes 2752512 | tf_op jit(solution)/shard_map/all_to_all | solution.py:111
  28.6 5.8 %collective-permute-start = (f32[2,24,256]{2,1,0:T(8,128)S(1)}, f32[2,24,256]{2,1,0:T(8,128)S(1)}, u32[]{:S(2)}, u32[]{:S(2)}) collective-permute-start(f32[2,24,256]{2,1,0:T(8,128)S(1)} %broadcast_select_fusion), channel_id=1, source_target_pairs={{0,16},{16,0},{1,17},{17,1},{2,18},{18,2},{3,19},{19,3},{4,20},{20... | collective-permute-start | bytes 147464 | tf_op jit(solution)/shard_map/ppermute | solution.py:132
  65.8 3.8 %collective-permute-start.1 = (bf16[16,24,512]{2,1,0:T(8,128)(2,1)S(1)}, bf16[16,24,512]{2,1,0:T(8,128)(2,1)S(1)}, u32[]{:S(2)}, u32[]{:S(2)}) collective-permute-start(bf16[16,24,512]{2,1,0:T(8,128)(2,1)S(1)} %fusion.6), channel_id=1, source_target_pairs={{0,16},{16,0},{1,17},{17,1},{2,18},{18,2},{3,19},{19,3},{4,20},{20... | collective-permute-start | bytes 1179656 | tf_op jit(solution)/shard_map/ppermute | solution.py:142
  70.5 22.5 %all-to-all-start.1 = ((bf16[16,24,512]{2,1,0:T(8,128)(2,1)}), bf16[16,24,512]{2,1,0:T(8,128)(2,1)S(1)}, u32[]{:S(2)}, u32[]{:S(2)}) async-start(bf16[16,24,512]{2,1,0:T(8,128)(2,1)} %fusion.5), calls=%async_computation.1 | async-start | bytes 786432 | tf_op jit(solution)/shard_map/all_to_all | solution.py:115
  79.3 13.8 %collective-permute-start.2 = (f32[2,2,24,256]{3,2,1,0:T(8,128)S(1)}, f32[2,2,24,256]{3,2,1,0:T(8,128)S(1)}, u32[]{:S(2)}, u32[]{:S(2)}) collective-permute-start(f32[2,2,24,256]{3,2,1,0:T(8,128)S(1)} %pad_maximum_fusion), channel_id=1, source_target_pairs={{0,0},{1,32},{2,64},{3,96},{4,128},{5,160},{6,192},{7,224},{8,256}... | collective-permute-start | bytes 294920 | tf_op jit(solution)/shard_map/ppermute | solution.py:138
  124.9 22.0 %all-to-all-start.3 = ((bf16[16,2,24,256]{3,2,1,0:T(8,128)(2,1)}), bf16[16,2,24,256]{3,2,1,0:T(8,128)(2,1)S(1)}, u32[]{:S(2)}, u32[]{:S(2)}) async-start(bf16[16,2,24,256]{3,2,1,0:T(8,128)(2,1)} %broadcast_in_dim.12), calls=%async_computation.3 | async-start | bytes 786432 | tf_op jit(solution)/shard_map/all_to_all | solution.py:111
  133.0 30.4 %collective-permute-start.3 = (f32[2,24,256]{2,1,0:T(8,128)S(1)}, f32[2,24,256]{2,1,0:T(8,128)S(1)}, u32[]{:S(2)}, u32[]{:S(2)}) collective-permute-start(f32[2,24,256]{2,1,0:T(8,128)S(1)} %bitcast.79), channel_id=1, source_target_pairs={{0,0},{1,32},{2,64},{3,96},{4,128},{5,160},{6,192},{7,224},{8,256}... | collective-permute-start | bytes 147464 | tf_op jit(solution)/shard_map/ppermute | solution.py:151
  146.8 0.7 copy-start.1
  153.8 22.5 %all-to-all-start.4 = ((bf16[16,24,512]{2,1,0:T(8,128)(2,1)}), bf16[16,24,512]{2,1,0:T(8,128)(2,1)S(1)}, u32[]{:S(2)}, u32[]{:S(2)}) async-start(bf16[16,24,512]{2,1,0:T(8,128)(2,1)} %shard_map.76), calls=%async_computation.4 | async-start | bytes 786432 | tf_op jit(solution)/shard_map/all_to_all | solution.py:150
  163.5 4.2 %collective-permute-start.4 = (f32[24,256]{1,0:T(8,128)S(1)}, f32[24,256]{1,0:T(8,128)S(1)}, u32[]{:S(2)}, u32[]{:S(2)}) collective-permute-start(f32[24,256]{1,0:T(8,128)S(1)} %select_bitcast_fusion.2), channel_id=1, source_target_pairs={{0,16},{16,0},{1,17},{17,1},{2,18},{18,2},{3,19},{19,3},{4,20},{20... | collective-permute-start | bytes 73736 | tf_op jit(solution)/shard_map/ppermute | solution.py:153
Sparse Core Ops, SparseCore 0:
  10.1 79.8 all-gather.2

commit v14 on v8

--- a/solution.py
+++ b/solution.py
@@ -108,7 +108,8 @@
         direction, basis, (((0, 2), (0, 2)), ((), ())), preferred_element_type=f32
     )
 
-    half = spread(returned.astype(bf16), ("x", "y"), 16)
+    returned, rotated = lax.optimization_barrier((returned.astype(bf16), rotated))
+    half = spread(returned, ("x", "y"), 16)
     rotated = lax.ppermute(rotated, ("x", "y", "z", "h"), TURN)
     keep, send = sort(rotated[0], rotated[1])
     rotated = jnp.concatenate(sort(keep, lax.ppermute(send, "c", SWAP)))

time: 214 us -> 218 us (1.019)
  blocking collectives: 63.2 us -> 90.4 us
  waiting for transfers between devices: 68 us -> 55.3 us
  starting transfers between devices: 48.9 us -> 42.8 us
  matrix products: 12.2 us -> 8.96 us
    all_to_all x2 -> x3, blocking collectives: 24 us -> 51 us  [spread(): return lax.all_to_all(copies, axes, 0, 0, tiled=True)]
    all_to_all x3 -> x2, waiting for transfers between devices: 51.4 us -> 38.7 us  [spread(): return lax.all_to_all(copies, axes, 0, 0, tiled=True)]
    all_to_all x3 -> x2, starting transfers between devices: 27.9 us -> 22.3 us  [spread(): return lax.all_to_all(copies, axes, 0, 0, tiled=True)]
    dot_general x1, matrix products: 5.68 us -> 2.3 us  [body(): lax.dot_general(direction, basis, (((0, 2), (0, 2)), ((), ())), preferred...]
  transfers between devices with their start and end apart: 10 -> 9, of which waited for: 7 -> 6; matrix products, arithmetic and copies ran while one was open for 5% -> 2% of each run, Pallas kernels for 0% -> 0%
where the time goes in v14:
time: 218 us; the launch traced here: 217 us
  blocking collectives  90.4 us (41%)
  waiting for transfers between devices  55.3 us (25%)
  starting transfers between devices  42.8 us (20%)
  between operations  14.2 us (7%)
  matrix products  8.96 us (4%)
    all_to_all x3, blocking collectives, spread(): return lax.all_to_all(copies, axes, 0, 0, tiled=True)  51 us
    all_to_all x2, waiting for transfers between devices, spread(): return lax.all_to_all(copies, axes, 0, 0, tiled=True)  38.7 us
    all_to_all x1, blocking collectives, collect(): got = lax.all_to_all(parts, axes, 0, 0, tiled=True)  26.4 us
    all_to_all x2, starting transfers between devices, spread(): return lax.all_to_all(copies, axes, 0, 0, tiled=True)  22.3 us
    all_to_all x1, waiting for transfers between devices, collect(): got = lax.all_to_all(parts, axes, 0, 0, tiled=True)  13.1 us
    all_gather x1, blocking collectives, body(): panels = spread(lax.all_gather(left_basis, 'h', tiled=True), 'z', 8)  9.28 us
    all_to_all x1, starting transfers between devices, collect(): got = lax.all_to_all(parts, axes, 0, 0, tiled=True)  8.79 us
    ppermute x1, starting transfers between devices, body(): blocks = sort(keep, lax.ppermute(send, 'c', SWAP))  4.91 us
  transfers between devices with their start and end apart: 9, of which 6 were waited for; matrix products, arithmetic and copies ran while one was open for 2% of the time, Pallas kernels for 0%

profile of v14, /device:TPU:1, one launch (start us, length us, event | category | flops | bytes accessed | tf_op | source)
XLA Modules:
  0.0 217.3 jit_solution(6073326719375892843)
XLA Ops:
  7.9 9.3 %all_gather.12 = bf16[96,896]{1,0:T(8,128)(2,1)S(1)} all-gather(bf16[48,896]{1,0:T(8,128)(2,1)} %param.6), channel_id=1, replica_groups=mesh['x'=4,'y'=4,'c'=2,'z'=8,'h'=2] {'h'}, dimensions={0}, use_global_device_ids=true | all-gather | bytes 258048 | tf_op jit(solution)/shard_map/all_gather | solution.py:93
  17.2 1.2 broadcast_in_dim.12
  18.4 10.2 %all-to-all-start = ((bf16[8,96,896]{2,1,0:T(8,128)(2,1)}), bf16[8,96,896]{2,1,0:T(8,128)(2,1)S(1)}, u32[]{:S(2)}, u32[]{:S(2)}) async-start(bf16[8,96,896]{2,1,0:T(8,128)(2,1)} %broadcast_in_dim.12), calls=%async_computation | async-start | bytes 2752512 | tf_op jit(solution)/shard_map/all_to_all | solution.py:68
  28.6 4.9 %collective-permute-start = (f32[2,24,256]{2,1,0:T(8,128)S(1)}, f32[2,24,256]{2,1,0:T(8,128)S(1)}, u32[]{:S(2)}, u32[]{:S(2)}) collective-permute-start(f32[2,24,256]{2,1,0:T(8,128)S(1)} %broadcast_select_fusion), channel_id=1, source_target_pairs={{0,16},{16,0},{1,17},{17,1},{2,18},{18,2},{3,19},{19,3},{4,20},{20... | collective-permute-start | bytes 147464 | tf_op jit(solution)/shard_map/ppermute | solution.py:89
  34.4 30.3 %all-to-all-done = bf16[8,96,896]{2,1,0:T(8,128)(2,1)S(1)} async-done(((bf16[8,96,896]{2,1,0:T(8,128)(2,1)}), bf16[8,96,896]{2,1,0:T(8,128)(2,1)S(1)}, u32[]{:S(2)}, u32[]{:S(2)}) %all-to-all-start) | async-done | bytes 1376288 | tf_op jit(solution)/shard_map/all_to_all | solution.py:68
  64.7 1.0 fusion.1
  65.8 2.5 %collective-permute-start.1 = (bf16[16,24,512]{2,1,0:T(8,128)(2,1)S(1)}, bf16[16,24,512]{2,1,0:T(8,128)(2,1)S(1)}, u32[]{:S(2)}, u32[]{:S(2)}) collective-permute-start(bf16[16,24,512]{2,1,0:T(8,128)(2,1)S(1)} %fusion.7), channel_id=1, source_target_pairs={{0,16},{16,0},{1,17},{17,1},{2,18},{18,2},{3,19},{19,3},{4,20},{20... | collective-permute-start | bytes 1179656 | tf_op jit(solution)/shard_map/ppermute | solution.py:99
  68.3 1.3 collective-permute-done.1
  69.6 1.0 fusion.6
  70.5 8.8 %all-to-all-start.1 = ((bf16[16,24,512]{2,1,0:T(8,128)(2,1)}), bf16[16,24,512]{2,1,0:T(8,128)(2,1)S(1)}, u32[]{:S(2)}, u32[]{:S(2)}) async-start(bf16[16,24,512]{2,1,0:T(8,128)(2,1)} %fusion.6), calls=%async_computation.1 | async-start | bytes 786432 | tf_op jit(solution)/shard_map/all_to_all | solution.py:72
  80.0 13.1 %all-to-all-done.1 = bf16[16,24,512]{2,1,0:T(8,128)(2,1)S(1)} async-done(((bf16[16,24,512]{2,1,0:T(8,128)(2,1)}), bf16[16,24,512]{2,1,0:T(8,128)(2,1)S(1)}, u32[]{:S(2)}, u32[]{:S(2)}) %all-to-all-start.1) | async-done | bytes 393248 | tf_op jit(solution)/shard_map/all_to_all | solution.py:72
  93.2 4.7 %convolution_convert_fusion = bf16[24,32,256]{2,0,1:T(8,128)(2,1)S(1)} fusion(bf16[32,512,256]{2,1,0:T(8,128)(2,1)} %bitcast.74, bf16[24,512]{1,0:T(8,128)(2,1)S(1)} %fusion.17), kind=kOutput, calls=%fused_computation.2 | convolution fusion | flops 201523200 | bytes 8806400 | tf_op jit(solution)/shard_map/rk,fkn->frn/dot_general | solution.py:103
  97.9 26.4 %all_to_all.35 = bf16[16,2,24,256]{3,2,1,0:T(8,128)(2,1)S(1)} all-to-all(bf16[16,2,24,256]{3,2,1,0:T(8,128)(2,1)S(1)} %bitcast.77), channel_id=1, replica_groups=mesh['x'=4,'y'=4,'c'=2,'z'=8,'h'=2] {'z','h'}, dimensions={0} | all-to-all | bytes 786432 | tf_op jit(solution)/shard_map/all_to_all | solution.py:72
  124.4 21.3 %all_to_all.36 = bf16[16,2,24,256]{3,2,1,0:T(8,128)(2,1)S(1)} all-to-all(bf16[16,2,24,256]{3,2,1,0:T(8,128)(2,1)S(1)} %broadcast_in_dim.14), channel_id=1, replica_groups=mesh['x'=4,'y'=4,'c'=2,'z'=8,'h'=2] {'z','h'}, dimensions={0} | all-to-all | bytes 786432 | tf_op jit(solution)/shard_map/all_to_all | solution.py:68
  145.7 2.3 %fusion = bf16[24,512]{1,0:T(8,128)(2,1)S(1)} fusion(bf16[32,24,256]{2,1,0:T(8,128)(2,1)S(1)} %bitcast.76, bf16[32,512,256]{2,1,0:T(8,128)(2,1)S(1)} %bitcast.75), kind=kOutput, calls=%fused_computation.4 | convolution fusion | flops 201338880 | bytes 8806400 | tf_op jit(solution)/shard_map/dot_general | solution.py:107
  149.4 12.1 %all-to-all-start.4 = ((bf16[16,24,512]{2,1,0:T(8,128)(2,1)}), bf16[16,24,512]{2,1,0:T(8,128)(2,1)S(1)}, u32[]{:S(2)}, u32[]{:S(2)}) async-start(bf16[16,24,512]{2,1,0:T(8,128)(2,1)} %broadcast_in_dim.15), calls=%async_computation.4 | async-start | bytes 786432 | tf_op jit(solution)/shard_map/all_to_all | solution.py:68
  161.6 3.0 %collective-permute-start.4 = (f32[24,256]{1,0:T(8,128)S(1)}, f32[24,256]{1,0:T(8,128)S(1)}, u32[]{:S(2)}, u32[]{:S(2)}) collective-permute-start(f32[24,256]{1,0:T(8,128)S(1)} %select_bitcast_fusion.2), channel_id=1, source_target_pairs={{0,16},{16,0},{1,17},{17,1},{2,18},{18,2},{3,19},{19,3},{4,20},{20... | collective-permute-start | bytes 73736 | tf_op jit(solution)/shard_map/ppermute | solution.py:115
  164.6 0.8 collective-permute-done.4
  166.1 8.4 %all-to-all-done.4 = bf16[16,24,512]{2,1,0:T(8,128)(2,1)S(1)} async-done(((bf16[16,24,512]{2,1,0:T(8,128)(2,1)}), bf16[16,24,512]{2,1,0:T(8,128)(2,1)S(1)}, u32[]{:S(2)}, u32[]{:S(2)}) %all-to-all-start.4) | async-done | bytes 393248 | tf_op jit(solution)/shard_map/all_to_all | solution.py:68
  174.5 3.7 %all_gather.15 = bf16[16,48,512]{2,1,0:T(8,128)(2,1)S(1)} all-gather(bf16[16,24,512]{2,1,0:T(8,128)(2,1)S(1)} %all-to-all-done.4), channel_id=1, replica_groups=mesh['x'=4,'y'=4,'c'=2,'z'=8,'h'=2] {'c'}, dimensions={1}, use_global_device_ids=true | all-gather | bytes 1179648 | tf_op jit(solution)/shard_map/all_gather | solution.py:118
  178.2 0.9 multiply_reduce_fusion
  179.2 7.3 %all_to_all.37 = f32[8,2,128]{2,1,0:T(2,128)S(1)} all-to-all(f32[8,2,128]{2,1,0:T(2,128)S(1)} %broadcast_in_dim.16), channel_id=1, replica_groups=mesh['x'=4,'y'=4,'c'=2,'z'=8,'h'=2] {'x','c'}, dimensions={0} | all-to-all | bytes 16384 | tf_op jit(solution)/shard_map/all_to_all | solution.py:68
  186.6 22.4 %all_to_all.38.sums_ref = f32[64,2,128]{2,1,0:T(2,128)S(1)} all-to-all(f32[64,2,128]{2,1,0:T(2,128)S(1)} %broadcast_in_dim.17), channel_id=1, replica_groups=mesh['x'=4,'y'=4,'c'=2,'z'=8,'h'=2] {'y','z','h'}, dimensions={0} | all-to-all | bytes 131072 | tf_op jit(solution)/shard_map/all_to_all | solution.py:68
  209.0 1.5 shard_map.76
  (34 shorter events, 4.7 us)
Async XLA Ops:
  7.2 86.0 %all-gather.3.cloned.1.call-start = ((), (), s32[]{:S(2)}) async-start(), calls=%async_computation.7 | async-start | bytes 8650752 | tf_op jit(solution)/shard_map/all_gather | solution.py:85
  17.2 11.4 %copy-start.2 = (f32[48,256]{1,0:T(8,128)S(1)}, f32[48,256]{1,0:T(8,128)}, u32[]{:S(2)}) copy-start(f32[48,256]{1,0:T(8,128)} %param.9) | copy-start | bytes 147460
  17.2 11.4 %copy-start.3 = (f32[48,256]{1,0:T(8,128)S(1)}, f32[48,256]{1,0:T(8,128)}, u32[]{:S(2)}) copy-start(f32[48,256]{1,0:T(8,128)} %param.8) | copy-start | bytes 147460
  18.4 15.1 %copy-start.1 = (f32[896,512]{1,0:T(8,128)S(1)}, f32[896,512]{1,0:T(8,128)}, u32[]{:S(2)}) copy-start(f32[896,512]{1,0:T(8,128)} %param.5) | copy-start | bytes 5505028
  18.4 46.3 %all-to-all-start = ((bf16[8,96,896]{2,1,0:T(8,128)(2,1)}), bf16[8,96,896]{2,1,0:T(8,128)(2,1)S(1)}, u32[]{:S(2)}, u32[]{:S(2)}) async-start(bf16[8,96,896]{2,1,0:T(8,128)(2,1)} %broadcast_in_dim.12), calls=%async_computation | async-start | bytes 2752512 | tf_op jit(solution)/shard_map/all_to_all | solution.py:68
  28.6 5.8 %collective-permute-start = (f32[2,24,256]{2,1,0:T(8,128)S(1)}, f32[2,24,256]{2,1,0:T(8,128)S(1)}, u32[]{:S(2)}, u32[]{:S(2)}) collective-permute-start(f32[2,24,256]{2,1,0:T(8,128)S(1)} %broadcast_select_fusion), channel_id=1, source_target_pairs={{0,16},{16,0},{1,17},{17,1},{2,18},{18,2},{3,19},{19,3},{4,20},{20... | collective-permute-start | bytes 147464 | tf_op jit(solution)/shard_map/ppermute | solution.py:89
  65.8 3.8 %collective-permute-start.1 = (bf16[16,24,512]{2,1,0:T(8,128)(2,1)S(1)}, bf16[16,24,512]{2,1,0:T(8,128)(2,1)S(1)}, u32[]{:S(2)}, u32[]{:S(2)}) collective-permute-start(bf16[16,24,512]{2,1,0:T(8,128)(2,1)S(1)} %fusion.7), channel_id=1, source_target_pairs={{0,16},{16,0},{1,17},{17,1},{2,18},{18,2},{3,19},{19,3},{4,20},{20... | collective-permute-start | bytes 1179656 | tf_op jit(solution)/shard_map/ppermute | solution.py:99
  70.5 22.5 %all-to-all-start.1 = ((bf16[16,24,512]{2,1,0:T(8,128)(2,1)}), bf16[16,24,512]{2,1,0:T(8,128)(2,1)S(1)}, u32[]{:S(2)}, u32[]{:S(2)}) async-start(bf16[16,24,512]{2,1,0:T(8,128)(2,1)} %fusion.6), calls=%async_computation.1 | async-start | bytes 786432 | tf_op jit(solution)/shard_map/all_to_all | solution.py:72
  79.3 13.8 %collective-permute-start.2 = (f32[2,2,24,256]{3,2,1,0:T(8,128)S(1)}, f32[2,2,24,256]{3,2,1,0:T(8,128)S(1)}, u32[]{:S(2)}, u32[]{:S(2)}) collective-permute-start(f32[2,2,24,256]{3,2,1,0:T(8,128)S(1)} %pad_maximum_fusion), channel_id=1, source_target_pairs={{0,0},{1,32},{2,64},{3,96},{4,128},{5,160},{6,192},{7,224},{8,256}... | collective-permute-start | bytes 294920 | tf_op jit(solution)/shard_map/ppermute | solution.py:95
  93.2 52.5 %copy-start = (bf16[16384,256]{1,0:T(8,128)(2,1)S(1)}, bf16[16384,256]{1,0:T(8,128)(2,1)}, u32[]{:S(2)}) copy-start(bf16[16384,256]{1,0:T(8,128)(2,1)} %all-gather.3.cloned.1.call-done) | copy-start | bytes 25165828
  148.0 13.6 %collective-permute-start.3 = (f32[2,24,256]{2,1,0:T(8,128)S(1)}, f32[2,24,256]{2,1,0:T(8,128)S(1)}, u32[]{:S(2)}, u32[]{:S(2)}) collective-permute-start(f32[2,24,256]{2,1,0:T(8,128)S(1)} %bitcast.85), channel_id=1, source_target_pairs={{0,0},{1,32},{2,64},{3,96},{4,128},{5,160},{6,192},{7,224},{8,256}... | collective-permute-start | bytes 147464 | tf_op jit(solution)/shard_map/ppermute | solution.py:113
  149.4 25.0 %all-to-all-start.4 = ((bf16[16,24,512]{2,1,0:T(8,128)(2,1)}), bf16[16,24,512]{2,1,0:T(8,128)(2,1)S(1)}, u32[]{:S(2)}, u32[]{:S(2)}) async-start(bf16[16,24,512]{2,1,0:T(8,128)(2,1)} %broadcast_in_dim.15), calls=%async_computation.4 | async-start | bytes 786432 | tf_op jit(solution)/shard_map/all_to_all | solution.py:68
  161.6 3.8 %collective-permute-start.4 = (f32[24,256]{1,0:T(8,128)S(1)}, f32[24,256]{1,0:T(8,128)S(1)}, u32[]{:S(2)}, u32[]{:S(2)}) collective-permute-start(f32[24,256]{1,0:T(8,128)S(1)} %select_bitcast_fusion.2), channel_id=1, source_target_pairs={{0,16},{16,0},{1,17},{17,1},{2,18},{18,2},{3,19},{19,3},{4,20},{20... | collective-permute-start | bytes 73736 | tf_op jit(solution)/shard_map/ppermute | solution.py:115
Sparse Core Ops, SparseCore 0:
  10.1 79.8 all-gather.2
